TPU v7x, 32 devices: a whole 2x2x4 slice. The times are simulated.
32 devices in a mesh: dev: 32 (over z, y, x, core).
Axes of the slice: x: 2, y: 2, z: 4, core: 2. Of those that a mesh axis runs over, the one named last changes fastest.
Arguments:
- hidden_in: bfloat16 [2, 2048, 1280], P(None, 'dev'), may hold values from -6 to 6
- clip_lengths: int32 [2, 3], replicated, may hold values from 1 to 1024, 2048 in all within a row
- ln1_gain: bfloat16 [1280], P('dev'), may hold values from 0.5 to 1.5
- ln1_bias: bfloat16 [1280], P('dev'), may hold values from -1.75 to 1.75
- w_query: bfloat16 [1280, 1280], P('dev'), may hold values from -0.15625 to 0.15625
- b_query: bfloat16 [1280], P('dev'), may hold values from -3 to 3
- w_key: bfloat16 [1280, 1280], P('dev'), may hold values from -0.15625 to 0.15625
- w_value: bfloat16 [1280, 1280], P('dev'), may hold values from -0.15625 to 0.15625
- b_value: bfloat16 [1280], P('dev'), may hold values from -3 to 3
- w_out: bfloat16 [1280, 1280], P('dev'), may hold values from -1 to 1
- b_out: bfloat16 [1280], P('dev'), may hold values from -3 to 3
- ln2_gain: bfloat16 [1280], P('dev'), may hold values from 0.5 to 1.5
- ln2_bias: bfloat16 [1280], P('dev'), may hold values from -1.75 to 1.75
- w_fc1: bfloat16 [1280, 5120], P('dev'), may hold values from -0.15625 to 0.15625
- b_fc1: bfloat16 [5120], P('dev'), may hold values from -3 to 3
- w_fc2: bfloat16 [5120, 1280], P('dev'), may hold values from -0.078125 to 0.078125
- b_fc2: bfloat16 [1280], P('dev'), may hold values from -3 to 3
- cotangent: bfloat16 [2, 2048, 1280], P(None, 'dev'), may hold values from -6 to 6
Outputs:
- layer_out: float32 [2, 2048, 1280], P(None, 'dev')
- input_grad: float32 [2, 2048, 1280], P(None, 'dev')
- grad_ln1_gain: float32 [1280], P('dev')
- grad_ln1_bias: float32 [1280], P('dev')
- grad_w_query: float32 [1280, 1280], P('dev')
- grad_b_query: float32 [1280], P('dev')
- grad_w_key: float32 [1280, 1280], P('dev')
- grad_w_value: float32 [1280, 1280], P('dev')
- grad_b_value: float32 [1280], P('dev')
- grad_w_out: float32 [1280, 1280], P('dev')
- grad_b_out: float32 [1280], P('dev')
- grad_ln2_gain: float32 [1280], P('dev')
- grad_ln2_bias: float32 [1280], P('dev')
- grad_w_fc1: float32 [1280, 5120], P('dev')
- grad_b_fc1: float32 [5120], P('dev')
- grad_w_fc2: float32 [5120, 1280], P('dev')
- grad_b_fc2: float32 [1280], P('dev')
Inputs may be any that keep to these rules, and one draw needn't show every extreme that they name: `clip_lengths`: in each micro-batch the 3 lengths sum to 2048, and some clip has exactly 1024 frames.
All inputs are finite; a program needn't handle non-finite values.
Results may differ from a plain program's by a relative error of at most 0.013.
Values may be sent and summed in bfloat16 or wider, within the bound.
No kernel may reach another device: no remote copies, remote signals or barrier semaphores. Data moves between devices by JAX's collectives and lax.ppermute only.
A program may use at most 448 MiB of HBM per device.

v0:
```python
import functools
import math

import jax
import jax.numpy as jnp
from jax import lax
from jax.experimental import pallas as pl
from jax.experimental.pallas import tpu as pltpu
from jax.sharding import PartitionSpec as P

eps = 1e-05
heads = 16
low = jnp.bfloat16
exact = jnp.float32
far = -1e30
lanes = 128
extra_rows = 8


def dot(a, b, ca, cb):
    return lax.dot_general(a, b, (((ca,), (cb,)), ((), ())), preferred_element_type=exact)


def normalized(v):
    mean = jnp.mean(v, axis=-1, keepdims=True)
    cent = v - mean
    inverse = lax.rsqrt(jnp.mean(cent * cent, axis=-1, keepdims=True) + eps)
    return cent * inverse, inverse


def norm_back(unit, inverse, gain, grad):
    scaled = grad * gain
    along = jnp.mean(scaled * unit, axis=-1, keepdims=True)
    return inverse * (scaled - jnp.mean(scaled, axis=-1, keepdims=True) - unit * along)


def tie(value, *others):
    return lax.optimization_barrier((value,) + others)[0]


def together(*values):
    return lax.optimization_barrier(values)


class Layout:
    def __init__(self, micro):
        self.count = lax.axis_size("dev")
        self.half = heads
        self.block = micro * heads
        self.blocks = self.count // self.block
        self.me = lax.axis_index("dev")
        self.rank = self.me % self.block
        self.mine = self.rank // self.half
        self.head = self.rank % self.half
        self.odd = self.rank % 2
        bits = [(self.me // bit) % 2 for bit in (1, 2, 4, 8)]
        self.place = jnp.stack(bits + [self.mine, self.head, self.odd]).astype(jnp.int32)
        self.halves = [list(range(s, s + self.half)) for s in range(0, self.count, self.half)]
        self.whole = [list(range(s, s + self.block)) for s in range(0, self.count, self.block)]
        self.rows = [list(range(s, s + self.blocks)) for s in range(0, self.count, self.blocks)]
        first = [d // self.half % 2 for d in range(self.count)]
        base = [d // self.block * self.block + 2 * (d % self.half) for d in range(self.count)]
        self.even_first = [(d, base[d] + first[d]) for d in range(self.count)]
        self.odd_first = [(d, base[d] + 1 - first[d]) for d in range(self.count)]

    def send(self, value, pairs):
        return lax.ppermute(value, "dev", pairs)

    def swapped(self, value, bit):
        return self.send(value, [(d, d ^ bit) for d in range(self.count)])

    def to_block(self, value):
        if self.blocks == 1:
            return value
        value = lax.all_gather(value, "dev", axis=0, tiled=True, axis_index_groups=self.rows)
        return self.send(value, [(d, d % self.blocks * self.block + d // self.blocks) for d in range(self.count)])

    def from_block(self, value):
        if self.blocks == 1:
            return value
        value = self.send(value, [(d % self.blocks * self.block + d // self.blocks, d) for d in range(self.count)])
        return lax.psum_scatter(value, "dev", scatter_dimension=0, tiled=True, axis_index_groups=self.rows)

    def partner(self, value):
        return self.swapped(value, self.half)

    def ordered(self, kept, got):
        return jnp.where(self.mine == 0, kept, got), jnp.where(self.mine == 0, got, kept)

    def exchanged(self, value):
        kept = lax.dynamic_index_in_dim(value, self.mine, 0, False)
        return kept, self.partner(lax.dynamic_index_in_dim(value, 1 - self.mine, 0, False))

    def send_rows_back(self, value):
        first = lax.dynamic_index_in_dim(value, self.mine, 0, False)
        second = lax.dynamic_index_in_dim(value, 1 - self.mine, 0, False)
        return self.send(first, self.even_first), self.send(second, self.odd_first)

    def gather_half(self, value):
        return lax.all_gather(value, "dev", axis=0, axis_index_groups=self.halves)

    def exchange_half(self, value):
        return lax.all_to_all(value, "dev", 0, 0, tiled=True, axis_index_groups=self.halves)

    def exchange_block(self, value):
        return lax.all_to_all(value, "dev", 0, 0, tiled=True, axis_index_groups=self.whole)

    def gather_tree(self, parts, beside=()):
        brought = []
        for stage in range(3):
            got = [self.swapped(piece, order[stage]) for piece, order in zip(parts, part_orders)]
            if beside:
                far = self.partner(tie(beside[stage], parts[0]))
                first, far = together(got[0], far)
                got = [first, *got[1:]]
                brought.append(far)
            if stage < 2:
                parts = merge(parts, got)
        other = [self.swapped(piece, 1) for piece in (*parts, *got)]
        return (*parts, *got), other, brought

    def reduce_half(self, away, kept, marks=None, before=None, arrived=None):
        got = [self.swapped(away, 1)]
        kept = [kept]
        for stage in range(3):
            if before and stage in before:
                got = [tie(got[0], *before[stage](marks)), *got[1:]]
            away, kept = split_terms(self.place, stage, kept, got)
            if marks is not None:
                marks.append(away[0])
            got = [self.swapped(piece, order[stage]) for piece, order in zip(away, part_orders)]
            if arrived is not None:
                arrived.append(got[2])
        return kept, got


small_cost = pl.CostEstimate(flops=1 << 10, bytes_accessed=1 << 10, transcendentals=0)


def far_off(v):
    return pltpu.with_memory_space_constraint(v, pltpu.HBM)


def params(megabytes):
    return pltpu.CompilerParams(vmem_limit_bytes=megabytes << 20)


part_orders = ((8, 4, 2), (4, 2, 8), (2, 8, 4))


def part_bounds(tokens):
    cut = tokens * 3 // 8 // 16 * 16
    return ((0, cut), (cut, 2 * cut), (2 * cut, tokens))


def split_kernel(stage, place_ref, *refs):
    place = {bit: place_ref[i] for i, bit in enumerate((1, 2, 4, 8))}
    if stage == 0:
        kept_ref, got_ref = refs[:2]
        outs = refs[2:]
        bounds = part_bounds(kept_ref.shape[1])
    else:
        outs = refs[6:]
    for part, order in enumerate(part_orders):
        left = [bit for bit in (8, 4, 2) if bit not in order[:stage]]
        at = left.index(order[stage])
        below = 1 << (len(left) - 1 - at)
        for half, side in ((0, 1 - place[order[stage]]), (1, place[order[stage]])):
            out_ref = outs[part + 3 * half]
            for j in range(out_ref.shape[0]):
                index = (j // below * 2 + side) * below + j % below
                if stage == 0:
                    start, end = bounds[part]
                    term = kept_ref[index, start:end].astype(exact) + got_ref[index, start:end].astype(exact)
                else:
                    term = refs[part][index].astype(exact) + refs[3 + part][index].astype(exact)
                out_ref[j] = term.astype(out_ref.dtype)


def split_terms(place, stage, kept, got):
    width = kept[0].shape[-1]
    bounds = part_bounds(kept[0].shape[1]) if stage == 0 else [(0, k.shape[1]) for k in kept]
    count = kept[0].shape[0] // 2
    cols = 256 if stage == 0 else 640
    spec = lambda n, t: pl.BlockSpec((n, t, cols), lambda i, p: (0, 0, i))
    outs = [(count, end - start) for start, end in bounds]
    res = pl.pallas_call(
        functools.partial(split_kernel, stage),
        grid_spec=pltpu.PrefetchScalarGridSpec(
            num_scalar_prefetch=1,
            grid=(width // cols,),
            in_specs=[spec(*v.shape[:2]) for v in (*kept, *got)],
            out_specs=[spec(*o) for o in outs] * 2,
        ),
        out_shape=[jax.ShapeDtypeStruct(o + (width,), kind) for kind in (low, exact) for o in outs],
        compiler_params=params(10),
        cost_estimate=small_cost,
        name="split_terms",
    )(place, *kept, *got)
    return res[:3], res[3:]


def last_sum(refs):
    return jnp.concatenate([refs[i][0].astype(exact) + refs[3 + i][0].astype(exact) for i in range(3)], axis=0)


def pack_kernel(place_ref, x_ref, v_ref, c_ref, first_ref, second_ref):
    rows, width = x_ref.shape[1:]
    mine = place_ref[4]
    fill = jnp.zeros((v_ref.shape[0], width - v_ref.shape[1]), exact)
    small = jnp.concatenate([v_ref[...].astype(exact), fill], axis=1)
    c = jnp.concatenate([c_ref[...].astype(exact), jnp.zeros((1, width - lanes - c_ref.shape[1]), exact)], axis=1)
    c = jnp.concatenate([jnp.zeros((1, lanes), exact), c], axis=1)
    row = lax.broadcasted_iota(jnp.int32, small.shape, 0)
    small = small + jnp.where(row == 0, c, 0.0)
    tail = small.astype(low)
    for out_ref, index in ((first_ref, mine), (second_ref, 1 - mine)):
        out_ref[:rows] = x_ref[index]
        out_ref[rows:] = tail


def pack(place, x, vectors, c):
    rows, width = x.shape[1:]
    out = jax.ShapeDtypeStruct((rows + extra_rows, width), low)
    return pl.pallas_call(
        pack_kernel,
        grid_spec=pltpu.PrefetchScalarGridSpec(
            num_scalar_prefetch=1,
            grid=(1,),
            in_specs=[whole_spec(v) for v in (x, vectors, c)],
            out_specs=[out_spec(out)] * 2,
        ),
        out_shape=[out, out],
        compiler_params=params(6),
        name="pack",
    )(place, x, vectors, c)


def arrange_kernel(rows, place_ref, first_ref, second_ref, x_ref, small_ref, *part_refs):
    mine = place_ref[4]
    for side, refs in enumerate(((first_ref, second_ref), (second_ref, first_ref))):

        @pl.when(mine == side)
        def _():
            x = jnp.concatenate([ref[:rows] for ref in refs], axis=0)
            x_ref[...] = x
            tail = [ref[rows:].astype(exact) for ref in refs]
            small_ref[...] = jnp.concatenate(tail, axis=0).astype(low)
            for part_ref, (start, end) in zip(part_refs, part_bounds(2 * rows)):
                part_ref[0] = x[start:end]


def arrange(place, first, second, rows):
    width = first.shape[1]
    shapes = [(2 * rows, width), (2 * extra_rows, width)]
    shapes += [(1, end - start, width) for start, end in part_bounds(2 * rows)]
    outs = [jax.ShapeDtypeStruct(shape, low) for shape in shapes]
    return pl.pallas_call(
        functools.partial(arrange_kernel, rows),
        grid_spec=pltpu.PrefetchScalarGridSpec(
            num_scalar_prefetch=1,
            grid=(1,),
            in_specs=[whole_spec(first), whole_spec(second)],
            out_specs=[out_spec(out) for out in outs],
        ),
        out_shape=outs,
        compiler_params=params(6),
        name="arrange",
    )(place, first, second)


def up_to_lanes(size):
    return -(-size // lanes) * lanes


def fold(v):
    return jnp.concatenate([v[i : i + 8] for i in range(0, v.shape[0], 8)], axis=1)


def unfold(v, size):
    return jnp.concatenate([v[:, i : i + size] for i in range(0, v.shape[1], size)], axis=0)


def unfold_kernel(in_ref, out_ref):
    size = out_ref.shape[1]
    chunk = in_ref.shape[2] // size * 8
    for device in range(0, in_ref.shape[0], 2):
        rows = [unfold(in_ref[device + i].astype(exact), size) for i in range(2)]
        out_ref[device * chunk : (device + 2) * chunk] = jnp.concatenate(rows, axis=0).astype(low)


def unfolded(v, size):
    return pl.pallas_call(
        unfold_kernel,
        out_shape=jax.ShapeDtypeStruct((v.size // size, size), low),
        compiler_params=params(8),
        cost_estimate=small_cost,
        name="unfolded",
    )(v)


def deal_kernel(hd, q_ref, k_ref, v_ref, w_ref, in_ref, hidden_ref):
    ff = w_ref.shape[1] // heads
    side_by_side = lambda pieces: jnp.concatenate([piece.astype(exact) for piece in pieces], axis=1).astype(low)
    for head in range(heads):
        at = [(slot * heads + head) * (ff // 2) for slot in range(2)]
        hidden = jnp.concatenate([w_ref[:, a : a + ff // 2].astype(exact) for a in at], axis=1)
        hidden = fold(hidden).astype(low)
        columns = side_by_side([ref[:, head * hd : (head + 1) * hd] for ref in (q_ref, k_ref, v_ref)])
        for device in range(head, in_ref.shape[0], heads):
            in_ref[device] = columns
            hidden_ref[device] = hidden


def deal(q, k, v, w, hd, block):
    chunk, ff = q.shape[0], w.shape[1] // heads
    return pl.pallas_call(
        functools.partial(deal_kernel, hd),
        out_shape=[jax.ShapeDtypeStruct(shape, low) for shape in ((block, chunk, 3 * hd), (block, 8, chunk * ff // 8))],
        compiler_params=params(8),
        name="deal",
    )(q, k, v, w)


def merge_kernel(*refs):
    for i in range(3):
        count = refs[i].shape[0]
        refs[6 + i][:count] = refs[i][...]
        refs[6 + i][count:] = refs[3 + i][...]


def merge(parts, got):
    width = parts[0].shape[2]
    cols = 640
    spec = lambda shape: pl.BlockSpec(shape[:2] + (cols,), lambda i: (0, 0, i))
    outs = [(2 * p.shape[0],) + p.shape[1:] for p in parts]
    return pl.pallas_call(
        merge_kernel,
        grid=(width // cols,),
        in_specs=[spec(v.shape) for v in (*parts, *got)],
        out_specs=[spec(o) for o in outs],
        out_shape=[jax.ShapeDtypeStruct(o, low) for o in outs],
        compiler_params=params(8),
        name="merge",
    )(*parts, *got)


def out_spec(v):
    return pl.BlockSpec(v.shape, lambda *_: (0,) * len(v.shape))


def tree_rows(place_ref, chip, refs, fill):
    mine = place_ref[1] + 2 * place_ref[2] + 4 * place_ref[3]
    apart = chip ^ mine
    step = {8: apart // 4, 4: apart // 2 % 2, 2: apart % 2}
    for part, order in enumerate(part_orders):
        index = 2 * step[order[1]] + step[order[0]]
        for late in range(2):

            @pl.when(step[order[2]] == late)
            def _():
                fill(part, refs[part + 3 * late], index)


def fill_rows(place_ref, chip, refs, out_ref, base, own):
    bounds = part_bounds(own)

    def fill(part, ref, index):
        start, end = bounds[part]
        out_ref[pl.ds(base + start, end - start)] = ref[index, : end - start]

    tree_rows(place_ref, chip, refs, fill)


def whole_spec(v):
    return pl.BlockSpec(v.shape, lambda *_: (0,) * len(v.shape), pipeline_mode=pl.Buffered(1))


def norm_kernel(hd, chunk, first, place_ref, *refs):
    pieces = refs[:6]
    a_ref, table_ref, x_scr = refs[-3:]
    step, _, own, width = a_ref.shape

    @pl.when(pl.program_id(0) == 0)
    def _():
        if first:
            tail = part_bounds(own)[2]

            def fill(chip, part, ref, index):
                if part != 2:
                    return
                small = ref[index, tail[1] - tail[0] :].astype(exact)
                for far_core in range(2):
                    for slot in range(2):
                        line = (2 * far_core + slot) * extra_rows
                        piece = small[line : line + extra_rows, :chunk]
                        for core in range(2):

                            @pl.when(place_ref[0] == core)
                            def _():
                                at = (heads * slot + 2 * chip + (core ^ far_core)) * chunk
                                table_ref[:, at : at + chunk] = piece

            for chip in range(8):
                tree_rows(place_ref, chip, pieces, functools.partial(fill, chip))
        else:
            table_ref[...] = refs[6][...]

    for j in range(step):
        fill_rows(place_ref, pl.program_id(0) * step + j, pieces, x_scr, j * own, own)
    unit, _ = normalized(x_scr[...].astype(exact))
    a_ref[...] = (unit * table_ref[0:1] + table_ref[1:2]).astype(low).reshape(a_ref.shape)


def norm(place, other, pieces, before, hd, own, chunk):
    width = pieces[0].shape[2]
    step = 4
    side = (lambda p: 1 - p[0]) if other else (lambda p: p[0])
    table = jax.ShapeDtypeStruct((extra_rows, width), exact)
    return pl.pallas_call(
        functools.partial(norm_kernel, hd, chunk, not before),
        grid_spec=pltpu.PrefetchScalarGridSpec(
            num_scalar_prefetch=1,
            grid=(8 // step,),
            in_specs=[whole_spec(v) for v in pieces] + ([whole_spec(table), pl.BlockSpec(memory_space=pl.ANY)] if before else []),
            out_specs=[pl.BlockSpec((step, 1, own, width), lambda i, p: (i, side(p), 0, 0)), out_spec(table)],
            scratch_shapes=[pltpu.VMEM((step * own, width), low)],
        ),
        out_shape=[pltpu.HBM((8, 2, own, width), low), table],
        input_output_aliases={8: 0} if before else {},
        compiler_params=params(30),
        cost_estimate=small_cost,
        name="norm",
    )(place, *pieces, *before[::-1])


def project_kernel(hd, clips, own_rows, place_ref, ends_ref, a_ref, w_ref, table_ref, qkv_ref, pad_ref, bias_ref):
    rows, width = a_ref.shape

    @pl.when(pl.program_id(0) == 0)
    def _():
        w = w_ref[...].astype(exact)
        fill = jnp.zeros((width, lanes - hd), exact)
        w = [v for i in range(3) for v in (w[:, i * hd : (i + 1) * hd], fill)]
        pad_ref[...] = jnp.concatenate(w, axis=1).astype(low)
        bias_ref[...] = jnp.zeros_like(bias_ref)
        for h in range(heads):

            @pl.when(place_ref[5] == h)
            def _():
                for line, at in ((2, 0), (3, 2 * lanes)):
                    bias_ref[0:1, at : at + hd] = table_ref[line : line + 1, h * hd : (h + 1) * hd]

    qkv = dot(a_ref[...], pad_ref[...], 1, 0) + bias_ref[0:1]
    column = lax.broadcasted_iota(jnp.int32, (rows, lanes), 1) - hd
    row = lax.broadcasted_iota(jnp.int32, (rows, lanes), 0) + pl.program_id(0) * rows
    shift = own_rows.bit_length() - 1
    token = (lax.shift_right_logical(row, shift) & 1) * (heads * own_rows)
    token += lax.shift_right_logical(row, shift + 1) * own_rows + (row & (own_rows - 1))
    clip = jnp.zeros_like(token)
    for i in range(clips):
        clip += (ends_ref[i] <= token).astype(jnp.int32)
    match = clip == column
    marked = (column >= 0) & (column <= clips)
    qkv_ref[:, :lanes] = (qkv[:, :lanes] + jnp.where(marked & ~match, far, 0.0)).astype(low)
    qkv_ref[:, lanes : 2 * lanes] = (qkv[:, lanes : 2 * lanes] + jnp.where(marked & match, 1.0, 0.0)).astype(low)
    qkv_ref[:, 2 * lanes :] = qkv[:, 2 * lanes :].astype(low)


def project(place, ends, a, w, table, hd, own_rows):
    tokens, width = a.shape
    rows = 512
    clips = ends.shape[0]
    assert own_rows & (own_rows - 1) == 0
    wide = jax.ShapeDtypeStruct((width, 3 * lanes), low)
    return pl.pallas_call(
        functools.partial(project_kernel, hd, clips, own_rows),
        grid_spec=pltpu.PrefetchScalarGridSpec(
            num_scalar_prefetch=2,
            grid=(tokens // rows,),
            in_specs=[
                pl.BlockSpec((rows, width), lambda i, p, e: (i, 0)),
                whole_spec(w),
                whole_spec(table),
            ],
            out_specs=[pl.BlockSpec((rows, 3 * lanes), lambda i, p, e: (i, 0)), out_spec(wide)],
            scratch_shapes=[pltpu.VMEM((8, 3 * lanes), exact)],
        ),
        out_shape=[jax.ShapeDtypeStruct((tokens, 3 * lanes), low), pltpu.HBM(wide.shape, low)],
        compiler_params=params(20),
        cost_estimate=small_cost,
        name="project",
    )(place, ends, far_off(a), w, table)


def join_kernel(x_ref, o_ref, w_ref, table_ref, x2_ref, *part_refs):
    o = o_ref[...].reshape(w_ref.shape[0], o_ref.shape[2])
    x2 = x_ref[...].astype(exact) + (dot(o, w_ref[...], 0, 0) + table_ref[4:5])
    x2_ref[...] = x2
    unit, _ = normalized(x2)
    a2 = (unit * table_ref[5:6] + table_ref[6:7]).astype(low)
    for part_ref, (start, end) in zip(part_refs, part_bounds(x2.shape[0])):
        part_ref[0] = a2[start:end]


def join(x, o, w, table):
    own, width = x.shape
    parts = [jax.ShapeDtypeStruct((1, end - start, width), low) for start, end in part_bounds(own)]
    return pl.pallas_call(
        join_kernel,
        out_shape=[jax.ShapeDtypeStruct(x.shape, exact)] + parts,
        compiler_params=params(10),
        cost_estimate=small_cost,
        name="join",
    )(x, o, far_off(w), table)


def accumulate(total_ref, term):
    @pl.when(pl.program_id(0) == 0)
    def _():
        total_ref[...] = term

    @pl.when(pl.program_id(0) > 0)
    def _():
        total_ref[...] += term


def at_end(write):
    pl.when(pl.program_id(0) == pl.num_programs(0) - 1)(write)


def fc2_grad_kernel(hid_ref, g_ref, out_ref, total_ref):
    rows = math.prod(g_ref.shape[:3])
    accumulate(total_ref, dot(hid_ref[...].reshape(rows, hid_ref.shape[3]), g_ref[...].reshape(rows, g_ref.shape[3]), 0, 0))

    @at_end
    def _():
        out_ref[...] = total_ref[...].astype(low).reshape(out_ref.shape)


def fc2_grad(hid, g):
    eight, two, own, width = g.shape
    ff = hid.shape[3]
    step = 2
    out = jax.ShapeDtypeStruct((2, ff // 2, width), low)
    return pl.pallas_call(
        fc2_grad_kernel,
        grid=(eight // step,),
        in_specs=[pl.BlockSpec((step, two, own, size), lambda i: (i, 0, 0, 0)) for size in (ff, width)],
        out_specs=out_spec(out),
        out_shape=out,
        scratch_shapes=[pltpu.VMEM((ff, width), exact)],
        compiler_params=params(12),
        cost_estimate=small_cost,
        name="fc2_grad",
    )(far_off(hid), far_off(g))


def fc1_grad_kernel(place_ref, *refs):
    mine, others, (du_ref, out_ref, a_scr, total_ref) = refs[:6], refs[6:12], refs[12:]
    chips, two, own, ff = du_ref.shape
    width = a_scr.shape[3]
    bounds = part_bounds(own)
    for j in range(chips):
        chip = pl.program_id(0) * chips + j
        for core, pieces in ((place_ref[0], mine), (1 - place_ref[0], others)):

            def fill(part, ref, index):
                start, end = bounds[part]
                a_scr[j, core, start:end] = ref[index]

            tree_rows(place_ref, chip, pieces, fill)
    rows = chips * two * own
    accumulate(total_ref, dot(du_ref[...].reshape(rows, ff), a_scr[...].reshape(rows, width), 0, 0))

    @at_end
    def _():
        total = total_ref[...].T
        chunk = width // out_ref.shape[0]
        for device in range(out_ref.shape[0]):
            out_ref[device] = fold(total[device * chunk : (device + 1) * chunk]).astype(low)


def fc1_grad(place, mine, others, du, chunk):
    eight, two, own, ff = du.shape
    width = mine[0].shape[2]
    step = 2
    out = jax.ShapeDtypeStruct((width // chunk, 8, chunk * ff // 8), low)
    return pl.pallas_call(
        fc1_grad_kernel,
        grid_spec=pltpu.PrefetchScalarGridSpec(
            num_scalar_prefetch=1,
            grid=(eight // step,),
            in_specs=[whole_spec(v) for v in (*mine, *others)] + [pl.BlockSpec((step, two, own, ff), lambda i, p: (i, 0, 0, 0))],
            out_specs=out_spec(out),
            scratch_shapes=[pltpu.VMEM((step, two, own, width), low), pltpu.VMEM((ff, width), exact)],
        ),
        out_shape=out,
        compiler_params=params(20),
        cost_estimate=small_cost,
        name="fc1_grad",
    )(place, *mine, *others, far_off(du))


def output_grad_kernel(o_ref, ga_ref, out_ref, total_ref):
    term = dot(o_ref[0], ga_ref[0], 1, 0)
    for piece in range(1, o_ref.shape[0]):
        term += dot(o_ref[piece], ga_ref[piece], 1, 0)
    accumulate(total_ref, term)

    @at_end
    def _():
        rows = out_ref.shape[1]
        for side in range(2):
            out_ref[side] = total_ref[side * rows : (side + 1) * rows].astype(low)


def output_grad(o, ga):
    count, hd, own = o.shape
    width = ga.shape[2]
    step = 4
    out = jax.ShapeDtypeStruct((2, hd // 2, width), low)
    return pl.pallas_call(
        output_grad_kernel,
        grid=(count // step,),
        in_specs=[pl.BlockSpec((step, hd, own), lambda i: (i, 0, 0)), pl.BlockSpec((step, own, width), lambda i: (i, 0, 0))],
        out_specs=out_spec(out),
        out_shape=out,
        scratch_shapes=[pltpu.VMEM((hd, width), exact)],
        compiler_params=params(8),
        cost_estimate=small_cost,
        name="output_grad",
    )(o, far_off(ga))


def feed_kernel(place_ref, *refs):
    pieces, (g_ref, w1_ref, w2_ref, c_ref) = refs[:6], refs[6:10]
    hid_ref, du_ref, y_ref, da_ref, sum_ref, a_scr = refs[-6:]
    step, own, width = da_ref.shape
    rows = step * own
    for j in range(step):
        fill_rows(place_ref, pl.program_id(0) * step + j, pieces, a_scr, j * own, own)
    w1, w2 = w1_ref[...], w2_ref[...]
    u = dot(a_scr[...], w1, 1, 0) + c_ref[...]
    d_hid = dot(g_ref[...].reshape(rows, width), w2, 1, 1)
    below = 0.5 * (1.0 + lax.erf(u * math.sqrt(0.5)))
    hid = (u * below).astype(low)
    hid_ref[...] = hid.reshape(hid_ref.shape)
    y_ref[...] = dot(hid, w2, 1, 0).reshape(y_ref.shape).astype(low)
    slope = below + u * (jnp.exp(-0.5 * u * u) * (1.0 / math.sqrt(2.0 * math.pi)))
    du = (d_hid * slope).astype(low)
    du_ref[...] = du.reshape(du_ref.shape)
    da_ref[...] = dot(du, w1, 1, 1).reshape(da_ref.shape).astype(da_ref.dtype)

    @pl.when(pl.program_id(0) == 0)
    def _():
        sum_ref[...] = jnp.zeros_like(sum_ref)

    sum_ref[...] += jnp.sum(du.astype(exact), axis=0, keepdims=True)


def feed(place, other, pieces, g, w1, w2, c1, before, own, kind):
    ff, width = w2.shape
    step = 4
    tokens = 8 * own
    side = (lambda p: 1 - p[0]) if other else (lambda p: p[0])
    pick = lambda size: pl.BlockSpec((step, 1, own, size), lambda i, p: (i, side(p), 0, 0))
    shape = lambda size: pltpu.HBM((8, 2, own, size), low)
    row = pl.BlockSpec((1, ff), lambda i, p: (0, 0))
    return pl.pallas_call(
        feed_kernel,
        grid_spec=pltpu.PrefetchScalarGridSpec(
            num_scalar_prefetch=1,
            grid=(8 // step,),
            in_specs=[whole_spec(v) for v in pieces]
            + [pick(width), whole_spec(w1), whole_spec(w2), row]
            + [pl.BlockSpec(memory_space=pl.ANY)] * len(before),
            out_specs=[pick(ff), pick(ff), pick(width), pl.BlockSpec((step, own, width), lambda i, p: (i, 0, 0)), row],
            scratch_shapes=[pltpu.VMEM((step * own, width), low)],
        ),
        out_shape=[
            shape(ff),
            shape(ff),
            shape(width),
            pltpu.HBM((8, own, width), kind),
            jax.ShapeDtypeStruct((1, ff), exact),
        ],
        input_output_aliases={11: 0, 12: 1, 13: 2} if before else {},
        compiler_params=params(34),
        cost_estimate=small_cost,
        name="feed",
    )(place, *pieces, far_off(g), w1, w2, c1, *before)


def terms_kernel(contract, place_ref, left_ref, right_ref, out_ref):
    rows = out_ref.shape[0] * out_ref.shape[1]
    left = left_ref[...].reshape(rows, left_ref.shape[-1])
    out_ref[...] = dot(left, right_ref[...], 1, contract).reshape(out_ref.shape).astype(out_ref.dtype)


def terms(place, other, left, right, contract, kind):
    eight, two, own, depth = left.shape
    width = right.shape[1 - contract]
    step = 4
    side = (lambda p: 1 - p[0]) if other else (lambda p: p[0])
    return pl.pallas_call(
        functools.partial(terms_kernel, contract),
        grid_spec=pltpu.PrefetchScalarGridSpec(
            num_scalar_prefetch=1,
            grid=(eight // step,),
            in_specs=[
                pl.BlockSpec((step, 1, own, depth), lambda i, p: (i, side(p), 0, 0)),
                pl.BlockSpec(right.shape, lambda i, p: (0, 0)),
            ],
            out_specs=pl.BlockSpec((step, own, width), lambda i, p: (i, 0, 0)),
        ),
        out_shape=jax.ShapeDtypeStruct((eight, own, width), kind),
        compiler_params=params(16),
        cost_estimate=small_cost,
        name="terms",
    )(place, left, right)


def rows_of(values, width):
    fill = jnp.zeros((8 - len(values), width), exact)
    return jnp.concatenate(values + [fill], axis=0)


def second_back_kernel(*refs):
    da2 = last_sum(refs[:6])
    x2_ref, g_ref, table_ref, w_ref, dx2_ref, ga_ref, do_ref, sum_ref = refs[6:]
    unit, inverse = normalized(x2_ref[...])
    g = g_ref[...].astype(exact)
    dx2 = g + norm_back(unit, inverse, table_ref[5:6], da2)
    dx2_ref[...] = dx2
    ga = dx2.astype(low)
    ga_ref[...] = ga
    do_ref[...] = dot(w_ref[...], ga, 1, 1).astype(low).reshape(do_ref.shape)
    total = lambda v: jnp.sum(v, axis=0, keepdims=True)
    sum_ref[...] = rows_of([total(da2 * unit), total(da2), total(ga.astype(exact)), total(g)], ga.shape[1])


def second_back(kept, got, x2, g, table, w, hd):
    own, width = x2.shape
    return pl.pallas_call(
        second_back_kernel,
        out_shape=[
            jax.ShapeDtypeStruct((own, width), exact),
            jax.ShapeDtypeStruct((own, width), low),
            jax.ShapeDtypeStruct((heads, hd, own), low),
            jax.ShapeDtypeStruct((8, width), exact),
        ],
        compiler_params=params(12),
        cost_estimate=small_cost,
        name="second_back",
    )(*kept, *got, x2, g, table, far_off(w))


def first_back_kernel(chunk, *refs):
    da1 = last_sum(refs[:6])
    x_ref, dx2_ref, table_ref, dx_ref, vec_ref = refs[6:]
    unit, inverse = normalized(x_ref[...].astype(exact))
    dx = dx2_ref[...] + norm_back(unit, inverse, table_ref[0:1], da1)
    dx_ref[...] = dx.astype(low)
    total = lambda v: jnp.sum(v, axis=0, keepdims=True)
    rows = [total(da1 * unit), total(da1)]
    fill = jnp.zeros((1, lanes // 2 - chunk), exact)
    for device in range(vec_ref.shape[0]):
        part = slice(device * chunk, (device + 1) * chunk)
        vec_ref[device] = jnp.concatenate([rows[0][:, part], fill, rows[1][:, part], fill], axis=1)


def first_back(kept, got, x, dx2, table, chunk, block):
    return pl.pallas_call(
        functools.partial(first_back_kernel, chunk),
        out_shape=[jax.ShapeDtypeStruct(x.shape, low), jax.ShapeDtypeStruct((block, 1, lanes), exact)],
        compiler_params=params(8),
        name="first_back",
    )(*kept, *got, x, dx2, table)


def head_grad_kernel(hd, chunk, place_ref, a_ref, d_ref, sum2_ref, sum_in_ref, sum_c_ref, sum_c2_ref, out_ref, total_ref, line_ref):
    accumulate(total_ref, dot(d_ref[...], a_ref[...], 0, 0))

    @at_end
    def _():
        block = out_ref.shape[0]
        head = place_ref[5]
        c = sum_c_ref[...] + sum_c2_ref[...]
        ff_rows = c.shape[1] // 2
        total = jnp.concatenate([total_ref[i * lanes : i * lanes + hd] for i in range(3)], axis=0).T
        line_ref[...] = jnp.zeros_like(line_ref)
        line_ref[0:4] = sum2_ref[0:4]
        for h in range(heads):

            @pl.when(head == h)
            def _():
                for line, at in ((4, 0), (5, 2 * lanes)):
                    line_ref[line : line + 1, h * hd : (h + 1) * hd] = sum_in_ref[0:1, at : at + hd]
                for slot in range(block // heads):
                    for line in range(ff_rows // chunk):
                        at, start = (slot * heads + h) * chunk, slot * ff_rows + line * chunk
                        line_ref[8 + line : 9 + line, at : at + chunk] = c[:, start : start + chunk]

        small = line_ref[...].T
        for device in range(block):
            part = slice(device * chunk, (device + 1) * chunk)
            out_ref[device] = jnp.concatenate([total[part], small[part]], axis=1).astype(low)


def head_grad(place, a, d, sum2, sum_in, sum_c, sum_c2, hd, chunk, block):
    tokens, width = a.shape
    rows = 512
    out = jax.ShapeDtypeStruct((block, chunk, up_to_lanes(3 * hd)), low)
    small = (sum2, sum_in, sum_c, sum_c2)
    return pl.pallas_call(
        functools.partial(head_grad_kernel, hd, chunk),
        grid_spec=pltpu.PrefetchScalarGridSpec(
            num_scalar_prefetch=1,
            grid=(tokens // rows,),
            in_specs=[pl.BlockSpec((rows, size), lambda i, p: (i, 0)) for size in (width, 3 * lanes)] + [whole_spec(v) for v in small],
            out_specs=out_spec(out),
            scratch_shapes=[pltpu.VMEM((3 * lanes, width), exact), pltpu.VMEM((out.shape[2] - 3 * hd, width), exact)],
        ),
        out_shape=out,
        compiler_params=params(16),
        cost_estimate=small_cost,
        name="head_grad",
    )(place, far_off(a), d, *small)


def collect_kernel(hd, in_ref, *refs):
    out_refs, small_ref = refs[:3], refs[3]
    count = in_ref.shape[0] // 2
    small = jnp.zeros((in_ref.shape[1], in_ref.shape[2] - 3 * hd), exact)
    for head in range(count):
        total = in_ref[head].astype(exact) + in_ref[count + head].astype(exact)
        small += total[:, 3 * hd :]
        for i, out_ref in enumerate(out_refs):
            out_ref[:, head * hd : (head + 1) * hd] = total[:, i * hd : (i + 1) * hd]
    small_ref[...] = small.T


def collect(terms_in, hd):
    block, chunk, size = terms_in.shape
    matrix = jax.ShapeDtypeStruct((chunk, block // 2 * hd), exact)
    return pl.pallas_call(
        functools.partial(collect_kernel, hd),
        out_shape=[matrix] * 3 + [jax.ShapeDtypeStruct((size - 3 * hd, chunk), exact)],
        compiler_params=params(8),
        name="collect",
    )(terms_in)


def collect_hidden_kernel(ff, in_ref, out_ref):
    count = in_ref.shape[0] // 2
    for piece in range(count):
        total = unfold(in_ref[piece].astype(exact) + in_ref[count + piece].astype(exact), ff)
        for slot in range(2):
            at = (slot * count + piece) * (ff // 2)
            out_ref[:, at : at + ff // 2] = total[:, slot * (ff // 2) : (slot + 1) * (ff // 2)]


def collect_hidden(terms_in, ff):
    block, _, size = terms_in.shape
    return pl.pallas_call(
        functools.partial(collect_hidden_kernel, ff),
        out_shape=jax.ShapeDtypeStruct((size * 8 // ff, block // 2 * ff), exact),
        compiler_params=params(8),
        name="collect_hidden",
    )(terms_in)


def attend_kernel(hd, coef, q_ref, k_ref, v_ref, o_ref, e_ref, inverse_ref, vt_ref):
    @pl.when(pl.program_id(0) == 0)
    def _():
        vt_ref[...] = v_ref[...].T

    s = dot(k_ref[...], q_ref[...], 1, 1)
    top = jnp.max(s, axis=0, keepdims=True)
    e = jnp.exp2((s - top) * coef)
    total = jnp.sum(e, axis=0, keepdims=True)
    inverse = 1.0 / total
    e = e.astype(low)
    e_ref[0] = e
    inverse_ref[0] = inverse
    o = (dot(vt_ref[...], e, 1, 0) * inverse).astype(low)
    for piece in range(o_ref.shape[0]):
        o_ref[piece] = o[:hd, piece * lanes : (piece + 1) * lanes]


def attend(q, q_at, k, k_at, v, v_at, hd, rows):
    tokens, keys = q.shape[0], k.shape[0]
    coef = math.log2(math.e) / hd**0.5
    steps = tokens // rows
    return pl.pallas_call(
        functools.partial(attend_kernel, hd, coef),
        grid=(steps,),
        in_specs=[
            pl.BlockSpec((rows, lanes), lambda i: (i, q_at)),
            pl.BlockSpec((keys, lanes), lambda i: (0, k_at)),
            pl.BlockSpec((keys, lanes), lambda i: (0, v_at)),
        ],
        out_specs=[
            pl.BlockSpec((rows // lanes, hd, lanes), lambda i: (i, 0, 0)),
            pl.BlockSpec((1, keys, rows), lambda i: (i, 0, 0)),
            pl.BlockSpec((1, 1, rows), lambda i: (i, 0, 0)),
        ],
        out_shape=[
            jax.ShapeDtypeStruct((tokens // lanes, hd, lanes), low),
            pltpu.HBM((steps, keys, rows), low),
            jax.ShapeDtypeStruct((steps, 1, rows), exact),
        ],
        scratch_shapes=[pltpu.VMEM((lanes, keys), low)],
        compiler_params=params(10 * keys // 1024),
        cost_estimate=small_cost,
        name="attend",
    )(q, k, v)


def attend_back_kernel(hd, scale, span, q_ref, k_ref, v_ref, do_ref, e_ref, inverse_ref, out_ref, sum_ref, kt_ref, dk_sum, dv_sum):
    step = pl.program_id(0)
    rows = q_ref.shape[0]

    @pl.when(step == 0)
    def _():
        kt_ref[...] = k_ref[...].T
        dk_sum[...] = jnp.zeros_like(dk_sum)
        dv_sum[...] = jnp.zeros_like(dv_sum)
        sum_ref[...] = jnp.zeros_like(sum_ref)

    pieces = do_ref.shape[0]
    dot_t = jnp.concatenate([do_ref[piece] for piece in range(pieces)], axis=1)
    fill = jnp.zeros((lanes - hd, dot_t.shape[1]), low)
    dot_t = jnp.concatenate([dot_t, fill], axis=0)
    q = q_ref[...]
    p = e_ref[0].astype(exact) * inverse_ref[0]
    dp = dot(v_ref[...], dot_t, 1, 0)
    r = jnp.sum(p * dp, axis=0, keepdims=True)
    ds = (p * (dp - r)).astype(low)
    dv_sum[...] += dot(p.astype(low), dot_t.T, 1, 0)
    dk_sum[...] += dot(ds, q, 1, 0)
    dq = dot(kt_ref[...], ds, 1, 0) * scale
    head = lax.broadcasted_iota(jnp.int32, dq.shape, 0) < hd
    dq = jnp.where(head, dq, 0.0).T.astype(low)
    out_ref[pl.ds(pl.multiple_of(span + step * rows, rows), rows), :lanes] = dq.astype(out_ref.dtype)
    sum_ref[0:1, :lanes] += jnp.sum(dq.astype(exact), axis=0, keepdims=True)

    @pl.when(step == pl.num_programs(0) - 1)
    def _():
        head = lax.broadcasted_iota(jnp.int32, dk_sum.shape, 1) < hd
        dk = jnp.where(head, dk_sum[...] * scale, 0.0)
        dv = dv_sum[...].astype(out_ref.dtype)
        out_ref[:, lanes : 2 * lanes] = dk.astype(out_ref.dtype)
        out_ref[:, 2 * lanes :] = dv
        sum_ref[0:1, 2 * lanes :] = jnp.sum(dv.astype(exact), axis=0, keepdims=True)


def attend_back(q, q_at, k, k_at, v, v_at, do, e, inverse, hd, rows, span, kind):
    tokens, keys = q.shape[0], k.shape[0]
    scale = 1.0 / hd**0.5
    steps = tokens // rows
    return pl.pallas_call(
        functools.partial(attend_back_kernel, hd, scale, span),
        grid=(steps,),
        in_specs=[
            pl.BlockSpec((rows, lanes), lambda i: (i, q_at)),
            pl.BlockSpec((keys, lanes), lambda i: (0, k_at)),
            pl.BlockSpec((keys, lanes), lambda i: (0, v_at)),
            pl.BlockSpec((rows // lanes, hd, lanes), lambda i: (i, 0, 0)),
            pl.BlockSpec((1, keys, rows), lambda i: (i, 0, 0)),
            pl.BlockSpec((1, 1, rows), lambda i: (i, 0, 0)),
        ],
        out_specs=[pl.BlockSpec((keys, 3 * lanes), lambda i: (0, 0)), pl.BlockSpec((8, 3 * lanes), lambda i: (0, 0))],
        out_shape=[pltpu.HBM((keys, 3 * lanes), kind), jax.ShapeDtypeStruct((8, 3 * lanes), exact)],
        scratch_shapes=[
            pltpu.VMEM((lanes, keys), low),
            pltpu.VMEM((keys, lanes), exact),
            pltpu.VMEM((keys, lanes), exact),
        ],
        compiler_params=params(14 * keys // 1024),
        cost_estimate=small_cost,
        name="attend_back",
    )(q, k, v, do, far_off(e), inverse)


def body(
    hidden_in,
    clip_lengths,
    ln1_gain,
    ln1_bias,
    w_query,
    b_query,
    w_key,
    w_value,
    b_value,
    w_out,
    b_out,
    ln2_gain,
    ln2_bias,
    w_fc1,
    b_fc1,
    w_fc2,
    b_fc2,
    cotangent,
):
    micro, rows, width = hidden_in.shape
    at = Layout(micro)
    place = at.place
    hd = width // heads
    own = 2 * rows
    tokens = at.half * own
    clips = clip_lengths.shape[1]
    chunk = width // at.block
    step_rows = 256

    vectors = [at.to_block(v) for v in (ln1_gain, ln1_bias, b_query, b_value, b_out, ln2_gain, ln2_bias, b_fc2)]
    ff_bias = at.to_block(b_fc1)
    ff_rows = ff_bias.shape[0]
    first, second = pack(place, hidden_in, jnp.stack(vectors), ff_bias[None])
    blocked = [at.to_block(w) for w in (w_query, w_key, w_value, w_fc1)]
    w_in, w1 = deal(*blocked, hd, at.block)
    ff = blocked[3].shape[1] // heads
    second = at.partner(second)
    wo_shard = at.to_block(w_out)
    g_far = jnp.concatenate([lax.dynamic_index_in_dim(cotangent, 1 - at.mine, 0, False), wo_shard], axis=0)
    second, w_in, w1, g_far = together(second, w_in, w1, g_far)

    x_own, small, *parts = arrange(place, first, second, rows)
    marks = []
    small_far = at.swapped(small, 1)
    parts[2] = jnp.concatenate([parts[2], small[None], small_far[None]], axis=1)
    c1 = small.reshape(2, extra_rows, width)[:, 0, lanes : lanes + ff_rows].reshape(1, 2 * ff_rows).astype(exact)
    w2_shard = at.to_block(w_fc2)
    mine, others, (g_far, *w2_far) = at.gather_tree(parts, [g_far, w2_shard[: ff_rows // 2], w2_shard[ff_rows // 2 :]])
    w2 = jnp.concatenate(at.ordered(w2_shard, jnp.concatenate(w2_far, axis=0)), axis=0)
    g_far, wo_far = g_far[:rows], g_far[rows:]
    wo = jnp.concatenate(at.ordered(wo_shard, wo_far), axis=0)
    *mine, w_in, wo = together(*mine, w_in, wo)
    w_in = at.exchange_block(w_in)
    wo = at.gather_half(wo).reshape(heads, 2, chunk, width).transpose(1, 0, 2, 3).reshape(width, width)
    before = norm(place, False, mine, (), hd, own, chunk)
    a1, table = norm(place, True, others, before, hd, own, chunk)
    w_in, a1, table = together(w_in, a1, table)

    w1 = at.exchange_block(tie(w1, w_in))
    w_in = w_in.reshape(width, 3 * hd)
    g_own = jnp.concatenate(at.ordered(lax.dynamic_index_in_dim(cotangent, at.mine, 0, False), g_far), axis=0)
    g_all = at.gather_half(g_own)

    lengths = lax.dynamic_index_in_dim(clip_lengths, at.mine, 0, False)
    ends = jnp.cumsum(lengths)
    ends = ends - at.me // at.block * tokens

    a1 = a1.reshape(tokens, width)
    qkv, w_pad = project(place, ends, a1, w_in, table, hd, rows)
    span = 0
    qkv_at = (qkv, 0, qkv, 1, qkv, 2)
    if at.blocks > 1:
        span = tokens // 2
        ahead = [(d, d + at.block) for d in range(at.count - at.block)]
        behind = [(d + at.block, d) for d in range(at.count - at.block)]
        nothing = jnp.where(jnp.arange(2 * lanes)[None] == hd + clips, 1.0, 0.0).astype(low)
        kv = qkv[:, lanes:]
        slots = kv.reshape(heads, 2, rows, 2 * lanes)
        before = at.send(slots[:, 1].reshape(span, 2 * lanes), ahead)
        after = at.send(slots[:, 0].reshape(span, 2 * lanes), behind)
        before = jnp.where(at.me < at.block, nothing, before)
        after = jnp.where(at.me >= at.count - at.block, nothing, after)
        kv = jnp.concatenate([before, kv, after], axis=0)
        qkv_at = (qkv, 0, kv, 0, kv, 1)
    o_head, expo, inverse = attend(*qkv_at, hd, step_rows)
    o_head, w1 = together(o_head, w1)
    w1 = unfolded(w1, ff)
    o_own = at.exchange_half(o_head)

    x2, *parts = join(x_own, o_own, wo, table)
    g_split = g_all.reshape(8, 2, own, width)
    mine, others, _ = at.gather_tree(parts)

    *before, kept, sum_c = feed(place, False, mine, g_split, w1, w2, c1, (), own, low)
    hid, du, y, away, sum_c2 = feed(place, True, others, g_split, w1, w2, c1, before, own, low)
    y = lax.psum_scatter(y.reshape(tokens, width), "dev", scatter_dimension=0, tiled=True, axis_index_groups=at.halves)
    marks, made = [], []

    def second_terms(marks):
        made.append(fc2_grad(tie(hid, marks[0]), g_split))
        return made

    def first_terms(marks):
        made.append(fc1_grad(place, mine, others, tie(du, marks[1]), chunk))
        return made[1:]

    kept, got = at.reduce_half(away, kept, marks, {1: second_terms, 2: first_terms})
    back_w2 = at.exchanged(tie(made[0], marks[1]))
    d_w1 = made[1]
    *sums, d_w1 = together(*kept, *got, *back_w2, d_w1)
    kept, got, back_w2 = sums[:3], sums[3:6], sums[6:]

    dx2, ga_own, do_own, sum2 = second_back(kept, got, x2, g_own, table, wo, hd)
    do_head = at.exchange_half(do_own)
    ga = at.gather_half(ga_own).reshape(tokens, width)
    d_w1 = at.exchange_block(tie(d_w1, do_head))

    kind = low if at.blocks == 1 else exact
    dqkv, sum_in = attend_back(*qkv_at, do_head, expo, inverse, hd, step_rows, span, kind)
    if at.blocks > 1:
        dkv = dqkv[:, lanes:]
        to_before = at.send(dkv[:span].astype(low), behind).astype(exact)
        to_after = at.send(dkv[span + tokens :].astype(low), ahead).astype(exact)
        halo = jnp.stack([t.reshape(heads, rows, 2 * lanes) for t in (to_after, to_before)], axis=1)
        dkv = dkv[span : span + tokens] + halo.reshape(tokens, 2 * lanes)
        dqkv = jnp.concatenate([dqkv[span : span + tokens, :lanes], dkv], axis=1).astype(low)
        sum_in = jnp.broadcast_to(jnp.sum(dqkv.astype(exact), axis=0, keepdims=True), (8, 3 * lanes))
    dqkv, sum_in, y, d_w1 = together(dqkv, sum_in, y, d_w1)
    split = dqkv.reshape(8, 2, own, 3 * lanes)
    away = terms(place, True, split, w_pad, 1, low)
    marks, made = [], []

    def projections(marks):
        made.append(head_grad(place, a1, tie(dqkv, marks[0]), sum2, sum_in, sum_c, sum_c2, hd, chunk, at.block))
        return made

    def output_weight(marks):
        late, o_late = together(ga, o_head, marks[1])[:2]
        made.append(output_grad(o_late, late.reshape(at.half, own, width)))
        return made[1:]

    kept, got = at.reduce_half(away, terms(place, False, split, w_pad, 1, low), marks, {1: projections, 2: output_weight})
    d_in = at.exchange_block(tie(made[0], marks[1]))
    kept_first, d_in = together(kept[0], d_in)
    kept = (kept_first, *kept[1:])

    dx, vec = first_back(kept, got, x_own, dx2, table, chunk, at.block)
    y, d_w1, *back_w2 = together(y, d_w1, *back_w2, dx)[:4]
    out = (x2 + (y.astype(exact) + table[7])).astype(low)

    input_grad = at.exchanged(dx.reshape(2, rows, width))
    layer_out = at.exchanged(out.reshape(2, rows, width))
    layer_out, input_grad = (jnp.stack(at.ordered(*v)).astype(exact) for v in (layer_out, input_grad))
    back_wo = at.send_rows_back(made[1])
    grad_w2 = at.from_block(back_w2[0].astype(exact) + back_w2[1].astype(exact))
    grad_w1 = at.from_block(collect_hidden(d_w1, ff))
    grad_wo = at.from_block(back_wo[0].astype(exact) + back_wo[1].astype(exact))
    vec = jnp.sum(at.exchange_block(vec), axis=(0, 1))
    grad_g1 = at.from_block(vec[:chunk])
    grad_b1 = at.from_block(vec[lanes // 2 : lanes // 2 + chunk])
    *grads, vec = collect(d_in, hd)
    grad_wq, grad_wk, grad_wv = (at.from_block(v) for v in grads)
    pieces = [at.from_block(vec[i]) for i in range(6)]
    grad_g2, grad_b2, grad_bo, grad_bf2, grad_bq, grad_bv = pieces
    grad_c1 = at.from_block(vec[8 : 8 + ff_rows // chunk].reshape(ff_rows))
    return (
        layer_out,
        input_grad,
        grad_g1,
        grad_b1,
        grad_wq,
        grad_bq,
        grad_wk,
        grad_wv,
        grad_bv,
        grad_wo,
        grad_bo,
        grad_g2,
        grad_b2,
        grad_w1,
        grad_c1,
        grad_w2,
        grad_bf2,
    )


def solution(mesh):
    tokens, vector, matrix = P(None, "dev", None), P("dev"), P("dev", None)
    grads = (vector, vector, matrix, vector, matrix, matrix, vector, matrix, vector, vector, vector, matrix, vector, matrix, vector)
    return jax.shard_map(
        body,
        mesh=mesh,
        in_specs=(tokens, P()) + grads + (tokens,),
        out_specs=(tokens, tokens) + grads,
        check_vma=False,
    )
```

profile of v0, /device:TPU:0, one launch (start us, length us, event | category | flops | bytes accessed | tf_op | source)
XLA Modules:
  0.0 406.6 jit_solution(8243148074003478457)
XLA Ops:
  10.5 4.1 %collective-permute-start = (bf16[72,1280]{1,0:T(8,128)(2,1)S(1)}, bf16[72,1280]{1,0:T(8,128)(2,1)S(1)}, u32[]{:S(2)}, u32[]{:S(2)}) collective-permute-start(bf16[72,1280]{1,0:T(8,128)(2,1)S(1)} %get-tuple-element.168), channel_id=1, source_target_pairs={{0,16},{1,17},{2,18},{3,19},{4,20},{5,21},{6,22},{7,23},{8,24},{9,... | collective-permute-start | bytes 552968 | tf_op jit(solution)/shard_map/ppermute | solution.py:67
  19.2 2.5 deal.1
  26.7 2.9 collective-permute-start.2
  31.1 2.0 collective-permute-done.2.refs_3_
  33.1 6.1 %collective-permute-done.3 = bf16[104,1280]{1,0:T(8,128)(2,1)S(1)} collective-permute-done((bf16[104,1280]{1,0:T(8,128)(2,1)S(1)}, bf16[104,1280]{1,0:T(8,128)(2,1)S(1)}, u32[]{:S(2)}, u32[]{:S(2)}) %collective-permute-start.3) | collective-permute-done | bytes 266272 | tf_op jit(solution)/shard_map/ppermute | solution.py:67
  43.7 1.7 collective-permute-start.7
  45.5 8.5 %collective-permute-done.7 = bf16[80,1280]{1,0:T(8,128)(2,1)S(1)} collective-permute-done((bf16[80,1280]{1,0:T(8,128)(2,1)S(1)}, bf16[80,1280]{1,0:T(8,128)(2,1)S(1)}, u32[]{:S(2)}, u32[]{:S(2)}) %collective-permute-start.7) | collective-permute-done | bytes 204832 | tf_op jit(solution)/shard_map/ppermute | solution.py:67
  62.1 10.3 %collective-permute-done.11 = bf16[80,1280]{1,0:T(8,128)(2,1)S(1)} collective-permute-done((bf16[80,1280]{1,0:T(8,128)(2,1)}, bf16[80,1280]{1,0:T(8,128)(2,1)S(1)}, u32[]{:S(2)}, u32[]{:S(2)}) %collective-permute-start.11) | collective-permute-done | bytes 204832 | tf_op jit(solution)/shard_map/ppermute | solution.py:67
  75.6 3.9 all-to-all-start
  85.0 7.1 %norm.2 = (bf16[8,2,128,1280]{3,2,1,0:T(8,128)(2,1)}, f32[8,1280]{1,0:T(8,128)S(1)}) custom-call(s32[7]{0:T(128)S(1)} %stack.76.place_ref, bf16[4,48,1280]{2,1,0:T(8,128)(2,1)} %get-tuple-element.193.refs_0_, bf16[4,48,1280]{2,1,0:T(8,128)(2,1)S(1)} %copy-done.26, bf16[4,64,1280]{2,1,0:T(8,128)(2,1)S(1)} %get-tuple-element.195.refs_2_, ...), custom_call_target="tpu_custom_call" | custom-call | flops 1024 | bytes 1024 | tf_op jit(solution)/shard_map/norm/pallas_call | solution.py:420
  92.1 3.9 norm.3
  96.0 3.8 all-to-all-done
  99.8 2.6 all-to-all-start.1
  102.7 7.3 %project.1 = (bf16[2048,384]{1,0:T(8,128)(2,1)S(1)}, bf16[1280,384]{1,0:T(8,128)(2,1)}) custom-call(s32[7]{0:T(128)S(1)} %stack.76.place_ref, s32[3]{0:T(128)S(1)} %subtract_bitcast_fusion.ends_ref, bf16[2048,1280]{1,0:T(8,128)(2,1)} %bitcast.94, bf16[1280,240]{1,0:T(8,128)(2,1)S(1)} %bitcast.89, f32[8,1280]{1,0:T(8,128)S(1)} %get-tuple-element.205.table_ref.refs_8_), custom_call_target="tpu_custom_call" | custom-call | flops 1024 | bytes 1024 | tf_op jit(solution)/shard_map/project/pallas_call | solution.py:476
  110.0 12.3 %attend.1 = (bf16[16,80,128]{2,1,0:T(8,128)(2,1)}, bf16[8,2048,256]{2,1,0:T(8,128)(2,1)}, f32[8,1,256]{2,1,0:T(1,128)S(1)}) custom-call(bf16[2048,384]{1,0:T(8,128)(2,1)S(1)} %get-tuple-element.206.q_ref.k_ref.v_ref, bf16[2048,384]{1,0:T(8,128)(2,1)S(1)} %get-tuple-element.206.q_ref.k_ref.v_ref, bf16[2048,384]{1,0:T(8,128)(2,1)S(1)} %get-tuple-element.206.q_ref.k_ref.v_ref), custom_call_target="tpu_custom_call" | custom-call | flops 1024 | bytes 1024 | tf_op jit(solution)/shard_map/attend/pallas_call | solution.py:896
  122.3 2.1 all-to-all-done.1.in_ref
  124.5 3.8 all-to-all-start.2
  128.5 4.1 %copy.39 = bf16[16,2,40,1280]{3,2,0,1:T(8,128)(2,1)} copy(bf16[16,2,40,1280]{3,2,1,0:T(8,128)(2,1)} %bitcast.103) | data formatting | bytes 6553600 | tf_op jit(solution)/shard_map/reshape | solution.py:1041
  132.6 4.1 %all-to-all-done.2.o_ref = bf16[16,80,128]{2,1,0:T(8,128)(2,1)S(1)} async-done(((bf16[16,80,128]{2,1,0:T(8,128)(2,1)}), bf16[16,80,128]{2,1,0:T(8,128)(2,1)S(1)}, u32[]{:S(2)}, u32[]{:S(2)}) %all-to-all-start.2) | async-done | bytes 327712 | tf_op jit(solution)/shard_map/all_to_all | solution.py:103
  136.8 2.9 join.1
  145.0 4.7 %collective-permute-done.22.refs_5_ = bf16[1,32,1280]{2,1,0:T(8,128)(2,1)S(1)} collective-permute-done((bf16[1,32,1280]{2,1,0:T(8,128)(2,1)S(1)}, bf16[1,32,1280]{2,1,0:T(8,128)(2,1)S(1)}, u32[]{:S(2)}, u32[]{:S(2)}) %collective-permute-start.22) | collective-permute-done | bytes 81952 | tf_op jit(solution)/shard_map/ppermute | solution.py:67
  151.1 2.5 collective-permute-start.24
  155.2 8.2 %collective-permute-done.25.refs_5_ = bf16[2,32,1280]{2,1,0:T(8,128)(2,1)S(1)} collective-permute-done((bf16[2,32,1280]{2,1,0:T(8,128)(2,1)S(1)}, bf16[2,32,1280]{2,1,0:T(8,128)(2,1)S(1)}, u32[]{:S(2)}, u32[]{:S(2)}) %collective-permute-start.25) | collective-permute-done | bytes 163872 | tf_op jit(solution)/shard_map/ppermute | solution.py:67
  166.2 2.0 collective-permute-start.26
  172.6 4.1 %collective-permute-done.28.refs_5_ = bf16[4,32,1280]{2,1,0:T(8,128)(2,1)} collective-permute-done((bf16[4,32,1280]{2,1,0:T(8,128)(2,1)S(1)}, bf16[4,32,1280]{2,1,0:T(8,128)(2,1)}, u32[]{:S(2)}, u32[]{:S(2)}) %collective-permute-start.28) | collective-permute-done | bytes 327712 | tf_op jit(solution)/shard_map/ppermute | solution.py:67
  183.2 10.8 %feed.2 = (bf16[8,2,128,320]{3,2,1,0:T(8,128)(2,1)}, bf16[8,2,128,320]{3,2,1,0:T(8,128)(2,1)}, bf16[8,2,128,1280]{3,2,1,0:T(8,128)(2,1)}, bf16[8,128,1280]{2,1,0:T(8,128)(2,1)}, f32[1,320]{1,0:T(1,128)S(1)}) custom-call(s32[7]{0:T(128)S(1)} %stack.76.place_ref, bf16[4,48,1280]{2,1,0:T(8,128)(2,1)} %get-tuple-element.219.refs_0_, ...), custom_call_target="tpu_custom_call" | custom-call | flops 1024 | bytes 1024 | tf_op jit(solution)/shard_map/feed/pallas_call | solution.py:670
  194.0 10.8 %feed.3 = (bf16[8,2,128,320]{3,2,1,0:T(8,128)(2,1)}, bf16[8,2,128,320]{3,2,1,0:T(8,128)(2,1)}, bf16[8,2,128,1280]{3,2,1,0:T(8,128)(2,1)}, bf16[8,128,1280]{2,1,0:T(8,128)(2,1)}, f32[1,320]{1,0:T(1,128)S(1)}) custom-call(s32[7]{0:T(128)S(1)} %stack.76.place_ref, ...), custom_call_target="tpu_custom_call", output_to_operand_aliasing={{0}: (11, {}), {1}: (12, {}), {2}: (13, {})} | custom-call | flops 1024 | bytes 1024 | tf_op jit(solution)/shard_map/feed/pallas_call | solution.py:670
  205.5 4.7 %collective-permute-done.35.refs_1_ = bf16[8,128,1280]{2,1,0:T(8,128)(2,1)S(1)} collective-permute-done((bf16[8,128,1280]{2,1,0:T(8,128)(2,1)}, bf16[8,128,1280]{2,1,0:T(8,128)(2,1)S(1)}, u32[]{:S(2)}, u32[]{:S(2)}) %collective-permute-start.35) | collective-permute-done | bytes 2621472 | tf_op jit(solution)/shard_map/ppermute | solution.py:67
  210.2 1.7 copy-done.11
  212.0 1.8 split_terms.6
  216.7 5.5 %fc2_grad.1 = bf16[2,160,1280]{2,1,0:T(8,128)(2,1)S(1)} custom-call(bf16[8,2,128,320]{3,2,1,0:T(8,128)(2,1)} %get-tuple-element.235.hid_ref, bf16[8,2,128,1280]{3,2,1,0:T(8,128)(2,1)} %bitcast.98), custom_call_target="tpu_custom_call" | custom-call | flops 1024 | bytes 1024 | tf_op jit(solution)/shard_map/fc2_grad/pallas_call | solution.py:546
  222.2 10.7 %collective-permute-done.36.refs_3_ = bf16[4,48,1280]{2,1,0:T(8,128)(2,1)S(1)} collective-permute-done((bf16[4,48,1280]{2,1,0:T(8,128)(2,1)S(1)}, bf16[4,48,1280]{2,1,0:T(8,128)(2,1)S(1)}, u32[]{:S(2)}, u32[]{:S(2)}) %collective-permute-start.36) | collective-permute-done | bytes 491552 | tf_op jit(solution)/shard_map/ppermute | solution.py:67
  235.5 1.8 collective-permute-start.45
  237.3 1.9 collective-permute-start.39
  240.9 8.6 %fc1_grad.1 = bf16[32,8,1600]{2,1,0:T(8,128)(2,1)} custom-call(s32[7]{0:T(128)S(1)} %stack.76.place_ref, bf16[4,48,1280]{2,1,0:T(8,128)(2,1)} %get-tuple-element.219.refs_0_, bf16[4,48,1280]{2,1,0:T(8,128)(2,1)} %get-tuple-element.220.refs_1_, bf16[4,32,1280]{2,1,0:T(8,128)(2,1)S(1)} %copy-done.17, bf16[4,48,1280]{2,1,0:T(8,128)(2,1)} %collective-permute-done.26.refs_3_, ...), custom_call_target="tpu_custom_call" | custom-call | flops 1024 | bytes 1024 | tf_op jit(solution)/shard_map/fc1_grad/pallas_call | solution.py:589
  249.5 5.9 %collective-permute-done.41.refs_5_ = bf16[2,32,1280]{2,1,0:T(8,128)(2,1)S(1)} collective-permute-done((bf16[2,32,1280]{2,1,0:T(8,128)(2,1)S(1)}, bf16[2,32,1280]{2,1,0:T(8,128)(2,1)S(1)}, u32[]{:S(2)}, u32[]{:S(2)}) %collective-permute-start.41) | collective-permute-done | bytes 163872 | tf_op jit(solution)/shard_map/ppermute | solution.py:67
  256.5 2.5 collective-permute-start.43
  260.3 3.2 collective-permute-done.44.refs_5_
  263.8 3.6 second_back.1
  268.3 14.8 %all_to_all.35.do_ref = bf16[16,80,128]{2,1,0:T(8,128)(2,1)} all-to-all(bf16[16,80,128]{2,1,0:T(8,128)(2,1)S(1)} %get-tuple-element.261), channel_id=1, replica_groups={{0,1,2,3,4,5,6,7,8,9,10,11,12,13,14,15},{16,17,18,19,20,21,22,23,24,25,..., dimensions={0} | all-to-all | bytes 655360 | tf_op jit(solution)/shard_map/all_to_all | solution.py:103
  283.1 3.5 all-to-all-start.4
  287.5 15.8 %attend_back.1 = (bf16[2048,384]{1,0:T(8,128)(2,1)}, f32[8,384]{1,0:T(8,128)S(1)}) custom-call(bf16[2048,384]{1,0:T(8,128)(2,1)S(1)} %get-tuple-element.206.q_ref.k_ref.v_ref, bf16[2048,384]{1,0:T(8,128)(2,1)S(1)} %get-tuple-element.206.q_ref.k_ref.v_ref, bf16[2048,384]{1,0:T(8,128)(2,1)S(1)} %get-tuple-element.206.q_ref.k_ref.v_ref, ...), custom_call_target="tpu_custom_call" | custom-call | flops 1024 | bytes 1024 | tf_op jit(solution)/shard_map/attend_back/pallas_call | solution.py:963
  303.3 7.0 %all-to-all-done.4.in_ref = bf16[32,8,1600]{2,1,0:T(8,128)(2,1)S(1)} async-done(((bf16[32,8,1600]{2,1,0:T(8,128)(2,1)}), bf16[32,8,1600]{2,1,0:T(8,128)(2,1)S(1)}, u32[]{:S(2)}, u32[]{:S(2)}) %all-to-all-start.4) | async-done | bytes 819232 | tf_op jit(solution)/shard_map/all_to_all | solution.py:106
  311.8 2.4 terms.3
  314.3 2.4 terms.2.refs_0_
  316.7 2.6 collective-permute-done.46.refs_1_
  319.3 1.8 split_terms.9
  321.1 2.4 collective-permute-start.47
  325.0 7.5 %head_grad.1 = bf16[32,40,256]{2,1,0:T(8,128)(2,1)} custom-call(s32[7]{0:T(128)S(1)} %stack.76.place_ref, bf16[2048,1280]{1,0:T(8,128)(2,1)} %bitcast.95, bf16[2048,384]{1,0:T(8,128)(2,1)S(1)} %copy-done.3, f32[8,1280]{1,0:T(8,128)S(1)} %get-tuple-element.280.sum2_ref, f32[8,384]{1,0:T(8,128)S(1)} %get-tuple-element.281.sum_in_ref, ...), custom_call_target="tpu_custom_call" | custom-call | flops 1024 | bytes 1024 | tf_op jit(solution)/shard_map/head_grad/pallas_call | solution.py:816
  332.5 5.5 %collective-permute-done.47.refs_3_ = bf16[4,48,1280]{2,1,0:T(8,128)(2,1)S(1)} collective-permute-done((bf16[4,48,1280]{2,1,0:T(8,128)(2,1)S(1)}, bf16[4,48,1280]{2,1,0:T(8,128)(2,1)S(1)}, u32[]{:S(2)}, u32[]{:S(2)}) %collective-permute-start.47) | collective-permute-done | bytes 491552 | tf_op jit(solution)/shard_map/ppermute | solution.py:67
  338.0 1.9 split_terms.10
  342.2 3.7 all-to-all-start.5
  345.9 1.8 collective-permute-start.50
  350.7 4.2 %output_grad.1 = bf16[2,40,1280]{2,1,0:T(8,128)(2,1)S(1)} custom-call(bf16[16,80,128]{2,1,0:T(8,128)(2,1)} %get-tuple-element.292.o_ref, bf16[16,128,1280]{2,1,0:T(8,128)(2,1)} %bitcast.102), custom_call_target="tpu_custom_call" | custom-call | flops 1024 | bytes 1024 | tf_op jit(solution)/shard_map/output_grad/pallas_call | solution.py:623
  355.9 4.2 %collective-permute-done.50.refs_3_ = bf16[2,48,1280]{2,1,0:T(8,128)(2,1)} collective-permute-done((bf16[2,48,1280]{2,1,0:T(8,128)(2,1)}, bf16[2,48,1280]{2,1,0:T(8,128)(2,1)}, u32[]{:S(2)}, u32[]{:S(2)}) %collective-permute-start.50) | collective-permute-done | bytes 245792 | tf_op jit(solution)/shard_map/ppermute | solution.py:67
  361.3 2.3 split_terms.11
  365.1 2.1 collective-permute-start.53
  368.6 1.9 collective-permute-start.55
  371.3 2.0 collective-permute-done.55.refs_5_
  375.2 2.2 first_back.1
  378.6 2.9 collective-permute-start.56
  382.3 4.6 %all-to-all-start.6 = ((f32[32,1,128]{2,1,0:T(1,128)}), f32[32,1,128]{2,1,0:T(1,128)S(1)}, u32[]{:S(2)}, u32[]{:S(2)}) async-start(f32[32,1,128]{2,1,0:T(1,128)} %get-tuple-element.308), calls=%async_computation.7 | async-start | bytes 32768 | tf_op jit(solution)/shard_map/all_to_all | solution.py:106
  389.6 1.9 collect_hidden.1
  392.2 3.6 all-to-all-done.6
  (260 shorter events, 95.6 us)
Async XLA Ops:
  7.2 121.3 %all-gather.7.cloned.1.call-start = ((), (), s32[]{:S(2)}) async-start(), calls=%async_computation.9 | async-start | bytes 3481600 | tf_op jit(solution)/shard_map/all_gather | solution.py:100
  10.5 12.7 %collective-permute-start = (bf16[72,1280]{1,0:T(8,128)(2,1)S(1)}, bf16[72,1280]{1,0:T(8,128)(2,1)S(1)}, u32[]{:S(2)}, u32[]{:S(2)}) collective-permute-start(bf16[72,1280]{1,0:T(8,128)(2,1)S(1)} %get-tuple-element.168), channel_id=1, source_target_pairs={{0,16},{1,17},{2,18},{3,19},{4,20},{5,21},{6,22},{7,23},{8,24},{9,... | collective-permute-start | bytes 552968 | tf_op jit(solution)/shard_map/ppermute | solution.py:67
  23.8 15.4 %collective-permute-start.3 = (bf16[104,1280]{1,0:T(8,128)(2,1)S(1)}, bf16[104,1280]{1,0:T(8,128)(2,1)S(1)}, u32[]{:S(2)}, u32[]{:S(2)}) collective-permute-start(bf16[104,1280]{1,0:T(8,128)(2,1)S(1)} %pad_maximum_fusion.2), channel_id=1, source_target_pairs={{0,16},{1,17},{2,18},{3,19},{4,20},{5,21},{6,22},{7,23},{8,24},{9,... | collective-permute-start | bytes 798728 | tf_op jit(solution)/shard_map/ppermute | solution.py:67
  25.1 14.2 %collective-permute-start.5 = (bf16[1,64,1280]{2,1,0:T(8,128)(2,1)S(1)}, bf16[1,64,1280]{2,1,0:T(8,128)(2,1)S(1)}, u32[]{:S(2)}, u32[]{:S(2)}) collective-permute-start(bf16[1,64,1280]{2,1,0:T(8,128)(2,1)S(1)} %pad_maximum_fusion.4.refs_2_), channel_id=1, source_target_pairs={{0,2},{1,3},{2,0},{3,1},{4,6},{5,7},{6,4},{7,5},{8,10},{9,11},{10,... | collective-permute-start | bytes 491528 | tf_op jit(solution)/shard_map/ppermute | solution.py:67
  26.7 6.4 %collective-permute-start.2 = (bf16[1,48,1280]{2,1,0:T(8,128)(2,1)S(1)}, bf16[1,48,1280]{2,1,0:T(8,128)(2,1)S(1)}, u32[]{:S(2)}, u32[]{:S(2)}) collective-permute-start(bf16[1,48,1280]{2,1,0:T(8,128)(2,1)S(1)} %get-tuple-element.173.refs_0_), channel_id=1, source_target_pairs={{0,8},{1,9},{2,10},{3,11},{4,12},{5,13},{6,14},{7,15},{8,0},{9,1},... | collective-permute-start | bytes 368648 | tf_op jit(solution)/shard_map/ppermute | solution.py:67
  29.6 9.7 %collective-permute-start.4 = (bf16[1,48,1280]{2,1,0:T(8,128)(2,1)S(1)}, bf16[1,48,1280]{2,1,0:T(8,128)(2,1)S(1)}, u32[]{:S(2)}, u32[]{:S(2)}) collective-permute-start(bf16[1,48,1280]{2,1,0:T(8,128)(2,1)S(1)} %get-tuple-element.174.refs_1_), channel_id=1, source_target_pairs={{0,4},{1,5},{2,6},{3,7},{4,0},{5,1},{6,2},{7,3},{8,12},{9,13},{10,... | collective-permute-start | bytes 368648 | tf_op jit(solution)/shard_map/ppermute | solution.py:67
  40.0 14.0 %collective-permute-start.6 = (bf16[2,48,1280]{2,1,0:T(8,128)(2,1)S(1)}, bf16[2,48,1280]{2,1,0:T(8,128)(2,1)S(1)}, u32[]{:S(2)}, u32[]{:S(2)}) collective-permute-start(bf16[2,48,1280]{2,1,0:T(8,128)(2,1)S(1)} %get-tuple-element.180.refs_0_), channel_id=1, source_target_pairs={{0,4},{1,5},{2,6},{3,7},{4,0},{5,1},{6,2},{7,3},{8,12},{9,13},{10,... | collective-permute-start | bytes 737288 | tf_op jit(solution)/shard_map/ppermute | solution.py:67
  41.5 12.4 %collective-permute-start.8 = (bf16[2,48,1280]{2,1,0:T(8,128)(2,1)S(1)}, bf16[2,48,1280]{2,1,0:T(8,128)(2,1)S(1)}, u32[]{:S(2)}, u32[]{:S(2)}) collective-permute-start(bf16[2,48,1280]{2,1,0:T(8,128)(2,1)S(1)} %get-tuple-element.181.refs_1_), channel_id=1, source_target_pairs={{0,2},{1,3},{2,0},{3,1},{4,6},{5,7},{6,4},{7,5},{8,10},{9,11},{10,... | collective-permute-start | bytes 737288 | tf_op jit(solution)/shard_map/ppermute | solution.py:67
  43.0 13.1 %collective-permute-start.9 = (bf16[2,64,1280]{2,1,0:T(8,128)(2,1)S(1)}, bf16[2,64,1280]{2,1,0:T(8,128)(2,1)S(1)}, u32[]{:S(2)}, u32[]{:S(2)}) collective-permute-start(bf16[2,64,1280]{2,1,0:T(8,128)(2,1)S(1)} %get-tuple-element.182.refs_2_), channel_id=1, source_target_pairs={{0,8},{1,9},{2,10},{3,11},{4,12},{5,13},{6,14},{7,15},{8,0},{9,1},... | collective-permute-start | bytes 983048 | tf_op jit(solution)/shard_map/ppermute | solution.py:67
  43.7 10.2 %collective-permute-start.7 = (bf16[80,1280]{1,0:T(8,128)(2,1)S(1)}, bf16[80,1280]{1,0:T(8,128)(2,1)S(1)}, u32[]{:S(2)}, u32[]{:S(2)}) collective-permute-start(bf16[80,1280]{1,0:T(8,128)(2,1)S(1)} %get-tuple-element.183), channel_id=1, source_target_pairs={{0,16},{1,17},{2,18},{3,19},{4,20},{5,21},{6,22},{7,23},{8,24},{9,... | collective-permute-start | bytes 614408 | tf_op jit(solution)/shard_map/ppermute | solution.py:67
  57.2 15.1 %collective-permute-start.10 = (bf16[4,48,1280]{2,1,0:T(8,128)(2,1)}, bf16[4,48,1280]{2,1,0:T(8,128)(2,1)S(1)}, u32[]{:S(2)}, u32[]{:S(2)}) collective-permute-start(bf16[4,48,1280]{2,1,0:T(8,128)(2,1)} %get-tuple-element.193.refs_0_), channel_id=1, source_target_pairs={{0,2},{1,3},{2,0},{3,1},{4,6},{5,7},{6,4},{7,5},{8,10},{9,11},{10,... | collective-permute-start | bytes 1474568 | tf_op jit(solution)/shard_map/ppermute | solution.py:67
  57.7 15.7 %collective-permute-start.12 = (bf16[4,48,1280]{2,1,0:T(8,128)(2,1)S(1)}, bf16[4,48,1280]{2,1,0:T(8,128)(2,1)}, u32[]{:S(2)}, u32[]{:S(2)}) collective-permute-start(bf16[4,48,1280]{2,1,0:T(8,128)(2,1)S(1)} %get-tuple-element.194.refs_1_), channel_id=1, source_target_pairs={{0,8},{1,9},{2,10},{3,11},{4,12},{5,13},{6,14},{7,15},{8,0},{9,1},... | collective-permute-start | bytes 1474568 | tf_op jit(solution)/shard_map/ppermute | solution.py:67
  58.9 14.7 %collective-permute-start.13 = (bf16[4,64,1280]{2,1,0:T(8,128)(2,1)S(1)}, bf16[4,64,1280]{2,1,0:T(8,128)(2,1)S(1)}, u32[]{:S(2)}, u32[]{:S(2)}) collective-permute-start(bf16[4,64,1280]{2,1,0:T(8,128)(2,1)S(1)} %get-tuple-element.195.refs_2_), channel_id=1, source_target_pairs={{0,4},{1,5},{2,6},{3,7},{4,0},{5,1},{6,2},{7,3},{8,12},{9,13},{10,... | collective-permute-start | bytes 1966088 | tf_op jit(solution)/shard_map/ppermute | solution.py:67
  60.3 12.1 %collective-permute-start.11 = (bf16[80,1280]{1,0:T(8,128)(2,1)}, bf16[80,1280]{1,0:T(8,128)(2,1)S(1)}, u32[]{:S(2)}, u32[]{:S(2)}) collective-permute-start(bf16[80,1280]{1,0:T(8,128)(2,1)} %get-tuple-element.188), channel_id=1, source_target_pairs={{0,16},{1,17},{2,18},{3,19},{4,20},{5,21},{6,22},{7,23},{8,24},{9,... | collective-permute-start | bytes 614408 | tf_op jit(solution)/shard_map/ppermute | solution.py:67
  73.6 108.6 %all-gather.9.cloned.1.call-start = ((), (), s32[]{:S(2)}) async-start(), calls=%async_computation.10 | async-start | bytes 5570560 | tf_op jit(solution)/shard_map/all_gather | solution.py:100
  75.6 24.2 %all-to-all-start = ((bf16[32,40,240]{2,1,0:T(8,128)(2,1)}), bf16[32,40,240]{2,1,0:T(8,128)(2,1)S(1)}, u32[]{:S(2)}, u32[]{:S(2)}) async-start(bf16[32,40,240]{2,1,0:T(8,128)(2,1)} %get-tuple-element.192), calls=%async_computation | async-start | bytes 1310720 | tf_op jit(solution)/shard_map/all_to_all | solution.py:106
  79.8 12.3 %collective-permute-start.16 = (bf16[4,64,1280]{2,1,0:T(8,128)(2,1)S(1)}, bf16[4,64,1280]{2,1,0:T(8,128)(2,1)S(1)}, u32[]{:S(2)}, u32[]{:S(2)}) collective-permute-start(bf16[4,64,1280]{2,1,0:T(8,128)(2,1)S(1)} %get-tuple-element.195.refs_2_), channel_id=1, source_target_pairs={{0,1},{1,0},{2,3},{3,2},{4,5},{5,4},{6,7},{7,6},{8,9},{9,8},{10,11... | collective-permute-start | bytes 1966088 | tf_op jit(solution)/shard_map/ppermute | solution.py:67
  80.1 12.0 %collective-permute-start.19 = (bf16[4,64,1280]{2,1,0:T(8,128)(2,1)}, bf16[4,64,1280]{2,1,0:T(8,128)(2,1)S(1)}, u32[]{:S(2)}, u32[]{:S(2)}) collective-permute-start(bf16[4,64,1280]{2,1,0:T(8,128)(2,1)} %copy-done.23), channel_id=1, source_target_pairs={{0,1},{1,0},{2,3},{3,2},{4,5},{5,4},{6,7},{7,6},{8,9},{9,8},{10,11... | collective-permute-start | bytes 1966088 | tf_op jit(solution)/shard_map/ppermute | solution.py:67
  80.3 11.8 %collective-permute-start.15 = (bf16[4,48,1280]{2,1,0:T(8,128)(2,1)}, bf16[4,48,1280]{2,1,0:T(8,128)(2,1)S(1)}, u32[]{:S(2)}, u32[]{:S(2)}) collective-permute-start(bf16[4,48,1280]{2,1,0:T(8,128)(2,1)} %copy-done.25), channel_id=1, source_target_pairs={{0,1},{1,0},{2,3},{3,2},{4,5},{5,4},{6,7},{7,6},{8,9},{9,8},{10,11... | collective-permute-start | bytes 1474568 | tf_op jit(solution)/shard_map/ppermute | solution.py:67
  80.6 11.5 %collective-permute-start.17 = (bf16[4,48,1280]{2,1,0:T(8,128)(2,1)}, bf16[4,48,1280]{2,1,0:T(8,128)(2,1)S(1)}, u32[]{:S(2)}, u32[]{:S(2)}) collective-permute-start(bf16[4,48,1280]{2,1,0:T(8,128)(2,1)} %copy-done.27), channel_id=1, source_target_pairs={{0,1},{1,0},{2,3},{3,2},{4,5},{5,4},{6,7},{7,6},{8,9},{9,8},{10,11... | collective-permute-start | bytes 1474568 | tf_op jit(solution)/shard_map/ppermute | solution.py:67
  81.6 10.5 %collective-permute-start.18 = (bf16[4,48,1280]{2,1,0:T(8,128)(2,1)}, bf16[4,48,1280]{2,1,0:T(8,128)(2,1)S(1)}, u32[]{:S(2)}, u32[]{:S(2)}) collective-permute-start(bf16[4,48,1280]{2,1,0:T(8,128)(2,1)} %collective-permute-done.12.refs_4_), channel_id=1, source_target_pairs={{0,1},{1,0},{2,3},{3,2},{4,5},{5,4},{6,7},{7,6},{8,9},{9,8},{10,11... | collective-permute-start | bytes 1474568 | tf_op jit(solution)/shard_map/ppermute | solution.py:67
  99.8 24.6 %all-to-all-start.1 = ((bf16[32,8,1600]{2,1,0:T(8,128)(2,1)}), bf16[32,8,1600]{2,1,0:T(8,128)(2,1)S(1)}, u32[]{:S(2)}, u32[]{:S(2)}) async-start(bf16[32,8,1600]{2,1,0:T(8,128)(2,1)} %get-tuple-element.209), calls=%async_computation.1 | async-start | bytes 1703936 | tf_op jit(solution)/shard_map/all_to_all | solution.py:106
  124.5 12.3 %all-to-all-start.2 = ((bf16[16,80,128]{2,1,0:T(8,128)(2,1)}), bf16[16,80,128]{2,1,0:T(8,128)(2,1)S(1)}, u32[]{:S(2)}, u32[]{:S(2)}) async-start(bf16[16,80,128]{2,1,0:T(8,128)(2,1)} %get-tuple-element.292.o_ref), calls=%async_computation.2 | async-start | bytes 655360 | tf_op jit(solution)/shard_map/all_to_all | solution.py:103
  128.3 182.1 %reduce-scatter.2.cloned.1.call-start = ((), (), s32[]{:S(2)}) async-start(), calls=%async_computation.8 | async-start | bytes 5570560 | tf_op jit(solution)/shard_map/reduce_scatter | solution.py:1083
  140.5 9.3 %collective-permute-start.20 = (bf16[1,48,1280]{2,1,0:T(8,128)(2,1)S(1)}, bf16[1,48,1280]{2,1,0:T(8,128)(2,1)S(1)}, u32[]{:S(2)}, u32[]{:S(2)}) collective-permute-start(bf16[1,48,1280]{2,1,0:T(8,128)(2,1)S(1)} %get-tuple-element.213.refs_0_), channel_id=1, source_target_pairs={{0,8},{1,9},{2,10},{3,11},{4,12},{5,13},{6,14},{7,15},{8,0},{9,1},... | collective-permute-start | bytes 368648 | tf_op jit(solution)/shard_map/ppermute | solution.py:67
  141.7 8.1 %collective-permute-start.21 = (bf16[1,48,1280]{2,1,0:T(8,128)(2,1)S(1)}, bf16[1,48,1280]{2,1,0:T(8,128)(2,1)S(1)}, u32[]{:S(2)}, u32[]{:S(2)}) collective-permute-start(bf16[1,48,1280]{2,1,0:T(8,128)(2,1)S(1)} %get-tuple-element.214.refs_1_), channel_id=1, source_target_pairs={{0,4},{1,5},{2,6},{3,7},{4,0},{5,1},{6,2},{7,3},{8,12},{9,13},{10,... | collective-permute-start | bytes 368648 | tf_op jit(solution)/shard_map/ppermute | solution.py:67
  143.3 6.5 %collective-permute-start.22 = (bf16[1,32,1280]{2,1,0:T(8,128)(2,1)S(1)}, bf16[1,32,1280]{2,1,0:T(8,128)(2,1)S(1)}, u32[]{:S(2)}, u32[]{:S(2)}) collective-permute-start(bf16[1,32,1280]{2,1,0:T(8,128)(2,1)S(1)} %get-tuple-element.215.refs_2_), channel_id=1, source_target_pairs={{0,2},{1,3},{2,0},{3,1},{4,6},{5,7},{6,4},{7,5},{8,10},{9,11},{10,... | collective-permute-start | bytes 245768 | tf_op jit(solution)/shard_map/ppermute | solution.py:67
  150.0 13.3 %collective-permute-start.23 = (bf16[2,48,1280]{2,1,0:T(8,128)(2,1)S(1)}, bf16[2,48,1280]{2,1,0:T(8,128)(2,1)S(1)}, u32[]{:S(2)}, u32[]{:S(2)}) collective-permute-start(bf16[2,48,1280]{2,1,0:T(8,128)(2,1)S(1)} %get-tuple-element.216.refs_0_), channel_id=1, source_target_pairs={{0,4},{1,5},{2,6},{3,7},{4,0},{5,1},{6,2},{7,3},{8,12},{9,13},{10,... | collective-permute-start | bytes 737288 | tf_op jit(solution)/shard_map/ppermute | solution.py:67
  151.1 13.9 %collective-permute-start.24 = (bf16[2,48,1280]{2,1,0:T(8,128)(2,1)S(1)}, bf16[2,48,1280]{2,1,0:T(8,128)(2,1)S(1)}, u32[]{:S(2)}, u32[]{:S(2)}) collective-permute-start(bf16[2,48,1280]{2,1,0:T(8,128)(2,1)S(1)} %get-tuple-element.217.refs_1_), channel_id=1, source_target_pairs={{0,2},{1,3},{2,0},{3,1},{4,6},{5,7},{6,4},{7,5},{8,10},{9,11},{10,... | collective-permute-start | bytes 737288 | tf_op jit(solution)/shard_map/ppermute | solution.py:67
  153.6 9.7 %collective-permute-start.25 = (bf16[2,32,1280]{2,1,0:T(8,128)(2,1)S(1)}, bf16[2,32,1280]{2,1,0:T(8,128)(2,1)S(1)}, u32[]{:S(2)}, u32[]{:S(2)}) collective-permute-start(bf16[2,32,1280]{2,1,0:T(8,128)(2,1)S(1)} %get-tuple-element.218.refs_2_), channel_id=1, source_target_pairs={{0,8},{1,9},{2,10},{3,11},{4,12},{5,13},{6,14},{7,15},{8,0},{9,1},... | collective-permute-start | bytes 491528 | tf_op jit(solution)/shard_map/ppermute | solution.py:67
  166.2 12.5 %collective-permute-start.26 = (bf16[4,48,1280]{2,1,0:T(8,128)(2,1)}, bf16[4,48,1280]{2,1,0:T(8,128)(2,1)}, u32[]{:S(2)}, u32[]{:S(2)}) collective-permute-start(bf16[4,48,1280]{2,1,0:T(8,128)(2,1)} %get-tuple-element.219.refs_0_), channel_id=1, source_target_pairs={{0,2},{1,3},{2,0},{3,1},{4,6},{5,7},{6,4},{7,5},{8,10},{9,11},{10,... | collective-permute-start | bytes 1474568 | tf_op jit(solution)/shard_map/ppermute | solution.py:67
  168.2 11.5 %collective-permute-start.27 = (bf16[4,48,1280]{2,1,0:T(8,128)(2,1)}, bf16[4,48,1280]{2,1,0:T(8,128)(2,1)}, u32[]{:S(2)}, u32[]{:S(2)}) collective-permute-start(bf16[4,48,1280]{2,1,0:T(8,128)(2,1)} %get-tuple-element.220.refs_1_), channel_id=1, source_target_pairs={{0,8},{1,9},{2,10},{3,11},{4,12},{5,13},{6,14},{7,15},{8,0},{9,1},... | collective-permute-start | bytes 1474568 | tf_op jit(solution)/shard_map/ppermute | solution.py:67
  169.4 7.3 %collective-permute-start.28 = (bf16[4,32,1280]{2,1,0:T(8,128)(2,1)S(1)}, bf16[4,32,1280]{2,1,0:T(8,128)(2,1)}, u32[]{:S(2)}, u32[]{:S(2)}) collective-permute-start(bf16[4,32,1280]{2,1,0:T(8,128)(2,1)S(1)} %get-tuple-element.221.refs_2_), channel_id=1, source_target_pairs={{0,4},{1,5},{2,6},{3,7},{4,0},{5,1},{6,2},{7,3},{8,12},{9,13},{10,... | collective-permute-start | bytes 983048 | tf_op jit(solution)/shard_map/ppermute | solution.py:67
  170.1 6.6 %collective-permute-start.31 = (bf16[4,32,1280]{2,1,0:T(8,128)(2,1)S(1)}, bf16[4,32,1280]{2,1,0:T(8,128)(2,1)S(1)}, u32[]{:S(2)}, u32[]{:S(2)}) collective-permute-start(bf16[4,32,1280]{2,1,0:T(8,128)(2,1)S(1)} %get-tuple-element.221.refs_2_), channel_id=1, source_target_pairs={{0,1},{1,0},{2,3},{3,2},{4,5},{5,4},{6,7},{7,6},{8,9},{9,8},{10,11... | collective-permute-start | bytes 983048 | tf_op jit(solution)/shard_map/ppermute | solution.py:67
  172.0 21.9 %collective-permute-start.29 = (bf16[4,48,1280]{2,1,0:T(8,128)(2,1)}, bf16[4,48,1280]{2,1,0:T(8,128)(2,1)}, u32[]{:S(2)}, u32[]{:S(2)}) collective-permute-start(bf16[4,48,1280]{2,1,0:T(8,128)(2,1)} %get-tuple-element.219.refs_0_), channel_id=1, source_target_pairs={{0,1},{1,0},{2,3},{3,2},{4,5},{5,4},{6,7},{7,6},{8,9},{9,8},{10,11... | collective-permute-start | bytes 1474568 | tf_op jit(solution)/shard_map/ppermute | solution.py:67
  176.7 17.3 %collective-permute-start.30 = (bf16[4,48,1280]{2,1,0:T(8,128)(2,1)}, bf16[4,48,1280]{2,1,0:T(8,128)(2,1)}, u32[]{:S(2)}, u32[]{:S(2)}) collective-permute-start(bf16[4,48,1280]{2,1,0:T(8,128)(2,1)} %get-tuple-element.220.refs_1_), channel_id=1, source_target_pairs={{0,1},{1,0},{2,3},{3,2},{4,5},{5,4},{6,7},{7,6},{8,9},{9,8},{10,11... | collective-permute-start | bytes 1474568 | tf_op jit(solution)/shard_map/ppermute | solution.py:67
  177.5 16.5 %collective-permute-start.34 = (bf16[4,32,1280]{2,1,0:T(8,128)(2,1)}, bf16[4,32,1280]{2,1,0:T(8,128)(2,1)}, u32[]{:S(2)}, u32[]{:S(2)}) collective-permute-start(bf16[4,32,1280]{2,1,0:T(8,128)(2,1)} %collective-permute-done.28.refs_5_), channel_id=1, source_target_pairs={{0,1},{1,0},{2,3},{3,2},{4,5},{5,4},{6,7},{7,6},{8,9},{9,8},{10,11... | collective-permute-start | bytes 983048 | tf_op jit(solution)/shard_map/ppermute | solution.py:67
  178.7 15.3 %collective-permute-start.32 = (bf16[4,48,1280]{2,1,0:T(8,128)(2,1)}, bf16[4,48,1280]{2,1,0:T(8,128)(2,1)}, u32[]{:S(2)}, u32[]{:S(2)}) collective-permute-start(bf16[4,48,1280]{2,1,0:T(8,128)(2,1)} %collective-permute-done.26.refs_3_), channel_id=1, source_target_pairs={{0,1},{1,0},{2,3},{3,2},{4,5},{5,4},{6,7},{7,6},{8,9},{9,8},{10,11... | collective-permute-start | bytes 1474568 | tf_op jit(solution)/shard_map/ppermute | solution.py:67
  179.7 14.3 %collective-permute-start.33 = (bf16[4,48,1280]{2,1,0:T(8,128)(2,1)}, bf16[4,48,1280]{2,1,0:T(8,128)(2,1)}, u32[]{:S(2)}, u32[]{:S(2)}) collective-permute-start(bf16[4,48,1280]{2,1,0:T(8,128)(2,1)} %collective-permute-done.27.refs_4_), channel_id=1, source_target_pairs={{0,1},{1,0},{2,3},{3,2},{4,5},{5,4},{6,7},{7,6},{8,9},{9,8},{10,11... | collective-permute-start | bytes 1474568 | tf_op jit(solution)/shard_map/ppermute | solution.py:67
  204.9 142.9 %all-gather.11.cloned.1.call-start = ((), (), s32[]{:S(2)}) async-start(), calls=%async_computation.11 | async-start | bytes 5570560 | tf_op jit(solution)/shard_map/all_gather | solution.py:100
  213.8 19.0 %collective-permute-start.36 = (bf16[4,48,1280]{2,1,0:T(8,128)(2,1)S(1)}, bf16[4,48,1280]{2,1,0:T(8,128)(2,1)S(1)}, u32[]{:S(2)}, u32[]{:S(2)}) collective-permute-start(bf16[4,48,1280]{2,1,0:T(8,128)(2,1)S(1)} %get-tuple-element.233), channel_id=1, source_target_pairs={{0,8},{1,9},{2,10},{3,11},{4,12},{5,13},{6,14},{7,15},{8,0},{9,1},... | collective-permute-start | bytes 1474568 | tf_op jit(solution)/shard_map/ppermute | solution.py:67
  214.9 18.5 %collective-permute-start.37 = (bf16[4,48,1280]{2,1,0:T(8,128)(2,1)S(1)}, bf16[4,48,1280]{2,1,0:T(8,128)(2,1)S(1)}, u32[]{:S(2)}, u32[]{:S(2)}) collective-permute-start(bf16[4,48,1280]{2,1,0:T(8,128)(2,1)S(1)} %get-tuple-element.237), channel_id=1, source_target_pairs={{0,4},{1,5},{2,6},{3,7},{4,0},{5,1},{6,2},{7,3},{8,12},{9,13},{10,... | collective-permute-start | bytes 1474568 | tf_op jit(solution)/shard_map/ppermute | solution.py:67
  216.0 17.4 %collective-permute-start.38 = (bf16[4,32,1280]{2,1,0:T(8,128)(2,1)S(1)}, bf16[4,32,1280]{2,1,0:T(8,128)(2,1)S(1)}, u32[]{:S(2)}, u32[]{:S(2)}) collective-permute-start(bf16[4,32,1280]{2,1,0:T(8,128)(2,1)S(1)} %get-tuple-element.238), channel_id=1, source_target_pairs={{0,2},{1,3},{2,0},{3,1},{4,6},{5,7},{6,4},{7,5},{8,10},{9,11},{10,... | collective-permute-start | bytes 983048 | tf_op jit(solution)/shard_map/ppermute | solution.py:67
  235.5 28.2 %collective-permute-start.45 = (bf16[160,1280]{1,0:T(8,128)(2,1)S(1)}, bf16[160,1280]{1,0:T(8,128)(2,1)S(1)}, u32[]{:S(2)}, u32[]{:S(2)}) collective-permute-start(bf16[160,1280]{1,0:T(8,128)(2,1)S(1)} %get-tuple-element.317), channel_id=1, source_target_pairs={{0,16},{1,17},{2,18},{3,19},{4,20},{5,21},{6,22},{7,23},{8,24},{9,... | collective-permute-start | bytes 1228808 | tf_op jit(solution)/shard_map/ppermute | solution.py:67
  237.3 12.2 %collective-permute-start.39 = (bf16[2,48,1280]{2,1,0:T(8,128)(2,1)S(1)}, bf16[2,48,1280]{2,1,0:T(8,128)(2,1)S(1)}, u32[]{:S(2)}, u32[]{:S(2)}) collective-permute-start(bf16[2,48,1280]{2,1,0:T(8,128)(2,1)S(1)} %get-tuple-element.242), channel_id=1, source_target_pairs={{0,4},{1,5},{2,6},{3,7},{4,0},{5,1},{6,2},{7,3},{8,12},{9,13},{10,... | collective-permute-start | bytes 737288 | tf_op jit(solution)/shard_map/ppermute | solution.py:67
  239.2 16.3 %collective-permute-start.40 = (bf16[2,48,1280]{2,1,0:T(8,128)(2,1)S(1)}, bf16[2,48,1280]{2,1,0:T(8,128)(2,1)S(1)}, u32[]{:S(2)}, u32[]{:S(2)}) collective-permute-start(bf16[2,48,1280]{2,1,0:T(8,128)(2,1)S(1)} %get-tuple-element.246), channel_id=1, source_target_pairs={{0,2},{1,3},{2,0},{3,1},{4,6},{5,7},{6,4},{7,5},{8,10},{9,11},{10,... | collective-permute-start | bytes 737288 | tf_op jit(solution)/shard_map/ppermute | solution.py:67
  239.9 15.5 %collective-permute-start.41 = (bf16[2,32,1280]{2,1,0:T(8,128)(2,1)S(1)}, bf16[2,32,1280]{2,1,0:T(8,128)(2,1)S(1)}, u32[]{:S(2)}, u32[]{:S(2)}) collective-permute-start(bf16[2,32,1280]{2,1,0:T(8,128)(2,1)S(1)} %get-tuple-element.247), channel_id=1, source_target_pairs={{0,8},{1,9},{2,10},{3,11},{4,12},{5,13},{6,14},{7,15},{8,0},{9,1},... | collective-permute-start | bytes 491528 | tf_op jit(solution)/shard_map/ppermute | solution.py:67
  256.5 7.3 %collective-permute-start.42 = (bf16[1,48,1280]{2,1,0:T(8,128)(2,1)S(1)}, bf16[1,48,1280]{2,1,0:T(8,128)(2,1)S(1)}, u32[]{:S(2)}, u32[]{:S(2)}) collective-permute-start(bf16[1,48,1280]{2,1,0:T(8,128)(2,1)S(1)} %get-tuple-element.251), channel_id=1, source_target_pairs={{0,2},{1,3},{2,0},{3,1},{4,6},{5,7},{6,4},{7,5},{8,10},{9,11},{10,... | collective-permute-start | bytes 368648 | tf_op jit(solution)/shard_map/ppermute | solution.py:67
  256.5 7.2 %collective-permute-start.43 = (bf16[1,48,1280]{2,1,0:T(8,128)(2,1)S(1)}, bf16[1,48,1280]{2,1,0:T(8,128)(2,1)S(1)}, u32[]{:S(2)}, u32[]{:S(2)}) collective-permute-start(bf16[1,48,1280]{2,1,0:T(8,128)(2,1)S(1)} %get-tuple-element.252), channel_id=1, source_target_pairs={{0,8},{1,9},{2,10},{3,11},{4,12},{5,13},{6,14},{7,15},{8,0},{9,1},... | collective-permute-start | bytes 368648 | tf_op jit(solution)/shard_map/ppermute | solution.py:67
  283.1 27.3 %all-to-all-start.4 = ((bf16[32,8,1600]{2,1,0:T(8,128)(2,1)}), bf16[32,8,1600]{2,1,0:T(8,128)(2,1)S(1)}, u32[]{:S(2)}, u32[]{:S(2)}) async-start(bf16[32,8,1600]{2,1,0:T(8,128)(2,1)} %fc1_grad.1), calls=%async_computation.5 | async-start | bytes 1703936 | tf_op jit(solution)/shard_map/all_to_all | solution.py:106
  321.1 16.8 %collective-permute-start.47 = (bf16[4,48,1280]{2,1,0:T(8,128)(2,1)S(1)}, bf16[4,48,1280]{2,1,0:T(8,128)(2,1)S(1)}, u32[]{:S(2)}, u32[]{:S(2)}) collective-permute-start(bf16[4,48,1280]{2,1,0:T(8,128)(2,1)S(1)} %get-tuple-element.278), channel_id=1, source_target_pairs={{0,8},{1,9},{2,10},{3,11},{4,12},{5,13},{6,14},{7,15},{8,0},{9,1},... | collective-permute-start | bytes 1474568 | tf_op jit(solution)/shard_map/ppermute | solution.py:67
  323.5 14.5 %collective-permute-start.48 = (bf16[4,48,1280]{2,1,0:T(8,128)(2,1)S(1)}, bf16[4,48,1280]{2,1,0:T(8,128)(2,1)S(1)}, u32[]{:S(2)}, u32[]{:S(2)}) collective-permute-start(bf16[4,48,1280]{2,1,0:T(8,128)(2,1)S(1)} %get-tuple-element.285), channel_id=1, source_target_pairs={{0,4},{1,5},{2,6},{3,7},{4,0},{5,1},{6,2},{7,3},{8,12},{9,13},{10,... | collective-permute-start | bytes 1474568 | tf_op jit(solution)/shard_map/ppermute | solution.py:67
  325.0 13.0 %collective-permute-start.49 = (bf16[4,32,1280]{2,1,0:T(8,128)(2,1)S(1)}, bf16[4,32,1280]{2,1,0:T(8,128)(2,1)S(1)}, u32[]{:S(2)}, u32[]{:S(2)}) collective-permute-start(bf16[4,32,1280]{2,1,0:T(8,128)(2,1)S(1)} %get-tuple-element.286), channel_id=1, source_target_pairs={{0,2},{1,3},{2,0},{3,1},{4,6},{5,7},{6,4},{7,5},{8,10},{9,11},{10,... | collective-permute-start | bytes 983048 | tf_op jit(solution)/shard_map/ppermute | solution.py:67
  342.2 29.1 %all-to-all-start.5 = ((bf16[32,40,256]{2,1,0:T(8,128)(2,1)}), bf16[32,40,256]{2,1,0:T(8,128)(2,1)S(1)}, u32[]{:S(2)}, u32[]{:S(2)}) async-start(bf16[32,40,256]{2,1,0:T(8,128)(2,1)} %head_grad.1), calls=%async_computation.6 | async-start | bytes 1310720 | tf_op jit(solution)/shard_map/all_to_all | solution.py:106
  345.9 14.2 %collective-permute-start.50 = (bf16[2,48,1280]{2,1,0:T(8,128)(2,1)}, bf16[2,48,1280]{2,1,0:T(8,128)(2,1)}, u32[]{:S(2)}, u32[]{:S(2)}) collective-permute-start(bf16[2,48,1280]{2,1,0:T(8,128)(2,1)} %get-tuple-element.290), channel_id=1, source_target_pairs={{0,4},{1,5},{2,6},{3,7},{4,0},{5,1},{6,2},{7,3},{8,12},{9,13},{10,... | collective-permute-start | bytes 737288 | tf_op jit(solution)/shard_map/ppermute | solution.py:67
  347.8 13.5 %collective-permute-start.51 = (bf16[2,48,1280]{2,1,0:T(8,128)(2,1)}, bf16[2,48,1280]{2,1,0:T(8,128)(2,1)S(1)}, u32[]{:S(2)}, u32[]{:S(2)}) collective-permute-start(bf16[2,48,1280]{2,1,0:T(8,128)(2,1)} %get-tuple-element.295), channel_id=1, source_target_pairs={{0,2},{1,3},{2,0},{3,1},{4,6},{5,7},{6,4},{7,5},{8,10},{9,11},{10,... | collective-permute-start | bytes 737288 | tf_op jit(solution)/shard_map/ppermute | solution.py:67
  349.2 12.1 %collective-permute-start.52 = (bf16[2,32,1280]{2,1,0:T(8,128)(2,1)}, bf16[2,32,1280]{2,1,0:T(8,128)(2,1)S(1)}, u32[]{:S(2)}, u32[]{:S(2)}) collective-permute-start(bf16[2,32,1280]{2,1,0:T(8,128)(2,1)} %get-tuple-element.296), channel_id=1, source_target_pairs={{0,8},{1,9},{2,10},{3,11},{4,12},{5,13},{6,14},{7,15},{8,0},{9,1},... | collective-permute-start | bytes 491528 | tf_op jit(solution)/shard_map/ppermute | solution.py:67
  355.0 15.6 %collective-permute-start.59 = (bf16[40,1280]{1,0:T(8,128)(2,1)S(1)}, bf16[40,1280]{1,0:T(8,128)(2,1)S(1)}, u32[]{:S(2)}, u32[]{:S(2)}) collective-permute-start(bf16[40,1280]{1,0:T(8,128)(2,1)S(1)} %get-tuple-element.332), channel_id=1, source_target_pairs={{0,1},{1,3},{2,5},{3,7},{4,9},{5,11},{6,13},{7,15},{8,17},{9,19},{... | collective-permute-start | bytes 307208 | tf_op jit(solution)/shard_map/ppermute | solution.py:67
  355.0 15.5 %collective-permute-start.58 = (bf16[40,1280]{1,0:T(8,128)(2,1)S(1)}, bf16[40,1280]{1,0:T(8,128)(2,1)S(1)}, u32[]{:S(2)}, u32[]{:S(2)}) collective-permute-start(bf16[40,1280]{1,0:T(8,128)(2,1)S(1)} %get-tuple-element.331), channel_id=1, source_target_pairs={{0,0},{1,2},{2,4},{3,6},{4,8},{5,10},{6,12},{7,14},{8,16},{9,18},{... | collective-permute-start | bytes 307208 | tf_op jit(solution)/shard_map/ppermute | solution.py:67
  365.1 8.2 %collective-permute-start.53 = (bf16[1,48,1280]{2,1,0:T(8,128)(2,1)}, bf16[1,48,1280]{2,1,0:T(8,128)(2,1)}, u32[]{:S(2)}, u32[]{:S(2)}) collective-permute-start(bf16[1,48,1280]{2,1,0:T(8,128)(2,1)} %get-tuple-element.302), channel_id=1, source_target_pairs={{0,2},{1,3},{2,0},{3,1},{4,6},{5,7},{6,4},{7,5},{8,10},{9,11},{10,... | collective-permute-start | bytes 368648 | tf_op jit(solution)/shard_map/ppermute | solution.py:67
  367.2 6.1 %collective-permute-start.54 = (bf16[1,48,1280]{2,1,0:T(8,128)(2,1)}, bf16[1,48,1280]{2,1,0:T(8,128)(2,1)}, u32[]{:S(2)}, u32[]{:S(2)}) collective-permute-start(bf16[1,48,1280]{2,1,0:T(8,128)(2,1)} %get-tuple-element.303), channel_id=1, source_target_pairs={{0,8},{1,9},{2,10},{3,11},{4,12},{5,13},{6,14},{7,15},{8,0},{9,1},... | collective-permute-start | bytes 368648 | tf_op jit(solution)/shard_map/ppermute | solution.py:67
  378.6 17.8 %collective-permute-start.56 = (bf16[64,1280]{1,0:T(8,128)(2,1)S(1)}, bf16[64,1280]{1,0:T(8,128)(2,1)}, u32[]{:S(2)}, u32[]{:S(2)}) collective-permute-start(bf16[64,1280]{1,0:T(8,128)(2,1)S(1)} %dynamic-slice_bitcast_fusion.3), channel_id=1, source_target_pairs={{0,16},{1,17},{2,18},{3,19},{4,20},{5,21},{6,22},{7,23},{8,24},{9,... | collective-permute-start | bytes 491528 | tf_op jit(solution)/shard_map/ppermute | solution.py:67
  382.2 16.0 %collective-permute-start.57 = (bf16[64,1280]{1,0:T(8,128)(2,1)}, bf16[64,1280]{1,0:T(8,128)(2,1)}, u32[]{:S(2)}, u32[]{:S(2)}) collective-permute-start(bf16[64,1280]{1,0:T(8,128)(2,1)} %dynamic-slice_bitcast_fusion.2), channel_id=1, source_target_pairs={{0,16},{1,17},{2,18},{3,19},{4,20},{5,21},{6,22},{7,23},{8,24},{9,... | collective-permute-start | bytes 491528 | tf_op jit(solution)/shard_map/ppermute | solution.py:67
  382.3 13.5 %all-to-all-start.6 = ((f32[32,1,128]{2,1,0:T(1,128)}), f32[32,1,128]{2,1,0:T(1,128)S(1)}, u32[]{:S(2)}, u32[]{:S(2)}) async-start(f32[32,1,128]{2,1,0:T(1,128)} %get-tuple-element.308), calls=%async_computation.7 | async-start | bytes 32768 | tf_op jit(solution)/shard_map/all_to_all | solution.py:106
  (60 other events, 630.7 us)
Sparse Core Ops, SparseCore 0:
  73.7 46.1 all-gather.6
  121.5 48.6 all-gather.8
  205.0 79.0 reduce-scatter.1
  285.5 47.0 all-gather.10
where the time goes:
time: 409 us; the launch traced here: 407 us
  Pallas kernels  127 us (31%)
  waiting for transfers between devices  114 us (28%)
  starting transfers between devices  87.7 us (21%)
  local copies, waits for them, and re-layouts  35.8 us (9%)
  blocking collectives  14.8 us (4%)
  between operations  14.6 us (4%)
  other arithmetic  12.3 us (3%)
    ppermute x60, waiting for transfers between devices, send(): return lax.ppermute(value, 'dev', pairs)  93.4 us
    ppermute x60, starting transfers between devices, send(): return lax.ppermute(value, 'dev', pairs)  65.2 us
    unnamed x109, local copies, waits for them, and re-layouts  24.1 us
    pallas_call x2, Pallas kernels, feed(): pl.pallas_call(feed_kernel, grid_spec=pltpu.PrefetchScalarGridSpec(num_sc...  21.6 us
    all_to_all x5, starting transfers between devices, exchange_block(): lax.all_to_all(value, 'dev', 0, 0, tiled=True, axis_index_groups=self.whole)  18.3 us
    all_to_all x5, waiting for transfers between devices, exchange_block(): lax.all_to_all(value, 'dev', 0, 0, tiled=True, axis_index_groups=self.whole)  16.5 us
    pallas_call x1, Pallas kernels, attend_back(): pl.pallas_call(functools.partial(attend_back_kernel, hd, scale, span), gr...  15.8 us
    all_to_all x1, blocking collectives, exchange_half(): lax.all_to_all(value, 'dev', 0, 0, tiled=True, axis_index_groups=self.hal...  14.8 us
  transfers between devices with their start and end apart: 70, of which 32 were waited for; matrix products, arithmetic and copies ran while one was open for 5% of the time, Pallas kernels for 27%

commit v1 on v0

--- a/solution.py
+++ b/solution.py
@@ -181,7 +181,7 @@
     width = kept[0].shape[-1]
     bounds = part_bounds(kept[0].shape[1]) if stage == 0 else [(0, k.shape[1]) for k in kept]
     count = kept[0].shape[0] // 2
-    cols = 256 if stage == 0 else 640
+    cols = (256, 640, width)[stage]
     spec = lambda n, t: pl.BlockSpec((n, t, cols), lambda i, p: (0, 0, i))
     outs = [(count, end - start) for start, end in bounds]
     res = pl.pallas_call(
@@ -192,7 +192,8 @@
             in_specs=[spec(*v.shape[:2]) for v in (*kept, *got)],
             out_specs=[spec(*o) for o in outs] * 2,
         ),
-        out_shape=[jax.ShapeDtypeStruct(o + (width,), kind) for kind in (low, exact) for o in outs],
+        out_shape=[jax.ShapeDtypeStruct(o + (width,), low) for o in outs]
+        + [(pltpu.HBM if stage == 2 else jax.ShapeDtypeStruct)(o + (width,), exact) for o in outs],
         compiler_params=params(10),
         cost_estimate=small_cost,
         name="split_terms",
@@ -233,7 +234,7 @@
         out_shape=[out, out],
         compiler_params=params(6),
         name="pack",
-    )(place, x, vectors, c)
+    )(place, far_off(x), vectors, c)
 
 
 def arrange_kernel(rows, place_ref, first_ref, second_ref, x_ref, small_ref, *part_refs):
@@ -319,7 +320,7 @@
         out_shape=[jax.ShapeDtypeStruct(shape, low) for shape in ((block, chunk, 3 * hd), (block, 8, chunk * ff // 8))],
         compiler_params=params(8),
         name="deal",
-    )(q, k, v, w)
+    )(*map(far_off, (q, k, v, w)))
 
 
 def merge_kernel(*refs):
@@ -753,33 +754,26 @@
         compiler_params=params(12),
         cost_estimate=small_cost,
         name="second_back",
-    )(*kept, *got, x2, g, table, far_off(w))
-
-
-def first_back_kernel(chunk, *refs):
+    )(*map(far_off, (*kept, *got)), x2, g, table, far_off(w))
+
+
+def first_back_kernel(*refs):
     da1 = last_sum(refs[:6])
-    x_ref, dx2_ref, table_ref, dx_ref, vec_ref = refs[6:]
+    x_ref, dx2_ref, table_ref, dx_ref = refs[6:]
     unit, inverse = normalized(x_ref[...].astype(exact))
-    dx = dx2_ref[...] + norm_back(unit, inverse, table_ref[0:1], da1)
-    dx_ref[...] = dx.astype(low)
-    total = lambda v: jnp.sum(v, axis=0, keepdims=True)
-    rows = [total(da1 * unit), total(da1)]
-    fill = jnp.zeros((1, lanes // 2 - chunk), exact)
-    for device in range(vec_ref.shape[0]):
-        part = slice(device * chunk, (device + 1) * chunk)
-        vec_ref[device] = jnp.concatenate([rows[0][:, part], fill, rows[1][:, part], fill], axis=1)
-
-
-def first_back(kept, got, x, dx2, table, chunk, block):
-    return pl.pallas_call(
-        functools.partial(first_back_kernel, chunk),
-        out_shape=[jax.ShapeDtypeStruct(x.shape, low), jax.ShapeDtypeStruct((block, 1, lanes), exact)],
+    dx_ref[...] = (dx2_ref[...] + norm_back(unit, inverse, table_ref[0:1], da1)).astype(low)
+
+
+def first_back(kept, got, x, dx2, table):
+    return pl.pallas_call(
+        first_back_kernel,
+        out_shape=jax.ShapeDtypeStruct(x.shape, low),
         compiler_params=params(8),
         name="first_back",
-    )(*kept, *got, x, dx2, table)
-
-
-def head_grad_kernel(hd, chunk, place_ref, a_ref, d_ref, sum2_ref, sum_in_ref, sum_c_ref, sum_c2_ref, out_ref, total_ref, line_ref):
+    )(*map(far_off, (*kept, *got)), x, dx2, table)
+
+
+def head_grad_kernel(hd, chunk, place_ref, a_ref, d_ref, w_ref, table_ref, sum2_ref, sum_in_ref, sum_c_ref, sum_c2_ref, out_ref, total_ref, line_ref):
     accumulate(total_ref, dot(d_ref[...], a_ref[...], 0, 0))
 
     @at_end
@@ -802,17 +796,24 @@
                         at, start = (slot * heads + h) * chunk, slot * ff_rows + line * chunk
                         line_ref[8 + line : 9 + line, at : at + chunk] = c[:, start : start + chunk]
 
+        line_ref[12:14] = table_ref[0:2]
         small = line_ref[...].T
+        gain, shift = small[:, 12:13], small[:, 13:14]
+        sums = jnp.concatenate([sum_in_ref[0:1, i * lanes : i * lanes + hd] for i in range(3)], axis=1)
+        w = w_ref[...].astype(exact)
+        d_shift = jnp.sum(w * sums, axis=1, keepdims=True)
+        d_gain = (jnp.sum(w * total, axis=1, keepdims=True) - shift * d_shift) / gain
+        small = jnp.concatenate([small[:, :6], d_gain, d_shift, small[:, 8:12], jnp.zeros_like(small[:, 12:])], axis=1)
         for device in range(block):
             part = slice(device * chunk, (device + 1) * chunk)
             out_ref[device] = jnp.concatenate([total[part], small[part]], axis=1).astype(low)
 
 
-def head_grad(place, a, d, sum2, sum_in, sum_c, sum_c2, hd, chunk, block):
+def head_grad(place, a, d, w, table, sum2, sum_in, sum_c, sum_c2, hd, chunk, block):
     tokens, width = a.shape
     rows = 512
     out = jax.ShapeDtypeStruct((block, chunk, up_to_lanes(3 * hd)), low)
-    small = (sum2, sum_in, sum_c, sum_c2)
+    small = (w, table, sum2, sum_in, sum_c, sum_c2)
     return pl.pallas_call(
         functools.partial(head_grad_kernel, hd, chunk),
         grid_spec=pltpu.PrefetchScalarGridSpec(
@@ -823,7 +824,7 @@
             scratch_shapes=[pltpu.VMEM((3 * lanes, width), exact), pltpu.VMEM((out.shape[2] - 3 * hd, width), exact)],
         ),
         out_shape=out,
-        compiler_params=params(16),
+        compiler_params=params(20),
         cost_estimate=small_cost,
         name="head_grad",
     )(place, far_off(a), d, *small)
@@ -951,7 +952,9 @@
         head = lax.broadcasted_iota(jnp.int32, dk_sum.shape, 1) < hd
         dk = jnp.where(head, dk_sum[...] * scale, 0.0)
         dv = dv_sum[...].astype(out_ref.dtype)
-        out_ref[:, lanes : 2 * lanes] = dk.astype(out_ref.dtype)
+        dk = dk.astype(out_ref.dtype)
+        out_ref[:, lanes : 2 * lanes] = dk
+        sum_ref[0:1, lanes : 2 * lanes] = jnp.sum(dk.astype(exact), axis=0, keepdims=True)
         out_ref[:, 2 * lanes :] = dv
         sum_ref[0:1, 2 * lanes :] = jnp.sum(dv.astype(exact), axis=0, keepdims=True)
 
@@ -1112,43 +1115,42 @@
         dkv = dkv[span : span + tokens] + halo.reshape(tokens, 2 * lanes)
         dqkv = jnp.concatenate([dqkv[span : span + tokens, :lanes], dkv], axis=1).astype(low)
         sum_in = jnp.broadcast_to(jnp.sum(dqkv.astype(exact), axis=0, keepdims=True), (8, 3 * lanes))
-    dqkv, sum_in, y, d_w1 = together(dqkv, sum_in, y, d_w1)
+    dqkv, sum_in, y = together(dqkv, sum_in, y)
     split = dqkv.reshape(8, 2, own, 3 * lanes)
-    away = terms(place, True, split, w_pad, 1, low)
-    marks, made = [], []
+    away, kept = (terms(place, other, split, w_pad, 1, low) for other in (True, False))
+    away, d_w1 = together(away, d_w1)
+    marks, made, moved = [], [], []
 
     def projections(marks):
-        made.append(head_grad(place, a1, tie(dqkv, marks[0]), sum2, sum_in, sum_c, sum_c2, hd, chunk, at.block))
+        made.append(head_grad(place, a1, tie(dqkv, marks[0]), w_in, table, sum2, sum_in, sum_c, sum_c2, hd, chunk, at.block))
         return made
 
     def output_weight(marks):
+        out = (x2 + (tie(y, marks[0]).astype(exact) + table[7])).astype(low)
+        moved.extend(at.exchanged(out.reshape(2, rows, width)))
         late, o_late = together(ga, o_head, marks[1])[:2]
         made.append(output_grad(o_late, late.reshape(at.half, own, width)))
-        return made[1:]
-
-    kept, got = at.reduce_half(away, terms(place, False, split, w_pad, 1, low), marks, {1: projections, 2: output_weight})
+        return made[1:] + moved
+
+    kept, got = at.reduce_half(away, kept, marks, {1: projections, 2: output_weight})
     d_in = at.exchange_block(tie(made[0], marks[1]))
     kept_first, d_in = together(kept[0], d_in)
     kept = (kept_first, *kept[1:])
 
-    dx, vec = first_back(kept, got, x_own, dx2, table, chunk, at.block)
-    y, d_w1, *back_w2 = together(y, d_w1, *back_w2, dx)[:4]
-    out = (x2 + (y.astype(exact) + table[7])).astype(low)
+    dx = first_back(kept, got, x_own, dx2, table)
+    d_w1, *back_w2 = together(d_w1, *back_w2, dx)[:3]
 
     input_grad = at.exchanged(dx.reshape(2, rows, width))
-    layer_out = at.exchanged(out.reshape(2, rows, width))
+    layer_out = moved
     layer_out, input_grad = (jnp.stack(at.ordered(*v)).astype(exact) for v in (layer_out, input_grad))
     back_wo = at.send_rows_back(made[1])
     grad_w2 = at.from_block(back_w2[0].astype(exact) + back_w2[1].astype(exact))
     grad_w1 = at.from_block(collect_hidden(d_w1, ff))
     grad_wo = at.from_block(back_wo[0].astype(exact) + back_wo[1].astype(exact))
-    vec = jnp.sum(at.exchange_block(vec), axis=(0, 1))
-    grad_g1 = at.from_block(vec[:chunk])
-    grad_b1 = at.from_block(vec[lanes // 2 : lanes // 2 + chunk])
     *grads, vec = collect(d_in, hd)
     grad_wq, grad_wk, grad_wv = (at.from_block(v) for v in grads)
-    pieces = [at.from_block(vec[i]) for i in range(6)]
-    grad_g2, grad_b2, grad_bo, grad_bf2, grad_bq, grad_bv = pieces
+    pieces = [at.from_block(vec[i]) for i in range(8)]
+    grad_g2, grad_b2, grad_bo, grad_bf2, grad_bq, grad_bv, grad_g1, grad_b1 = pieces
     grad_c1 = at.from_block(vec[8 : 8 + ff_rows // chunk].reshape(ff_rows))
     return (
         layer_out,

time: 409 us -> 397 us (0.971)
  local copies, waits for them, and re-layouts: 35.8 us -> 28.7 us
  starting transfers between devices: 87.7 us -> 83.3 us
    all_to_all x5 -> x4, waiting for transfers between devices: 16.5 us -> 8.46 us  [exchange_block(): lax.all_to_all(value, 'dev', 0, 0, tiled=True, axis_index_groups=self.whole)]
    ppermute x60, waiting for transfers between devices: 93.4 us -> 99.3 us  [send(): return lax.ppermute(value, 'dev', pairs)]
    unnamed x109 -> x101, local copies, waits for them, and re-layouts: 24.1 us -> 18.3 us
    all_to_all x5 -> x4, starting transfers between devices: 18.3 us -> 14.6 us  [exchange_block(): lax.all_to_all(value, 'dev', 0, 0, tiled=True, axis_index_groups=self.whole)]
  transfers between devices with their start and end apart: 70 -> 69, of which waited for: 32 -> 31; matrix products, arithmetic and copies ran while one was open for 5% -> 5% of each run, Pallas kernels for 27% -> 29%
where the time goes in v1:
time: 397 us; the launch traced here: 395 us
  Pallas kernels  130 us (33%)
  waiting for transfers between devices  112 us (28%)
  starting transfers between devices  83.3 us (21%)
  local copies, waits for them, and re-layouts  28.7 us (7%)
  between operations  14.6 us (4%)
  blocking collectives  14 us (4%)
  other arithmetic  12.8 us (3%)
    ppermute x60, waiting for transfers between devices, send(): return lax.ppermute(value, 'dev', pairs)  99.3 us
    ppermute x60, starting transfers between devices, send(): return lax.ppermute(value, 'dev', pairs)  64.8 us
    pallas_call x2, Pallas kernels, feed(): pl.pallas_call(feed_kernel, grid_spec=pltpu.PrefetchScalarGridSpec(num_sc...  21.6 us
    unnamed x101, local copies, waits for them, and re-layouts  18.3 us
    pallas_call x1, Pallas kernels, attend_back(): pl.pallas_call(functools.partial(attend_back_kernel, hd, scale, span), gr...  15.8 us
    all_to_all x4, starting transfers between devices, exchange_block(): lax.all_to_all(value, 'dev', 0, 0, tiled=True, axis_index_groups=self.whole)  14.6 us
    all_to_all x1, blocking collectives, exchange_half(): lax.all_to_all(value, 'dev', 0, 0, tiled=True, axis_index_groups=self.hal...  14 us
    pallas_call x1, Pallas kernels, attend(): pl.pallas_call(functools.partial(attend_kernel, hd, coef), grid=(steps,),...  12.3 us
  transfers between devices with their start and end apart: 69, of which 31 were waited for; matrix products, arithmetic and copies ran while one was open for 5% of the time, Pallas kernels for 29%

profile of v1, /device:TPU:0, one launch (start us, length us, event | category | flops | bytes accessed | tf_op | source)
XLA Modules:
  0.0 395.0 jit_solution(881788552681620643)
XLA Ops:
  10.5 4.1 %collective-permute-start = (bf16[72,1280]{1,0:T(8,128)(2,1)S(1)}, bf16[72,1280]{1,0:T(8,128)(2,1)S(1)}, u32[]{:S(2)}, u32[]{:S(2)}) collective-permute-start(bf16[72,1280]{1,0:T(8,128)(2,1)S(1)} %get-tuple-element.167), channel_id=1, source_target_pairs={{0,16},{1,17},{2,18},{3,19},{4,20},{5,21},{6,22},{7,23},{8,24},{9,... | collective-permute-start | bytes 552968 | tf_op jit(solution)/shard_map/ppermute | solution.py:67
  15.5 3.6 deal.1
  20.1 3.1 collective-permute-done.second_ref
  26.7 2.9 collective-permute-start.2
  31.1 2.0 collective-permute-done.2.refs_3_
  33.1 6.1 %collective-permute-done.3 = bf16[104,1280]{1,0:T(8,128)(2,1)S(1)} collective-permute-done((bf16[104,1280]{1,0:T(8,128)(2,1)S(1)}, bf16[104,1280]{1,0:T(8,128)(2,1)S(1)}, u32[]{:S(2)}, u32[]{:S(2)}) %collective-permute-start.3) | collective-permute-done | bytes 266272 | tf_op jit(solution)/shard_map/ppermute | solution.py:67
  43.4 1.7 collective-permute-start.7
  45.2 8.5 %collective-permute-done.7 = bf16[80,1280]{1,0:T(8,128)(2,1)S(1)} collective-permute-done((bf16[80,1280]{1,0:T(8,128)(2,1)S(1)}, bf16[80,1280]{1,0:T(8,128)(2,1)S(1)}, u32[]{:S(2)}, u32[]{:S(2)}) %collective-permute-start.7) | collective-permute-done | bytes 204832 | tf_op jit(solution)/shard_map/ppermute | solution.py:67
  53.6 2.2 collective-permute-done.9.refs_5_
  59.5 1.8 collective-permute-start.11
  61.9 9.5 %collective-permute-done.11 = bf16[80,1280]{1,0:T(8,128)(2,1)} collective-permute-done((bf16[80,1280]{1,0:T(8,128)(2,1)}, bf16[80,1280]{1,0:T(8,128)(2,1)}, u32[]{:S(2)}, u32[]{:S(2)}) %collective-permute-start.11) | collective-permute-done | bytes 204832 | tf_op jit(solution)/shard_map/ppermute | solution.py:67
  75.0 3.6 all-to-all-start
  84.1 6.9 %norm.2 = (bf16[8,2,128,1280]{3,2,1,0:T(8,128)(2,1)}, f32[8,1280]{1,0:T(8,128)S(1)}) custom-call(s32[7]{0:T(128)S(1)} %stack.76.place_ref, bf16[4,48,1280]{2,1,0:T(8,128)(2,1)} %get-tuple-element.192.refs_0_, bf16[4,48,1280]{2,1,0:T(8,128)(2,1)S(1)} %copy-done.27, bf16[4,64,1280]{2,1,0:T(8,128)(2,1)S(1)} %get-tuple-element.194.refs_2_, ...), custom_call_target="tpu_custom_call" | custom-call | flops 1024 | bytes 1024 | tf_op jit(solution)/shard_map/norm/pallas_call | solution.py:421
  91.1 3.9 norm.3
  95.0 4.0 %all-to-all-done = bf16[32,40,240]{2,1,0:T(8,128)(2,1)S(1)} async-done(((bf16[32,40,240]{2,1,0:T(8,128)(2,1)}), bf16[32,40,240]{2,1,0:T(8,128)(2,1)S(1)}, u32[]{:S(2)}, u32[]{:S(2)}) %all-to-all-start) | async-done | bytes 614432 | tf_op jit(solution)/shard_map/all_to_all | solution.py:106
  99.0 2.6 all-to-all-start.1
  101.9 7.4 %project.1 = (bf16[2048,384]{1,0:T(8,128)(2,1)S(1)}, bf16[1280,384]{1,0:T(8,128)(2,1)}) custom-call(s32[7]{0:T(128)S(1)} %stack.76.place_ref, s32[3]{0:T(128)S(1)} %subtract_bitcast_fusion.ends_ref, bf16[2048,1280]{1,0:T(8,128)(2,1)} %bitcast.98, bf16[1280,240]{1,0:T(8,128)(2,1)S(1)} %bitcast.89, f32[8,1280]{1,0:T(8,128)S(1)} %get-tuple-element.204.table_ref.refs_8_), custom_call_target="tpu_custom_call" | custom-call | flops 1024 | bytes 1024 | tf_op jit(solution)/shard_map/project/pallas_call | solution.py:477
  109.2 12.3 %attend.1 = (bf16[16,80,128]{2,1,0:T(8,128)(2,1)}, bf16[8,2048,256]{2,1,0:T(8,128)(2,1)}, f32[8,1,256]{2,1,0:T(1,128)S(1)}) custom-call(bf16[2048,384]{1,0:T(8,128)(2,1)S(1)} %get-tuple-element.205.q_ref.k_ref.v_ref, bf16[2048,384]{1,0:T(8,128)(2,1)S(1)} %get-tuple-element.205.q_ref.k_ref.v_ref, bf16[2048,384]{1,0:T(8,128)(2,1)S(1)} %get-tuple-element.205.q_ref.k_ref.v_ref), custom_call_target="tpu_custom_call" | custom-call | flops 1024 | bytes 1024 | tf_op jit(solution)/shard_map/attend/pallas_call | solution.py:897
  121.6 2.5 all-to-all-done.1.in_ref
  124.0 3.5 all-to-all-start.2
  127.8 4.1 %copy.39 = bf16[16,2,40,1280]{3,2,0,1:T(8,128)(2,1)} copy(bf16[16,2,40,1280]{3,2,1,0:T(8,128)(2,1)} %bitcast.104) | data formatting | bytes 6553600 | tf_op jit(solution)/shard_map/reshape | solution.py:1044
  131.9 4.1 %all-to-all-done.2.o_ref = bf16[16,80,128]{2,1,0:T(8,128)(2,1)S(1)} async-done(((bf16[16,80,128]{2,1,0:T(8,128)(2,1)}), bf16[16,80,128]{2,1,0:T(8,128)(2,1)S(1)}, u32[]{:S(2)}, u32[]{:S(2)}) %all-to-all-start.2) | async-done | bytes 327712 | tf_op jit(solution)/shard_map/all_to_all | solution.py:103
  136.0 2.9 join.1
  143.7 5.3 %collective-permute-done.22.refs_5_ = bf16[1,32,1280]{2,1,0:T(8,128)(2,1)S(1)} collective-permute-done((bf16[1,32,1280]{2,1,0:T(8,128)(2,1)S(1)}, bf16[1,32,1280]{2,1,0:T(8,128)(2,1)S(1)}, u32[]{:S(2)}, u32[]{:S(2)}) %collective-permute-start.22) | collective-permute-done | bytes 81952 | tf_op jit(solution)/shard_map/ppermute | solution.py:67
  150.0 2.6 collective-permute-start.24
  153.8 8.5 %collective-permute-done.25.refs_5_ = bf16[2,32,1280]{2,1,0:T(8,128)(2,1)S(1)} collective-permute-done((bf16[2,32,1280]{2,1,0:T(8,128)(2,1)S(1)}, bf16[2,32,1280]{2,1,0:T(8,128)(2,1)S(1)}, u32[]{:S(2)}, u32[]{:S(2)}) %collective-permute-start.25) | collective-permute-done | bytes 163872 | tf_op jit(solution)/shard_map/ppermute | solution.py:67
  165.1 1.9 collective-permute-start.26
  171.6 5.3 %collective-permute-done.28.refs_5_ = bf16[4,32,1280]{2,1,0:T(8,128)(2,1)} collective-permute-done((bf16[4,32,1280]{2,1,0:T(8,128)(2,1)S(1)}, bf16[4,32,1280]{2,1,0:T(8,128)(2,1)}, u32[]{:S(2)}, u32[]{:S(2)}) %collective-permute-start.28) | collective-permute-done | bytes 327712 | tf_op jit(solution)/shard_map/ppermute | solution.py:67
  183.2 10.8 %feed.2 = (bf16[8,2,128,320]{3,2,1,0:T(8,128)(2,1)}, bf16[8,2,128,320]{3,2,1,0:T(8,128)(2,1)}, bf16[8,2,128,1280]{3,2,1,0:T(8,128)(2,1)}, bf16[8,128,1280]{2,1,0:T(8,128)(2,1)}, f32[1,320]{1,0:T(1,128)S(1)}) custom-call(s32[7]{0:T(128)S(1)} %stack.76.place_ref, bf16[4,48,1280]{2,1,0:T(8,128)(2,1)} %get-tuple-element.218.refs_0_, ...), custom_call_target="tpu_custom_call" | custom-call | flops 1024 | bytes 1024 | tf_op jit(solution)/shard_map/feed/pallas_call | solution.py:671
  194.1 10.8 %feed.3 = (bf16[8,2,128,320]{3,2,1,0:T(8,128)(2,1)}, bf16[8,2,128,320]{3,2,1,0:T(8,128)(2,1)}, bf16[8,2,128,1280]{3,2,1,0:T(8,128)(2,1)}, bf16[8,128,1280]{2,1,0:T(8,128)(2,1)}, f32[1,320]{1,0:T(1,128)S(1)}) custom-call(s32[7]{0:T(128)S(1)} %stack.76.place_ref, ...), custom_call_target="tpu_custom_call", output_to_operand_aliasing={{0}: (11, {}), {1}: (12, {}), {2}: (13, {})} | custom-call | flops 1024 | bytes 1024 | tf_op jit(solution)/shard_map/feed/pallas_call | solution.py:671
  205.5 4.7 %collective-permute-done.35.refs_1_ = bf16[8,128,1280]{2,1,0:T(8,128)(2,1)S(1)} collective-permute-done((bf16[8,128,1280]{2,1,0:T(8,128)(2,1)}, bf16[8,128,1280]{2,1,0:T(8,128)(2,1)S(1)}, u32[]{:S(2)}, u32[]{:S(2)}) %collective-permute-start.35) | collective-permute-done | bytes 2621472 | tf_op jit(solution)/shard_map/ppermute | solution.py:67
  210.3 1.7 copy-done.13
  212.0 1.8 split_terms.6
  216.2 5.5 %fc2_grad.1 = bf16[2,160,1280]{2,1,0:T(8,128)(2,1)S(1)} custom-call(bf16[8,2,128,320]{3,2,1,0:T(8,128)(2,1)} %get-tuple-element.234.hid_ref, bf16[8,2,128,1280]{3,2,1,0:T(8,128)(2,1)} %bitcast.97), custom_call_target="tpu_custom_call" | custom-call | flops 1024 | bytes 1024 | tf_op jit(solution)/shard_map/fc2_grad/pallas_call | solution.py:547
  221.7 10.6 %collective-permute-done.36.refs_3_ = bf16[4,48,1280]{2,1,0:T(8,128)(2,1)S(1)} collective-permute-done((bf16[4,48,1280]{2,1,0:T(8,128)(2,1)S(1)}, bf16[4,48,1280]{2,1,0:T(8,128)(2,1)S(1)}, u32[]{:S(2)}, u32[]{:S(2)}) %collective-permute-start.36) | collective-permute-done | bytes 491552 | tf_op jit(solution)/shard_map/ppermute | solution.py:67
  239.9 8.6 %fc1_grad.1 = bf16[32,8,1600]{2,1,0:T(8,128)(2,1)} custom-call(s32[7]{0:T(128)S(1)} %stack.76.place_ref, bf16[4,48,1280]{2,1,0:T(8,128)(2,1)} %get-tuple-element.218.refs_0_, bf16[4,48,1280]{2,1,0:T(8,128)(2,1)} %get-tuple-element.219.refs_1_, bf16[4,32,1280]{2,1,0:T(8,128)(2,1)S(1)} %copy-done.20, bf16[4,48,1280]{2,1,0:T(8,128)(2,1)} %collective-permute-done.26.refs_3_, ...), custom_call_target="tpu_custom_call" | custom-call | flops 1024 | bytes 1024 | tf_op jit(solution)/shard_map/fc1_grad/pallas_call | solution.py:590
  248.5 4.8 %collective-permute-done.41.refs_5_ = bf16[2,32,1280]{2,1,0:T(8,128)(2,1)S(1)} collective-permute-done((bf16[2,32,1280]{2,1,0:T(8,128)(2,1)S(1)}, bf16[2,32,1280]{2,1,0:T(8,128)(2,1)S(1)}, u32[]{:S(2)}, u32[]{:S(2)}) %collective-permute-start.41) | collective-permute-done | bytes 163872 | tf_op jit(solution)/shard_map/ppermute | solution.py:67
  254.8 2.5 collective-permute-start.43
  257.3 2.8 collective-permute-start.44
  260.1 2.8 collective-permute-done.44.refs_5_
  263.6 3.9 second_back.1
  268.4 14.0 %all_to_all.30.do_ref = bf16[16,80,128]{2,1,0:T(8,128)(2,1)} all-to-all(bf16[16,80,128]{2,1,0:T(8,128)(2,1)S(1)} %get-tuple-element.260), channel_id=1, replica_groups={{0,1,2,3,4,5,6,7,8,9,10,11,12,13,14,15},{16,17,18,19,20,21,22,23,24,25,..., dimensions={0} | all-to-all | bytes 655360 | tf_op jit(solution)/shard_map/all_to_all | solution.py:103
  282.4 4.7 %all-to-all-start.4 = ((bf16[32,8,1600]{2,1,0:T(8,128)(2,1)}), bf16[32,8,1600]{2,1,0:T(8,128)(2,1)S(1)}, u32[]{:S(2)}, u32[]{:S(2)}) async-start(bf16[32,8,1600]{2,1,0:T(8,128)(2,1)} %fc1_grad.1), calls=%async_computation.5 | async-start | bytes 1703936 | tf_op jit(solution)/shard_map/all_to_all | solution.py:106
  288.1 15.8 %attend_back.1 = (bf16[2048,384]{1,0:T(8,128)(2,1)}, f32[8,384]{1,0:T(8,128)S(1)}) custom-call(bf16[2048,384]{1,0:T(8,128)(2,1)S(1)} %get-tuple-element.205.q_ref.k_ref.v_ref, bf16[2048,384]{1,0:T(8,128)(2,1)S(1)} %get-tuple-element.205.q_ref.k_ref.v_ref, bf16[2048,384]{1,0:T(8,128)(2,1)S(1)} %get-tuple-element.205.q_ref.k_ref.v_ref, ...), custom_call_target="tpu_custom_call" | custom-call | flops 1024 | bytes 1024 | tf_op jit(solution)/shard_map/attend_back/pallas_call | solution.py:966
  305.3 2.4 terms.3
  309.3 2.0 all-to-all-done.4.in_ref
  311.3 2.4 terms.2.refs_0_
  313.8 2.7 collective-permute-done.46.refs_1_
  316.5 1.8 split_terms.9
  320.7 1.9 collective-permute-start.49
  323.6 8.4 %head_grad.1 = bf16[32,40,256]{2,1,0:T(8,128)(2,1)} custom-call(s32[7]{0:T(128)S(1)} %stack.76.place_ref, bf16[2048,1280]{1,0:T(8,128)(2,1)} %bitcast.99, bf16[2048,384]{1,0:T(8,128)(2,1)S(1)} %copy-done.3, bf16[1280,240]{1,0:T(8,128)(2,1)S(1)} %bitcast.90, f32[8,1280]{1,0:T(8,128)S(1)} %get-tuple-element.204.table_ref.refs_8_, ...), custom_call_target="tpu_custom_call" | custom-call | flops 1024 | bytes 1024 | tf_op jit(solution)/shard_map/head_grad/pallas_call | solution.py:817
  332.7 9.4 %collective-permute-done.48.refs_3_ = bf16[4,48,1280]{2,1,0:T(8,128)(2,1)S(1)} collective-permute-done((bf16[4,48,1280]{2,1,0:T(8,128)(2,1)S(1)}, bf16[4,48,1280]{2,1,0:T(8,128)(2,1)S(1)}, u32[]{:S(2)}, u32[]{:S(2)}) %collective-permute-start.48) | collective-permute-done | bytes 491552 | tf_op jit(solution)/shard_map/ppermute | solution.py:67
  342.1 1.9 split_terms.10
  345.5 3.7 all-to-all-start.5
  350.9 1.8 collective-permute-start.51
  355.6 4.2 %output_grad.1 = bf16[2,40,1280]{2,1,0:T(8,128)(2,1)S(1)} custom-call(bf16[16,80,128]{2,1,0:T(8,128)(2,1)} %get-tuple-element.290.o_ref, bf16[16,128,1280]{2,1,0:T(8,128)(2,1)} %bitcast.103), custom_call_target="tpu_custom_call" | custom-call | flops 1024 | bytes 1024 | tf_op jit(solution)/shard_map/output_grad/pallas_call | solution.py:624
  361.5 2.1 collective-permute-done.51.refs_3_
  366.1 2.1 collective-permute-start.54
  369.6 1.9 collective-permute-start.56
  372.3 1.8 collective-permute-done.56.refs_5_
  375.9 1.8 first_back.1
  377.7 2.8 collective-permute-start.57
  381.7 1.9 collect_hidden.1
  384.2 2.1 convert_add_fusion
  (249 shorter events, 88.3 us)
Async XLA Ops:
  7.2 120.6 %all-gather.7.cloned.1.call-start = ((), (), s32[]{:S(2)}) async-start(), calls=%async_computation.8 | async-start | bytes 3481600 | tf_op jit(solution)/shard_map/all_gather | solution.py:100
  10.5 12.7 %collective-permute-start = (bf16[72,1280]{1,0:T(8,128)(2,1)S(1)}, bf16[72,1280]{1,0:T(8,128)(2,1)S(1)}, u32[]{:S(2)}, u32[]{:S(2)}) collective-permute-start(bf16[72,1280]{1,0:T(8,128)(2,1)S(1)} %get-tuple-element.167), channel_id=1, source_target_pairs={{0,16},{1,17},{2,18},{3,19},{4,20},{5,21},{6,22},{7,23},{8,24},{9,... | collective-permute-start | bytes 552968 | tf_op jit(solution)/shard_map/ppermute | solution.py:67
  23.8 15.4 %collective-permute-start.3 = (bf16[104,1280]{1,0:T(8,128)(2,1)S(1)}, bf16[104,1280]{1,0:T(8,128)(2,1)S(1)}, u32[]{:S(2)}, u32[]{:S(2)}) collective-permute-start(bf16[104,1280]{1,0:T(8,128)(2,1)S(1)} %pad_maximum_fusion.2), channel_id=1, source_target_pairs={{0,16},{1,17},{2,18},{3,19},{4,20},{5,21},{6,22},{7,23},{8,24},{9,... | collective-permute-start | bytes 798728 | tf_op jit(solution)/shard_map/ppermute | solution.py:67
  25.1 14.2 %collective-permute-start.5 = (bf16[1,64,1280]{2,1,0:T(8,128)(2,1)S(1)}, bf16[1,64,1280]{2,1,0:T(8,128)(2,1)S(1)}, u32[]{:S(2)}, u32[]{:S(2)}) collective-permute-start(bf16[1,64,1280]{2,1,0:T(8,128)(2,1)S(1)} %pad_maximum_fusion.4.refs_2_), channel_id=1, source_target_pairs={{0,2},{1,3},{2,0},{3,1},{4,6},{5,7},{6,4},{7,5},{8,10},{9,11},{10,... | collective-permute-start | bytes 491528 | tf_op jit(solution)/shard_map/ppermute | solution.py:67
  26.7 6.4 %collective-permute-start.2 = (bf16[1,48,1280]{2,1,0:T(8,128)(2,1)S(1)}, bf16[1,48,1280]{2,1,0:T(8,128)(2,1)S(1)}, u32[]{:S(2)}, u32[]{:S(2)}) collective-permute-start(bf16[1,48,1280]{2,1,0:T(8,128)(2,1)S(1)} %get-tuple-element.172.refs_0_), channel_id=1, source_target_pairs={{0,8},{1,9},{2,10},{3,11},{4,12},{5,13},{6,14},{7,15},{8,0},{9,1},... | collective-permute-start | bytes 368648 | tf_op jit(solution)/shard_map/ppermute | solution.py:67
  29.6 9.7 %collective-permute-start.4 = (bf16[1,48,1280]{2,1,0:T(8,128)(2,1)S(1)}, bf16[1,48,1280]{2,1,0:T(8,128)(2,1)S(1)}, u32[]{:S(2)}, u32[]{:S(2)}) collective-permute-start(bf16[1,48,1280]{2,1,0:T(8,128)(2,1)S(1)} %get-tuple-element.173.refs_1_), channel_id=1, source_target_pairs={{0,4},{1,5},{2,6},{3,7},{4,0},{5,1},{6,2},{7,3},{8,12},{9,13},{10,... | collective-permute-start | bytes 368648 | tf_op jit(solution)/shard_map/ppermute | solution.py:67
  39.6 14.0 %collective-permute-start.6 = (bf16[2,48,1280]{2,1,0:T(8,128)(2,1)S(1)}, bf16[2,48,1280]{2,1,0:T(8,128)(2,1)S(1)}, u32[]{:S(2)}, u32[]{:S(2)}) collective-permute-start(bf16[2,48,1280]{2,1,0:T(8,128)(2,1)S(1)} %get-tuple-element.179.refs_0_), channel_id=1, source_target_pairs={{0,4},{1,5},{2,6},{3,7},{4,0},{5,1},{6,2},{7,3},{8,12},{9,13},{10,... | collective-permute-start | bytes 737288 | tf_op jit(solution)/shard_map/ppermute | solution.py:67
  41.2 12.4 %collective-permute-start.8 = (bf16[2,48,1280]{2,1,0:T(8,128)(2,1)S(1)}, bf16[2,48,1280]{2,1,0:T(8,128)(2,1)S(1)}, u32[]{:S(2)}, u32[]{:S(2)}) collective-permute-start(bf16[2,48,1280]{2,1,0:T(8,128)(2,1)S(1)} %get-tuple-element.180.refs_1_), channel_id=1, source_target_pairs={{0,2},{1,3},{2,0},{3,1},{4,6},{5,7},{6,4},{7,5},{8,10},{9,11},{10,... | collective-permute-start | bytes 737288 | tf_op jit(solution)/shard_map/ppermute | solution.py:67
  42.7 13.1 %collective-permute-start.9 = (bf16[2,64,1280]{2,1,0:T(8,128)(2,1)S(1)}, bf16[2,64,1280]{2,1,0:T(8,128)(2,1)S(1)}, u32[]{:S(2)}, u32[]{:S(2)}) collective-permute-start(bf16[2,64,1280]{2,1,0:T(8,128)(2,1)S(1)} %get-tuple-element.181.refs_2_), channel_id=1, source_target_pairs={{0,8},{1,9},{2,10},{3,11},{4,12},{5,13},{6,14},{7,15},{8,0},{9,1},... | collective-permute-start | bytes 983048 | tf_op jit(solution)/shard_map/ppermute | solution.py:67
  43.4 10.2 %collective-permute-start.7 = (bf16[80,1280]{1,0:T(8,128)(2,1)S(1)}, bf16[80,1280]{1,0:T(8,128)(2,1)S(1)}, u32[]{:S(2)}, u32[]{:S(2)}) collective-permute-start(bf16[80,1280]{1,0:T(8,128)(2,1)S(1)} %get-tuple-element.182), channel_id=1, source_target_pairs={{0,16},{1,17},{2,18},{3,19},{4,20},{5,21},{6,22},{7,23},{8,24},{9,... | collective-permute-start | bytes 614408 | tf_op jit(solution)/shard_map/ppermute | solution.py:67
  56.9 14.5 %collective-permute-start.10 = (bf16[4,48,1280]{2,1,0:T(8,128)(2,1)}, bf16[4,48,1280]{2,1,0:T(8,128)(2,1)S(1)}, u32[]{:S(2)}, u32[]{:S(2)}) collective-permute-start(bf16[4,48,1280]{2,1,0:T(8,128)(2,1)} %get-tuple-element.192.refs_0_), channel_id=1, source_target_pairs={{0,2},{1,3},{2,0},{3,1},{4,6},{5,7},{6,4},{7,5},{8,10},{9,11},{10,... | collective-permute-start | bytes 1474568 | tf_op jit(solution)/shard_map/ppermute | solution.py:67
  57.4 15.6 %collective-permute-start.12 = (bf16[4,48,1280]{2,1,0:T(8,128)(2,1)S(1)}, bf16[4,48,1280]{2,1,0:T(8,128)(2,1)S(1)}, u32[]{:S(2)}, u32[]{:S(2)}) collective-permute-start(bf16[4,48,1280]{2,1,0:T(8,128)(2,1)S(1)} %get-tuple-element.193.refs_1_), channel_id=1, source_target_pairs={{0,8},{1,9},{2,10},{3,11},{4,12},{5,13},{6,14},{7,15},{8,0},{9,1},... | collective-permute-start | bytes 1474568 | tf_op jit(solution)/shard_map/ppermute | solution.py:67
  57.9 15.1 %collective-permute-start.13 = (bf16[4,64,1280]{2,1,0:T(8,128)(2,1)S(1)}, bf16[4,64,1280]{2,1,0:T(8,128)(2,1)S(1)}, u32[]{:S(2)}, u32[]{:S(2)}) collective-permute-start(bf16[4,64,1280]{2,1,0:T(8,128)(2,1)S(1)} %get-tuple-element.194.refs_2_), channel_id=1, source_target_pairs={{0,4},{1,5},{2,6},{3,7},{4,0},{5,1},{6,2},{7,3},{8,12},{9,13},{10,... | collective-permute-start | bytes 1966088 | tf_op jit(solution)/shard_map/ppermute | solution.py:67
  59.5 11.9 %collective-permute-start.11 = (bf16[80,1280]{1,0:T(8,128)(2,1)}, bf16[80,1280]{1,0:T(8,128)(2,1)}, u32[]{:S(2)}, u32[]{:S(2)}) collective-permute-start(bf16[80,1280]{1,0:T(8,128)(2,1)} %get-tuple-element.187), channel_id=1, source_target_pairs={{0,16},{1,17},{2,18},{3,19},{4,20},{5,21},{6,22},{7,23},{8,24},{9,... | collective-permute-start | bytes 614408 | tf_op jit(solution)/shard_map/ppermute | solution.py:67
  73.0 109.2 %all-gather.9.cloned.1.call-start = ((), (), s32[]{:S(2)}) async-start(), calls=%async_computation.9 | async-start | bytes 5570560 | tf_op jit(solution)/shard_map/all_gather | solution.py:100
  75.0 24.0 %all-to-all-start = ((bf16[32,40,240]{2,1,0:T(8,128)(2,1)}), bf16[32,40,240]{2,1,0:T(8,128)(2,1)S(1)}, u32[]{:S(2)}, u32[]{:S(2)}) async-start(bf16[32,40,240]{2,1,0:T(8,128)(2,1)} %get-tuple-element.191), calls=%async_computation | async-start | bytes 1310720 | tf_op jit(solution)/shard_map/all_to_all | solution.py:106
  79.0 12.1 %collective-permute-start.16 = (bf16[4,64,1280]{2,1,0:T(8,128)(2,1)S(1)}, bf16[4,64,1280]{2,1,0:T(8,128)(2,1)S(1)}, u32[]{:S(2)}, u32[]{:S(2)}) collective-permute-start(bf16[4,64,1280]{2,1,0:T(8,128)(2,1)S(1)} %get-tuple-element.194.refs_2_), channel_id=1, source_target_pairs={{0,1},{1,0},{2,3},{3,2},{4,5},{5,4},{6,7},{7,6},{8,9},{9,8},{10,11... | collective-permute-start | bytes 1966088 | tf_op jit(solution)/shard_map/ppermute | solution.py:67
  79.2 11.9 %collective-permute-start.19 = (bf16[4,64,1280]{2,1,0:T(8,128)(2,1)S(1)}, bf16[4,64,1280]{2,1,0:T(8,128)(2,1)S(1)}, u32[]{:S(2)}, u32[]{:S(2)}) collective-permute-start(bf16[4,64,1280]{2,1,0:T(8,128)(2,1)S(1)} %collective-permute-done.13.refs_5_), channel_id=1, source_target_pairs={{0,1},{1,0},{2,3},{3,2},{4,5},{5,4},{6,7},{7,6},{8,9},{9,8},{10,11... | collective-permute-start | bytes 1966088 | tf_op jit(solution)/shard_map/ppermute | solution.py:67
  79.5 11.6 %collective-permute-start.15 = (bf16[4,48,1280]{2,1,0:T(8,128)(2,1)}, bf16[4,48,1280]{2,1,0:T(8,128)(2,1)S(1)}, u32[]{:S(2)}, u32[]{:S(2)}) collective-permute-start(bf16[4,48,1280]{2,1,0:T(8,128)(2,1)} %copy-done.26), channel_id=1, source_target_pairs={{0,1},{1,0},{2,3},{3,2},{4,5},{5,4},{6,7},{7,6},{8,9},{9,8},{10,11... | collective-permute-start | bytes 1474568 | tf_op jit(solution)/shard_map/ppermute | solution.py:67
  79.7 11.3 %collective-permute-start.17 = (bf16[4,48,1280]{2,1,0:T(8,128)(2,1)}, bf16[4,48,1280]{2,1,0:T(8,128)(2,1)S(1)}, u32[]{:S(2)}, u32[]{:S(2)}) collective-permute-start(bf16[4,48,1280]{2,1,0:T(8,128)(2,1)} %copy-done.28), channel_id=1, source_target_pairs={{0,1},{1,0},{2,3},{3,2},{4,5},{5,4},{6,7},{7,6},{8,9},{9,8},{10,11... | collective-permute-start | bytes 1474568 | tf_op jit(solution)/shard_map/ppermute | solution.py:67
  80.8 10.3 %collective-permute-start.18 = (bf16[4,48,1280]{2,1,0:T(8,128)(2,1)}, bf16[4,48,1280]{2,1,0:T(8,128)(2,1)S(1)}, u32[]{:S(2)}, u32[]{:S(2)}) collective-permute-start(bf16[4,48,1280]{2,1,0:T(8,128)(2,1)} %copy-done.30), channel_id=1, source_target_pairs={{0,1},{1,0},{2,3},{3,2},{4,5},{5,4},{6,7},{7,6},{8,9},{9,8},{10,11... | collective-permute-start | bytes 1474568 | tf_op jit(solution)/shard_map/ppermute | solution.py:67
  99.0 25.0 %all-to-all-start.1 = ((bf16[32,8,1600]{2,1,0:T(8,128)(2,1)}), bf16[32,8,1600]{2,1,0:T(8,128)(2,1)S(1)}, u32[]{:S(2)}, u32[]{:S(2)}) async-start(bf16[32,8,1600]{2,1,0:T(8,128)(2,1)} %get-tuple-element.208), calls=%async_computation.1 | async-start | bytes 1703936 | tf_op jit(solution)/shard_map/all_to_all | solution.py:106
  124.0 12.0 %all-to-all-start.2 = ((bf16[16,80,128]{2,1,0:T(8,128)(2,1)}), bf16[16,80,128]{2,1,0:T(8,128)(2,1)S(1)}, u32[]{:S(2)}, u32[]{:S(2)}) async-start(bf16[16,80,128]{2,1,0:T(8,128)(2,1)} %get-tuple-element.290.o_ref), calls=%async_computation.2 | async-start | bytes 655360 | tf_op jit(solution)/shard_map/all_to_all | solution.py:103
  127.6 176.4 %reduce-scatter.2.cloned.1.call-start = ((), (), s32[]{:S(2)}) async-start(), calls=%async_computation.7 | async-start | bytes 5570560 | tf_op jit(solution)/shard_map/reduce_scatter | solution.py:1086
  139.8 9.2 %collective-permute-start.20 = (bf16[1,48,1280]{2,1,0:T(8,128)(2,1)S(1)}, bf16[1,48,1280]{2,1,0:T(8,128)(2,1)S(1)}, u32[]{:S(2)}, u32[]{:S(2)}) collective-permute-start(bf16[1,48,1280]{2,1,0:T(8,128)(2,1)S(1)} %get-tuple-element.212.refs_0_), channel_id=1, source_target_pairs={{0,8},{1,9},{2,10},{3,11},{4,12},{5,13},{6,14},{7,15},{8,0},{9,1},... | collective-permute-start | bytes 368648 | tf_op jit(solution)/shard_map/ppermute | solution.py:67
  140.9 8.0 %collective-permute-start.21 = (bf16[1,48,1280]{2,1,0:T(8,128)(2,1)S(1)}, bf16[1,48,1280]{2,1,0:T(8,128)(2,1)S(1)}, u32[]{:S(2)}, u32[]{:S(2)}) collective-permute-start(bf16[1,48,1280]{2,1,0:T(8,128)(2,1)S(1)} %get-tuple-element.213.refs_1_), channel_id=1, source_target_pairs={{0,4},{1,5},{2,6},{3,7},{4,0},{5,1},{6,2},{7,3},{8,12},{9,13},{10,... | collective-permute-start | bytes 368648 | tf_op jit(solution)/shard_map/ppermute | solution.py:67
  142.5 6.5 %collective-permute-start.22 = (bf16[1,32,1280]{2,1,0:T(8,128)(2,1)S(1)}, bf16[1,32,1280]{2,1,0:T(8,128)(2,1)S(1)}, u32[]{:S(2)}, u32[]{:S(2)}) collective-permute-start(bf16[1,32,1280]{2,1,0:T(8,128)(2,1)S(1)} %get-tuple-element.214.refs_2_), channel_id=1, source_target_pairs={{0,2},{1,3},{2,0},{3,1},{4,6},{5,7},{6,4},{7,5},{8,10},{9,11},{10,... | collective-permute-start | bytes 245768 | tf_op jit(solution)/shard_map/ppermute | solution.py:67
  149.2 13.1 %collective-permute-start.23 = (bf16[2,48,1280]{2,1,0:T(8,128)(2,1)S(1)}, bf16[2,48,1280]{2,1,0:T(8,128)(2,1)S(1)}, u32[]{:S(2)}, u32[]{:S(2)}) collective-permute-start(bf16[2,48,1280]{2,1,0:T(8,128)(2,1)S(1)} %get-tuple-element.215.refs_0_), channel_id=1, source_target_pairs={{0,4},{1,5},{2,6},{3,7},{4,0},{5,1},{6,2},{7,3},{8,12},{9,13},{10,... | collective-permute-start | bytes 737288 | tf_op jit(solution)/shard_map/ppermute | solution.py:67
  150.0 14.0 %collective-permute-start.24 = (bf16[2,48,1280]{2,1,0:T(8,128)(2,1)S(1)}, bf16[2,48,1280]{2,1,0:T(8,128)(2,1)S(1)}, u32[]{:S(2)}, u32[]{:S(2)}) collective-permute-start(bf16[2,48,1280]{2,1,0:T(8,128)(2,1)S(1)} %get-tuple-element.216.refs_1_), channel_id=1, source_target_pairs={{0,2},{1,3},{2,0},{3,1},{4,6},{5,7},{6,4},{7,5},{8,10},{9,11},{10,... | collective-permute-start | bytes 737288 | tf_op jit(solution)/shard_map/ppermute | solution.py:67
  152.5 9.8 %collective-permute-start.25 = (bf16[2,32,1280]{2,1,0:T(8,128)(2,1)S(1)}, bf16[2,32,1280]{2,1,0:T(8,128)(2,1)S(1)}, u32[]{:S(2)}, u32[]{:S(2)}) collective-permute-start(bf16[2,32,1280]{2,1,0:T(8,128)(2,1)S(1)} %get-tuple-element.217.refs_2_), channel_id=1, source_target_pairs={{0,8},{1,9},{2,10},{3,11},{4,12},{5,13},{6,14},{7,15},{8,0},{9,1},... | collective-permute-start | bytes 491528 | tf_op jit(solution)/shard_map/ppermute | solution.py:67
  165.1 13.1 %collective-permute-start.26 = (bf16[4,48,1280]{2,1,0:T(8,128)(2,1)}, bf16[4,48,1280]{2,1,0:T(8,128)(2,1)}, u32[]{:S(2)}, u32[]{:S(2)}) collective-permute-start(bf16[4,48,1280]{2,1,0:T(8,128)(2,1)} %get-tuple-element.218.refs_0_), channel_id=1, source_target_pairs={{0,2},{1,3},{2,0},{3,1},{4,6},{5,7},{6,4},{7,5},{8,10},{9,11},{10,... | collective-permute-start | bytes 1474568 | tf_op jit(solution)/shard_map/ppermute | solution.py:67
  167.1 12.6 %collective-permute-start.27 = (bf16[4,48,1280]{2,1,0:T(8,128)(2,1)}, bf16[4,48,1280]{2,1,0:T(8,128)(2,1)}, u32[]{:S(2)}, u32[]{:S(2)}) collective-permute-start(bf16[4,48,1280]{2,1,0:T(8,128)(2,1)} %get-tuple-element.219.refs_1_), channel_id=1, source_target_pairs={{0,8},{1,9},{2,10},{3,11},{4,12},{5,13},{6,14},{7,15},{8,0},{9,1},... | collective-permute-start | bytes 1474568 | tf_op jit(solution)/shard_map/ppermute | solution.py:67
  168.4 8.5 %collective-permute-start.28 = (bf16[4,32,1280]{2,1,0:T(8,128)(2,1)S(1)}, bf16[4,32,1280]{2,1,0:T(8,128)(2,1)}, u32[]{:S(2)}, u32[]{:S(2)}) collective-permute-start(bf16[4,32,1280]{2,1,0:T(8,128)(2,1)S(1)} %get-tuple-element.220.refs_2_), channel_id=1, source_target_pairs={{0,4},{1,5},{2,6},{3,7},{4,0},{5,1},{6,2},{7,3},{8,12},{9,13},{10,... | collective-permute-start | bytes 983048 | tf_op jit(solution)/shard_map/ppermute | solution.py:67
  169.1 7.8 %collective-permute-start.31 = (bf16[4,32,1280]{2,1,0:T(8,128)(2,1)S(1)}, bf16[4,32,1280]{2,1,0:T(8,128)(2,1)S(1)}, u32[]{:S(2)}, u32[]{:S(2)}) collective-permute-start(bf16[4,32,1280]{2,1,0:T(8,128)(2,1)S(1)} %get-tuple-element.220.refs_2_), channel_id=1, source_target_pairs={{0,1},{1,0},{2,3},{3,2},{4,5},{5,4},{6,7},{7,6},{8,9},{9,8},{10,11... | collective-permute-start | bytes 983048 | tf_op jit(solution)/shard_map/ppermute | solution.py:67
  171.0 23.0 %collective-permute-start.29 = (bf16[4,48,1280]{2,1,0:T(8,128)(2,1)}, bf16[4,48,1280]{2,1,0:T(8,128)(2,1)}, u32[]{:S(2)}, u32[]{:S(2)}) collective-permute-start(bf16[4,48,1280]{2,1,0:T(8,128)(2,1)} %get-tuple-element.218.refs_0_), channel_id=1, source_target_pairs={{0,1},{1,0},{2,3},{3,2},{4,5},{5,4},{6,7},{7,6},{8,9},{9,8},{10,11... | collective-permute-start | bytes 1474568 | tf_op jit(solution)/shard_map/ppermute | solution.py:67
  176.9 17.1 %collective-permute-start.30 = (bf16[4,48,1280]{2,1,0:T(8,128)(2,1)}, bf16[4,48,1280]{2,1,0:T(8,128)(2,1)}, u32[]{:S(2)}, u32[]{:S(2)}) collective-permute-start(bf16[4,48,1280]{2,1,0:T(8,128)(2,1)} %get-tuple-element.219.refs_1_), channel_id=1, source_target_pairs={{0,1},{1,0},{2,3},{3,2},{4,5},{5,4},{6,7},{7,6},{8,9},{9,8},{10,11... | collective-permute-start | bytes 1474568 | tf_op jit(solution)/shard_map/ppermute | solution.py:67
  177.6 16.4 %collective-permute-start.34 = (bf16[4,32,1280]{2,1,0:T(8,128)(2,1)}, bf16[4,32,1280]{2,1,0:T(8,128)(2,1)}, u32[]{:S(2)}, u32[]{:S(2)}) collective-permute-start(bf16[4,32,1280]{2,1,0:T(8,128)(2,1)} %collective-permute-done.28.refs_5_), channel_id=1, source_target_pairs={{0,1},{1,0},{2,3},{3,2},{4,5},{5,4},{6,7},{7,6},{8,9},{9,8},{10,11... | collective-permute-start | bytes 983048 | tf_op jit(solution)/shard_map/ppermute | solution.py:67
  178.2 15.8 %collective-permute-start.32 = (bf16[4,48,1280]{2,1,0:T(8,128)(2,1)}, bf16[4,48,1280]{2,1,0:T(8,128)(2,1)}, u32[]{:S(2)}, u32[]{:S(2)}) collective-permute-start(bf16[4,48,1280]{2,1,0:T(8,128)(2,1)} %collective-permute-done.26.refs_3_), channel_id=1, source_target_pairs={{0,1},{1,0},{2,3},{3,2},{4,5},{5,4},{6,7},{7,6},{8,9},{9,8},{10,11... | collective-permute-start | bytes 1474568 | tf_op jit(solution)/shard_map/ppermute | solution.py:67
  179.7 14.4 %collective-permute-start.33 = (bf16[4,48,1280]{2,1,0:T(8,128)(2,1)}, bf16[4,48,1280]{2,1,0:T(8,128)(2,1)}, u32[]{:S(2)}, u32[]{:S(2)}) collective-permute-start(bf16[4,48,1280]{2,1,0:T(8,128)(2,1)} %collective-permute-done.27.refs_4_), channel_id=1, source_target_pairs={{0,1},{1,0},{2,3},{3,2},{4,5},{5,4},{6,7},{7,6},{8,9},{9,8},{10,11... | collective-permute-start | bytes 1474568 | tf_op jit(solution)/shard_map/ppermute | solution.py:67
  204.9 147.8 %all-gather.11.cloned.1.call-start = ((), (), s32[]{:S(2)}) async-start(), calls=%async_computation.10 | async-start | bytes 5570560 | tf_op jit(solution)/shard_map/all_gather | solution.py:100
  213.8 18.4 %collective-permute-start.36 = (bf16[4,48,1280]{2,1,0:T(8,128)(2,1)S(1)}, bf16[4,48,1280]{2,1,0:T(8,128)(2,1)S(1)}, u32[]{:S(2)}, u32[]{:S(2)}) collective-permute-start(bf16[4,48,1280]{2,1,0:T(8,128)(2,1)S(1)} %get-tuple-element.232), channel_id=1, source_target_pairs={{0,8},{1,9},{2,10},{3,11},{4,12},{5,13},{6,14},{7,15},{8,0},{9,1},... | collective-permute-start | bytes 1474568 | tf_op jit(solution)/shard_map/ppermute | solution.py:67
  215.0 18.5 %collective-permute-start.37 = (bf16[4,48,1280]{2,1,0:T(8,128)(2,1)S(1)}, bf16[4,48,1280]{2,1,0:T(8,128)(2,1)S(1)}, u32[]{:S(2)}, u32[]{:S(2)}) collective-permute-start(bf16[4,48,1280]{2,1,0:T(8,128)(2,1)S(1)} %get-tuple-element.236), channel_id=1, source_target_pairs={{0,4},{1,5},{2,6},{3,7},{4,0},{5,1},{6,2},{7,3},{8,12},{9,13},{10,... | collective-permute-start | bytes 1474568 | tf_op jit(solution)/shard_map/ppermute | solution.py:67
  215.5 17.0 %collective-permute-start.38 = (bf16[4,32,1280]{2,1,0:T(8,128)(2,1)S(1)}, bf16[4,32,1280]{2,1,0:T(8,128)(2,1)S(1)}, u32[]{:S(2)}, u32[]{:S(2)}) collective-permute-start(bf16[4,32,1280]{2,1,0:T(8,128)(2,1)S(1)} %get-tuple-element.237), channel_id=1, source_target_pairs={{0,2},{1,3},{2,0},{3,1},{4,6},{5,7},{6,4},{7,5},{8,10},{9,11},{10,... | collective-permute-start | bytes 983048 | tf_op jit(solution)/shard_map/ppermute | solution.py:67
  235.6 27.3 %collective-permute-start.45 = (bf16[160,1280]{1,0:T(8,128)(2,1)S(1)}, bf16[160,1280]{1,0:T(8,128)(2,1)S(1)}, u32[]{:S(2)}, u32[]{:S(2)}) collective-permute-start(bf16[160,1280]{1,0:T(8,128)(2,1)S(1)} %get-tuple-element.317), channel_id=1, source_target_pairs={{0,16},{1,17},{2,18},{3,19},{4,20},{5,21},{6,22},{7,23},{8,24},{9,... | collective-permute-start | bytes 1228808 | tf_op jit(solution)/shard_map/ppermute | solution.py:67
  236.1 12.4 %collective-permute-start.39 = (bf16[2,48,1280]{2,1,0:T(8,128)(2,1)S(1)}, bf16[2,48,1280]{2,1,0:T(8,128)(2,1)S(1)}, u32[]{:S(2)}, u32[]{:S(2)}) collective-permute-start(bf16[2,48,1280]{2,1,0:T(8,128)(2,1)S(1)} %get-tuple-element.241), channel_id=1, source_target_pairs={{0,4},{1,5},{2,6},{3,7},{4,0},{5,1},{6,2},{7,3},{8,12},{9,13},{10,... | collective-permute-start | bytes 737288 | tf_op jit(solution)/shard_map/ppermute | solution.py:67
  237.2 16.1 %collective-permute-start.40 = (bf16[2,48,1280]{2,1,0:T(8,128)(2,1)S(1)}, bf16[2,48,1280]{2,1,0:T(8,128)(2,1)S(1)}, u32[]{:S(2)}, u32[]{:S(2)}) collective-permute-start(bf16[2,48,1280]{2,1,0:T(8,128)(2,1)S(1)} %get-tuple-element.245), channel_id=1, source_target_pairs={{0,2},{1,3},{2,0},{3,1},{4,6},{5,7},{6,4},{7,5},{8,10},{9,11},{10,... | collective-permute-start | bytes 737288 | tf_op jit(solution)/shard_map/ppermute | solution.py:67
  238.7 14.6 %collective-permute-start.41 = (bf16[2,32,1280]{2,1,0:T(8,128)(2,1)S(1)}, bf16[2,32,1280]{2,1,0:T(8,128)(2,1)S(1)}, u32[]{:S(2)}, u32[]{:S(2)}) collective-permute-start(bf16[2,32,1280]{2,1,0:T(8,128)(2,1)S(1)} %get-tuple-element.246), channel_id=1, source_target_pairs={{0,8},{1,9},{2,10},{3,11},{4,12},{5,13},{6,14},{7,15},{8,0},{9,1},... | collective-permute-start | bytes 491528 | tf_op jit(solution)/shard_map/ppermute | solution.py:67
  254.8 8.1 %collective-permute-start.42 = (bf16[1,48,1280]{2,1,0:T(8,128)(2,1)S(1)}, bf16[1,48,1280]{2,1,0:T(8,128)(2,1)S(1)}, u32[]{:S(2)}, u32[]{:S(2)}) collective-permute-start(bf16[1,48,1280]{2,1,0:T(8,128)(2,1)S(1)} %get-tuple-element.250), channel_id=1, source_target_pairs={{0,2},{1,3},{2,0},{3,1},{4,6},{5,7},{6,4},{7,5},{8,10},{9,11},{10,... | collective-permute-start | bytes 368648 | tf_op jit(solution)/shard_map/ppermute | solution.py:67
  254.8 8.1 %collective-permute-start.43 = (bf16[1,48,1280]{2,1,0:T(8,128)(2,1)S(1)}, bf16[1,48,1280]{2,1,0:T(8,128)(2,1)S(1)}, u32[]{:S(2)}, u32[]{:S(2)}) collective-permute-start(bf16[1,48,1280]{2,1,0:T(8,128)(2,1)S(1)} %get-tuple-element.251), channel_id=1, source_target_pairs={{0,8},{1,9},{2,10},{3,11},{4,12},{5,13},{6,14},{7,15},{8,0},{9,1},... | collective-permute-start | bytes 368648 | tf_op jit(solution)/shard_map/ppermute | solution.py:67
  257.3 5.6 %collective-permute-start.44 = (bf16[1,32,1280]{2,1,0:T(8,128)(2,1)S(1)}, bf16[1,32,1280]{2,1,0:T(8,128)(2,1)S(1)}, u32[]{:S(2)}, u32[]{:S(2)}) collective-permute-start(bf16[1,32,1280]{2,1,0:T(8,128)(2,1)S(1)} %get-tuple-element.252), channel_id=1, source_target_pairs={{0,4},{1,5},{2,6},{3,7},{4,0},{5,1},{6,2},{7,3},{8,12},{9,13},{10,... | collective-permute-start | bytes 245768 | tf_op jit(solution)/shard_map/ppermute | solution.py:67
  282.4 28.8 %all-to-all-start.4 = ((bf16[32,8,1600]{2,1,0:T(8,128)(2,1)}), bf16[32,8,1600]{2,1,0:T(8,128)(2,1)S(1)}, u32[]{:S(2)}, u32[]{:S(2)}) async-start(bf16[32,8,1600]{2,1,0:T(8,128)(2,1)} %fc1_grad.1), calls=%async_computation.5 | async-start | bytes 1703936 | tf_op jit(solution)/shard_map/all_to_all | solution.py:106
  318.5 13.4 %collective-permute-start.47 = (bf16[64,1280]{1,0:T(8,128)(2,1)S(1)}, bf16[64,1280]{1,0:T(8,128)(2,1)S(1)}, u32[]{:S(2)}, u32[]{:S(2)}) collective-permute-start(bf16[64,1280]{1,0:T(8,128)(2,1)S(1)} %dynamic-slice_bitcast_fusion.3), channel_id=1, source_target_pairs={{0,16},{1,17},{2,18},{3,19},{4,20},{5,21},{6,22},{7,23},{8,24},{9,... | collective-permute-start | bytes 491528 | tf_op jit(solution)/shard_map/ppermute | solution.py:67
  320.2 21.8 %collective-permute-start.48 = (bf16[4,48,1280]{2,1,0:T(8,128)(2,1)S(1)}, bf16[4,48,1280]{2,1,0:T(8,128)(2,1)S(1)}, u32[]{:S(2)}, u32[]{:S(2)}) collective-permute-start(bf16[4,48,1280]{2,1,0:T(8,128)(2,1)S(1)} %get-tuple-element.272), channel_id=1, source_target_pairs={{0,8},{1,9},{2,10},{3,11},{4,12},{5,13},{6,14},{7,15},{8,0},{9,1},... | collective-permute-start | bytes 1474568 | tf_op jit(solution)/shard_map/ppermute | solution.py:67
  320.7 21.4 %collective-permute-start.49 = (bf16[4,48,1280]{2,1,0:T(8,128)(2,1)S(1)}, bf16[4,48,1280]{2,1,0:T(8,128)(2,1)S(1)}, u32[]{:S(2)}, u32[]{:S(2)}) collective-permute-start(bf16[4,48,1280]{2,1,0:T(8,128)(2,1)S(1)} %get-tuple-element.283), channel_id=1, source_target_pairs={{0,4},{1,5},{2,6},{3,7},{4,0},{5,1},{6,2},{7,3},{8,12},{9,13},{10,... | collective-permute-start | bytes 1474568 | tf_op jit(solution)/shard_map/ppermute | solution.py:67
  322.6 19.5 %collective-permute-start.50 = (bf16[4,32,1280]{2,1,0:T(8,128)(2,1)S(1)}, bf16[4,32,1280]{2,1,0:T(8,128)(2,1)S(1)}, u32[]{:S(2)}, u32[]{:S(2)}) collective-permute-start(bf16[4,32,1280]{2,1,0:T(8,128)(2,1)S(1)} %get-tuple-element.284), channel_id=1, source_target_pairs={{0,2},{1,3},{2,0},{3,1},{4,6},{5,7},{6,4},{7,5},{8,10},{9,11},{10,... | collective-permute-start | bytes 983048 | tf_op jit(solution)/shard_map/ppermute | solution.py:67
  345.5 26.8 %all-to-all-start.5 = ((bf16[32,40,256]{2,1,0:T(8,128)(2,1)}), bf16[32,40,256]{2,1,0:T(8,128)(2,1)S(1)}, u32[]{:S(2)}, u32[]{:S(2)}) async-start(bf16[32,40,256]{2,1,0:T(8,128)(2,1)} %head_grad.1), calls=%async_computation.6 | async-start | bytes 1310720 | tf_op jit(solution)/shard_map/all_to_all | solution.py:106
  350.9 12.7 %collective-permute-start.51 = (bf16[2,48,1280]{2,1,0:T(8,128)(2,1)}, bf16[2,48,1280]{2,1,0:T(8,128)(2,1)S(1)}, u32[]{:S(2)}, u32[]{:S(2)}) collective-permute-start(bf16[2,48,1280]{2,1,0:T(8,128)(2,1)} %get-tuple-element.288), channel_id=1, source_target_pairs={{0,4},{1,5},{2,6},{3,7},{4,0},{5,1},{6,2},{7,3},{8,12},{9,13},{10,... | collective-permute-start | bytes 737288 | tf_op jit(solution)/shard_map/ppermute | solution.py:67
  352.7 12.0 %collective-permute-start.52 = (bf16[2,48,1280]{2,1,0:T(8,128)(2,1)}, bf16[2,48,1280]{2,1,0:T(8,128)(2,1)S(1)}, u32[]{:S(2)}, u32[]{:S(2)}) collective-permute-start(bf16[2,48,1280]{2,1,0:T(8,128)(2,1)} %get-tuple-element.293), channel_id=1, source_target_pairs={{0,2},{1,3},{2,0},{3,1},{4,6},{5,7},{6,4},{7,5},{8,10},{9,11},{10,... | collective-permute-start | bytes 737288 | tf_op jit(solution)/shard_map/ppermute | solution.py:67
  354.1 10.5 %collective-permute-start.53 = (bf16[2,32,1280]{2,1,0:T(8,128)(2,1)}, bf16[2,32,1280]{2,1,0:T(8,128)(2,1)S(1)}, u32[]{:S(2)}, u32[]{:S(2)}) collective-permute-start(bf16[2,32,1280]{2,1,0:T(8,128)(2,1)} %get-tuple-element.294), channel_id=1, source_target_pairs={{0,8},{1,9},{2,10},{3,11},{4,12},{5,13},{6,14},{7,15},{8,0},{9,1},... | collective-permute-start | bytes 491528 | tf_op jit(solution)/shard_map/ppermute | solution.py:67
  359.8 11.8 %collective-permute-start.59 = (bf16[40,1280]{1,0:T(8,128)(2,1)S(1)}, bf16[40,1280]{1,0:T(8,128)(2,1)S(1)}, u32[]{:S(2)}, u32[]{:S(2)}) collective-permute-start(bf16[40,1280]{1,0:T(8,128)(2,1)S(1)} %get-tuple-element.330), channel_id=1, source_target_pairs={{0,1},{1,3},{2,5},{3,7},{4,9},{5,11},{6,13},{7,15},{8,17},{9,19},{... | collective-permute-start | bytes 307208 | tf_op jit(solution)/shard_map/ppermute | solution.py:67
  359.9 11.7 %collective-permute-start.58 = (bf16[40,1280]{1,0:T(8,128)(2,1)S(1)}, bf16[40,1280]{1,0:T(8,128)(2,1)S(1)}, u32[]{:S(2)}, u32[]{:S(2)}) collective-permute-start(bf16[40,1280]{1,0:T(8,128)(2,1)S(1)} %get-tuple-element.329), channel_id=1, source_target_pairs={{0,0},{1,2},{2,4},{3,6},{4,8},{5,10},{6,12},{7,14},{8,16},{9,18},{... | collective-permute-start | bytes 307208 | tf_op jit(solution)/shard_map/ppermute | solution.py:67
  366.1 8.0 %collective-permute-start.54 = (bf16[1,48,1280]{2,1,0:T(8,128)(2,1)S(1)}, bf16[1,48,1280]{2,1,0:T(8,128)(2,1)S(1)}, u32[]{:S(2)}, u32[]{:S(2)}) collective-permute-start(bf16[1,48,1280]{2,1,0:T(8,128)(2,1)S(1)} %get-tuple-element.300), channel_id=1, source_target_pairs={{0,2},{1,3},{2,0},{3,1},{4,6},{5,7},{6,4},{7,5},{8,10},{9,11},{10,... | collective-permute-start | bytes 368648 | tf_op jit(solution)/shard_map/ppermute | solution.py:67
  368.2 5.9 %collective-permute-start.55 = (bf16[1,48,1280]{2,1,0:T(8,128)(2,1)S(1)}, bf16[1,48,1280]{2,1,0:T(8,128)(2,1)S(1)}, u32[]{:S(2)}, u32[]{:S(2)}) collective-permute-start(bf16[1,48,1280]{2,1,0:T(8,128)(2,1)S(1)} %get-tuple-element.301), channel_id=1, source_target_pairs={{0,8},{1,9},{2,10},{3,11},{4,12},{5,13},{6,14},{7,15},{8,0},{9,1},... | collective-permute-start | bytes 368648 | tf_op jit(solution)/shard_map/ppermute | solution.py:67
  377.7 9.9 %collective-permute-start.57 = (bf16[64,1280]{1,0:T(8,128)(2,1)S(1)}, bf16[64,1280]{1,0:T(8,128)(2,1)S(1)}, u32[]{:S(2)}, u32[]{:S(2)}) collective-permute-start(bf16[64,1280]{1,0:T(8,128)(2,1)S(1)} %dynamic-slice_bitcast_fusion.2), channel_id=1, source_target_pairs={{0,16},{1,17},{2,18},{3,19},{4,20},{5,21},{6,22},{7,23},{8,24},{9,... | collective-permute-start | bytes 491528 | tf_op jit(solution)/shard_map/ppermute | solution.py:67
  (55 other events, 527.7 us)
Sparse Core Ops, SparseCore 0:
  73.2 46.3 all-gather.6
  121.2 47.7 all-gather.8
  205.0 74.0 reduce-scatter.1
  280.5 58.4 all-gather.10

commit v2 on v1

--- a/solution.py
+++ b/solution.py
@@ -913,7 +913,7 @@
             jax.ShapeDtypeStruct((steps, 1, rows), exact),
         ],
         scratch_shapes=[pltpu.VMEM((lanes, keys), low)],
-        compiler_params=params(10 * keys // 1024),
+        compiler_params=params((20 * rows * keys >> 20) + (2 * keys >> 10)),
         cost_estimate=small_cost,
         name="attend",
     )(q, k, v)
@@ -981,7 +981,7 @@
             pltpu.VMEM((keys, lanes), exact),
             pltpu.VMEM((keys, lanes), exact),
         ],
-        compiler_params=params(14 * keys // 1024),
+        compiler_params=params((24 * rows * keys >> 20) + (6 * keys >> 10)),
         cost_estimate=small_cost,
         name="attend_back",
     )(q, k, v, do, far_off(e), inverse)
@@ -1015,7 +1015,7 @@
     tokens = at.half * own
     clips = clip_lengths.shape[1]
     chunk = width // at.block
-    step_rows = 256
+    step_rows = 512 if at.blocks == 1 else 256
 
     vectors = [at.to_block(v) for v in (ln1_gain, ln1_bias, b_query, b_value, b_out, ln2_gain, ln2_bias, b_fc2)]
     ff_bias = at.to_block(b_fc1)

time: 397 us -> 409 us (1.030); the launches traced: 395 us -> 401 us
  starting transfers between devices: 83.3 us -> 90.1 us
    all_to_all x4, starting transfers between devices: 14.6 us -> 23.1 us  [exchange_block(): lax.all_to_all(value, 'dev', 0, 0, tiled=True, axis_index_groups=self.whole)]
    all_to_all x4, waiting for transfers between devices: 8.46 us -> 14.8 us  [exchange_block(): lax.all_to_all(value, 'dev', 0, 0, tiled=True, axis_index_groups=self.whole)]
  transfers between devices with their start and end apart: 69 -> 69, of which waited for: 31 -> 30; matrix products, arithmetic and copies ran while one was open for 5% -> 5% of each run, Pallas kernels for 29% -> 27%
where the time goes in v2:
time: 409 us; the launch traced here: 401 us
  Pallas kernels  126 us (31%)
  waiting for transfers between devices  115 us (28%)
  starting transfers between devices  90.1 us (22%)
  local copies, waits for them, and re-layouts  28.7 us (7%)
  between operations  14.8 us (4%)
  blocking collectives  14.6 us (4%)
  other arithmetic  12.8 us (3%)
    ppermute x60, waiting for transfers between devices, send(): return lax.ppermute(value, 'dev', pairs)  95.8 us
    ppermute x60, starting transfers between devices, send(): return lax.ppermute(value, 'dev', pairs)  63 us
    all_to_all x4, starting transfers between devices, exchange_block(): lax.all_to_all(value, 'dev', 0, 0, tiled=True, axis_index_groups=self.whole)  23.1 us
    pallas_call x2, Pallas kernels, feed(): pl.pallas_call(feed_kernel, grid_spec=pltpu.PrefetchScalarGridSpec(num_sc...  21.6 us
    unnamed x101, local copies, waits for them, and re-layouts  18.3 us
    all_to_all x4, waiting for transfers between devices, exchange_block(): lax.all_to_all(value, 'dev', 0, 0, tiled=True, axis_index_groups=self.whole)  14.8 us
    all_to_all x1, blocking collectives, exchange_half(): lax.all_to_all(value, 'dev', 0, 0, tiled=True, axis_index_groups=self.hal...  14.6 us
    pallas_call x1, Pallas kernels, attend_back(): pl.pallas_call(functools.partial(attend_back_kernel, hd, scale, span), gr...  14.5 us
  transfers between devices with their start and end apart: 69, of which 30 were waited for; matrix products, arithmetic and copies ran while one was open for 5% of the time, Pallas kernels for 27%

profile of v2, /device:TPU:0, one launch (start us, length us, event | category | flops | bytes accessed | tf_op | source)
XLA Modules:
  0.0 401.5 jit_solution(16190297046653835247)
XLA Ops:
  10.5 4.1 %collective-permute-start = (bf16[72,1280]{1,0:T(8,128)(2,1)S(1)}, bf16[72,1280]{1,0:T(8,128)(2,1)S(1)}, u32[]{:S(2)}, u32[]{:S(2)}) collective-permute-start(bf16[72,1280]{1,0:T(8,128)(2,1)S(1)} %get-tuple-element.167), channel_id=1, source_target_pairs={{0,16},{1,17},{2,18},{3,19},{4,20},{5,21},{6,22},{7,23},{8,24},{9,... | collective-permute-start | bytes 552968 | tf_op jit(solution)/shard_map/ppermute | solution.py:67
  15.5 3.6 deal.1
  20.1 3.1 collective-permute-done.second_ref
  26.7 2.9 collective-permute-start.2
  31.1 2.0 collective-permute-done.2.refs_3_
  33.1 6.1 %collective-permute-done.3 = bf16[104,1280]{1,0:T(8,128)(2,1)S(1)} collective-permute-done((bf16[104,1280]{1,0:T(8,128)(2,1)S(1)}, bf16[104,1280]{1,0:T(8,128)(2,1)S(1)}, u32[]{:S(2)}, u32[]{:S(2)}) %collective-permute-start.3) | collective-permute-done | bytes 266272 | tf_op jit(solution)/shard_map/ppermute | solution.py:67
  43.4 1.7 collective-permute-start.7
  45.2 8.5 %collective-permute-done.7 = bf16[80,1280]{1,0:T(8,128)(2,1)S(1)} collective-permute-done((bf16[80,1280]{1,0:T(8,128)(2,1)S(1)}, bf16[80,1280]{1,0:T(8,128)(2,1)S(1)}, u32[]{:S(2)}, u32[]{:S(2)}) %collective-permute-start.7) | collective-permute-done | bytes 204832 | tf_op jit(solution)/shard_map/ppermute | solution.py:67
  53.6 2.2 collective-permute-done.9.refs_5_
  59.5 1.8 collective-permute-start.11
  61.9 9.5 %collective-permute-done.11 = bf16[80,1280]{1,0:T(8,128)(2,1)} collective-permute-done((bf16[80,1280]{1,0:T(8,128)(2,1)}, bf16[80,1280]{1,0:T(8,128)(2,1)}, u32[]{:S(2)}, u32[]{:S(2)}) %collective-permute-start.11) | collective-permute-done | bytes 204832 | tf_op jit(solution)/shard_map/ppermute | solution.py:67
  75.0 3.6 all-to-all-start
  84.1 6.9 %norm.2 = (bf16[8,2,128,1280]{3,2,1,0:T(8,128)(2,1)}, f32[8,1280]{1,0:T(8,128)S(1)}) custom-call(s32[7]{0:T(128)S(1)} %stack.76.place_ref, bf16[4,48,1280]{2,1,0:T(8,128)(2,1)} %get-tuple-element.192.refs_0_, bf16[4,48,1280]{2,1,0:T(8,128)(2,1)S(1)} %copy-done.27, bf16[4,64,1280]{2,1,0:T(8,128)(2,1)S(1)} %get-tuple-element.194.refs_2_, ...), custom_call_target="tpu_custom_call" | custom-call | flops 1024 | bytes 1024 | tf_op jit(solution)/shard_map/norm/pallas_call | solution.py:421
  91.1 3.9 norm.3
  95.0 4.0 all-to-all-done
  99.0 2.6 all-to-all-start.1
  101.9 7.4 %project.1 = (bf16[2048,384]{1,0:T(8,128)(2,1)S(1)}, bf16[1280,384]{1,0:T(8,128)(2,1)}) custom-call(s32[7]{0:T(128)S(1)} %stack.76.place_ref, s32[3]{0:T(128)S(1)} %subtract_bitcast_fusion.ends_ref, bf16[2048,1280]{1,0:T(8,128)(2,1)} %bitcast.98, bf16[1280,240]{1,0:T(8,128)(2,1)S(1)} %bitcast.89, f32[8,1280]{1,0:T(8,128)S(1)} %get-tuple-element.204.table_ref.refs_8_), custom_call_target="tpu_custom_call" | custom-call | flops 1024 | bytes 1024 | tf_op jit(solution)/shard_map/project/pallas_call | solution.py:477
  109.2 9.9 %attend.1 = (bf16[16,80,128]{2,1,0:T(8,128)(2,1)}, bf16[4,2048,512]{2,1,0:T(8,128)(2,1)}, f32[4,1,512]{2,1,0:T(1,128)S(1)}) custom-call(bf16[2048,384]{1,0:T(8,128)(2,1)S(1)} %get-tuple-element.205.q_ref.k_ref.v_ref, bf16[2048,384]{1,0:T(8,128)(2,1)S(1)} %get-tuple-element.205.q_ref.k_ref.v_ref, bf16[2048,384]{1,0:T(8,128)(2,1)S(1)} %get-tuple-element.205.q_ref.k_ref.v_ref), custom_call_target="tpu_custom_call" | custom-call | flops 1024 | bytes 1024 | tf_op jit(solution)/shard_map/attend/pallas_call | solution.py:897
  119.1 4.9 %all-to-all-done.1.in_ref = bf16[32,8,1600]{2,1,0:T(8,128)(2,1)S(1)} async-done(((bf16[32,8,1600]{2,1,0:T(8,128)(2,1)}), bf16[32,8,1600]{2,1,0:T(8,128)(2,1)S(1)}, u32[]{:S(2)}, u32[]{:S(2)}) %all-to-all-start.1) | async-done | bytes 819232 | tf_op jit(solution)/shard_map/all_to_all | solution.py:106
  124.0 3.5 all-to-all-start.2
  127.9 4.1 %copy.39 = bf16[16,2,40,1280]{3,2,0,1:T(8,128)(2,1)} copy(bf16[16,2,40,1280]{3,2,1,0:T(8,128)(2,1)} %bitcast.104) | data formatting | bytes 6553600 | tf_op jit(solution)/shard_map/reshape | solution.py:1044
  132.0 4.0 %all-to-all-done.2.o_ref = bf16[16,80,128]{2,1,0:T(8,128)(2,1)S(1)} async-done(((bf16[16,80,128]{2,1,0:T(8,128)(2,1)}), bf16[16,80,128]{2,1,0:T(8,128)(2,1)S(1)}, u32[]{:S(2)}, u32[]{:S(2)}) %all-to-all-start.2) | async-done | bytes 327712 | tf_op jit(solution)/shard_map/all_to_all | solution.py:103
  136.0 2.9 join.1
  143.7 5.3 %collective-permute-done.22.refs_5_ = bf16[1,32,1280]{2,1,0:T(8,128)(2,1)S(1)} collective-permute-done((bf16[1,32,1280]{2,1,0:T(8,128)(2,1)S(1)}, bf16[1,32,1280]{2,1,0:T(8,128)(2,1)S(1)}, u32[]{:S(2)}, u32[]{:S(2)}) %collective-permute-start.22) | collective-permute-done | bytes 81952 | tf_op jit(solution)/shard_map/ppermute | solution.py:67
  150.0 2.6 collective-permute-start.24
  153.8 8.6 %collective-permute-done.25.refs_5_ = bf16[2,32,1280]{2,1,0:T(8,128)(2,1)S(1)} collective-permute-done((bf16[2,32,1280]{2,1,0:T(8,128)(2,1)S(1)}, bf16[2,32,1280]{2,1,0:T(8,128)(2,1)S(1)}, u32[]{:S(2)}, u32[]{:S(2)}) %collective-permute-start.25) | collective-permute-done | bytes 163872 | tf_op jit(solution)/shard_map/ppermute | solution.py:67
  165.1 1.9 collective-permute-start.26
  171.6 5.2 %collective-permute-done.28.refs_5_ = bf16[4,32,1280]{2,1,0:T(8,128)(2,1)} collective-permute-done((bf16[4,32,1280]{2,1,0:T(8,128)(2,1)S(1)}, bf16[4,32,1280]{2,1,0:T(8,128)(2,1)}, u32[]{:S(2)}, u32[]{:S(2)}) %collective-permute-start.28) | collective-permute-done | bytes 327712 | tf_op jit(solution)/shard_map/ppermute | solution.py:67
  183.2 10.8 %feed.2 = (bf16[8,2,128,320]{3,2,1,0:T(8,128)(2,1)}, bf16[8,2,128,320]{3,2,1,0:T(8,128)(2,1)}, bf16[8,2,128,1280]{3,2,1,0:T(8,128)(2,1)}, bf16[8,128,1280]{2,1,0:T(8,128)(2,1)}, f32[1,320]{1,0:T(1,128)S(1)}) custom-call(s32[7]{0:T(128)S(1)} %stack.76.place_ref, bf16[4,48,1280]{2,1,0:T(8,128)(2,1)} %get-tuple-element.218.refs_0_, ...), custom_call_target="tpu_custom_call" | custom-call | flops 1024 | bytes 1024 | tf_op jit(solution)/shard_map/feed/pallas_call | solution.py:671
  194.1 10.8 %feed.3 = (bf16[8,2,128,320]{3,2,1,0:T(8,128)(2,1)}, bf16[8,2,128,320]{3,2,1,0:T(8,128)(2,1)}, bf16[8,2,128,1280]{3,2,1,0:T(8,128)(2,1)}, bf16[8,128,1280]{2,1,0:T(8,128)(2,1)}, f32[1,320]{1,0:T(1,128)S(1)}) custom-call(s32[7]{0:T(128)S(1)} %stack.76.place_ref, ...), custom_call_target="tpu_custom_call", output_to_operand_aliasing={{0}: (11, {}), {1}: (12, {}), {2}: (13, {})} | custom-call | flops 1024 | bytes 1024 | tf_op jit(solution)/shard_map/feed/pallas_call | solution.py:671
  205.5 4.7 %collective-permute-done.35.refs_1_ = bf16[8,128,1280]{2,1,0:T(8,128)(2,1)S(1)} collective-permute-done((bf16[8,128,1280]{2,1,0:T(8,128)(2,1)}, bf16[8,128,1280]{2,1,0:T(8,128)(2,1)S(1)}, u32[]{:S(2)}, u32[]{:S(2)}) %collective-permute-start.35) | collective-permute-done | bytes 2621472 | tf_op jit(solution)/shard_map/ppermute | solution.py:67
  210.3 1.7 copy-done.13
  212.0 1.8 split_terms.6
  216.1 5.4 %fc2_grad.1 = bf16[2,160,1280]{2,1,0:T(8,128)(2,1)S(1)} custom-call(bf16[8,2,128,320]{3,2,1,0:T(8,128)(2,1)} %get-tuple-element.234.hid_ref, bf16[8,2,128,1280]{3,2,1,0:T(8,128)(2,1)} %bitcast.97), custom_call_target="tpu_custom_call" | custom-call | flops 1024 | bytes 1024 | tf_op jit(solution)/shard_map/fc2_grad/pallas_call | solution.py:547
  221.6 10.8 %collective-permute-done.36.refs_3_ = bf16[4,48,1280]{2,1,0:T(8,128)(2,1)S(1)} collective-permute-done((bf16[4,48,1280]{2,1,0:T(8,128)(2,1)S(1)}, bf16[4,48,1280]{2,1,0:T(8,128)(2,1)S(1)}, u32[]{:S(2)}, u32[]{:S(2)}) %collective-permute-start.36) | collective-permute-done | bytes 491552 | tf_op jit(solution)/shard_map/ppermute | solution.py:67
  239.7 8.6 %fc1_grad.1 = bf16[32,8,1600]{2,1,0:T(8,128)(2,1)} custom-call(s32[7]{0:T(128)S(1)} %stack.76.place_ref, bf16[4,48,1280]{2,1,0:T(8,128)(2,1)} %get-tuple-element.218.refs_0_, bf16[4,48,1280]{2,1,0:T(8,128)(2,1)} %get-tuple-element.219.refs_1_, bf16[4,32,1280]{2,1,0:T(8,128)(2,1)S(1)} %copy-done.20, bf16[4,48,1280]{2,1,0:T(8,128)(2,1)} %collective-permute-done.26.refs_3_, ...), custom_call_target="tpu_custom_call" | custom-call | flops 1024 | bytes 1024 | tf_op jit(solution)/shard_map/fc1_grad/pallas_call | solution.py:590
  248.4 4.2 %collective-permute-done.41.refs_5_ = bf16[2,32,1280]{2,1,0:T(8,128)(2,1)S(1)} collective-permute-done((bf16[2,32,1280]{2,1,0:T(8,128)(2,1)S(1)}, bf16[2,32,1280]{2,1,0:T(8,128)(2,1)S(1)}, u32[]{:S(2)}, u32[]{:S(2)}) %collective-permute-start.41) | collective-permute-done | bytes 163872 | tf_op jit(solution)/shard_map/ppermute | solution.py:67
  254.0 2.5 collective-permute-start.43
  256.5 2.8 collective-permute-start.44
  259.3 2.6 collective-permute-done.44.refs_5_
  262.6 3.9 second_back.1
  267.4 14.6 %all_to_all.30.do_ref = bf16[16,80,128]{2,1,0:T(8,128)(2,1)} all-to-all(bf16[16,80,128]{2,1,0:T(8,128)(2,1)S(1)} %get-tuple-element.260), channel_id=1, replica_groups={{0,1,2,3,4,5,6,7,8,9,10,11,12,13,14,15},{16,17,18,19,20,21,22,23,24,25,..., dimensions={0} | all-to-all | bytes 655360 | tf_op jit(solution)/shard_map/all_to_all | solution.py:103
  282.0 13.1 %all-to-all-start.4 = ((bf16[32,8,1600]{2,1,0:T(8,128)(2,1)}), bf16[32,8,1600]{2,1,0:T(8,128)(2,1)S(1)}, u32[]{:S(2)}, u32[]{:S(2)}) async-start(bf16[32,8,1600]{2,1,0:T(8,128)(2,1)} %fc1_grad.1), calls=%async_computation.5 | async-start | bytes 1703936 | tf_op jit(solution)/shard_map/all_to_all | solution.py:106
  296.1 14.5 %attend_back.1 = (bf16[2048,384]{1,0:T(8,128)(2,1)}, f32[8,384]{1,0:T(8,128)S(1)}) custom-call(bf16[2048,384]{1,0:T(8,128)(2,1)S(1)} %get-tuple-element.205.q_ref.k_ref.v_ref, bf16[2048,384]{1,0:T(8,128)(2,1)S(1)} %get-tuple-element.205.q_ref.k_ref.v_ref, bf16[2048,384]{1,0:T(8,128)(2,1)S(1)} %get-tuple-element.205.q_ref.k_ref.v_ref, ...), custom_call_target="tpu_custom_call" | custom-call | flops 1024 | bytes 1024 | tf_op jit(solution)/shard_map/attend_back/pallas_call | solution.py:966
  312.0 2.4 terms.3
  316.0 5.8 %all-to-all-done.4.in_ref = bf16[32,8,1600]{2,1,0:T(8,128)(2,1)S(1)} async-done(((bf16[32,8,1600]{2,1,0:T(8,128)(2,1)}), bf16[32,8,1600]{2,1,0:T(8,128)(2,1)S(1)}, u32[]{:S(2)}, u32[]{:S(2)}) %all-to-all-start.4) | async-done | bytes 819232 | tf_op jit(solution)/shard_map/all_to_all | solution.py:106
  321.8 2.4 terms.2.refs_0_
  324.3 2.7 collective-permute-done.46.refs_1_
  327.0 1.8 split_terms.9
  329.9 1.8 collective-permute-start.48
  332.4 8.4 %head_grad.1 = bf16[32,40,256]{2,1,0:T(8,128)(2,1)} custom-call(s32[7]{0:T(128)S(1)} %stack.76.place_ref, bf16[2048,1280]{1,0:T(8,128)(2,1)} %bitcast.99, bf16[2048,384]{1,0:T(8,128)(2,1)S(1)} %copy-done.3, bf16[1280,240]{1,0:T(8,128)(2,1)S(1)} %bitcast.90, f32[8,1280]{1,0:T(8,128)S(1)} %get-tuple-element.204.table_ref.refs_8_, ...), custom_call_target="tpu_custom_call" | custom-call | flops 1024 | bytes 1024 | tf_op jit(solution)/shard_map/head_grad/pallas_call | solution.py:817
  341.6 6.8 %collective-permute-done.48.refs_3_ = bf16[4,48,1280]{2,1,0:T(8,128)(2,1)S(1)} collective-permute-done((bf16[4,48,1280]{2,1,0:T(8,128)(2,1)S(1)}, bf16[4,48,1280]{2,1,0:T(8,128)(2,1)S(1)}, u32[]{:S(2)}, u32[]{:S(2)}) %collective-permute-start.48) | collective-permute-done | bytes 491552 | tf_op jit(solution)/shard_map/ppermute | solution.py:67
  348.4 1.9 split_terms.10
  351.8 3.7 all-to-all-start.5
  357.1 1.8 collective-permute-start.51
  361.9 4.2 %output_grad.1 = bf16[2,40,1280]{2,1,0:T(8,128)(2,1)S(1)} custom-call(bf16[16,80,128]{2,1,0:T(8,128)(2,1)} %get-tuple-element.290.o_ref, bf16[16,128,1280]{2,1,0:T(8,128)(2,1)} %bitcast.103), custom_call_target="tpu_custom_call" | custom-call | flops 1024 | bytes 1024 | tf_op jit(solution)/shard_map/output_grad/pallas_call | solution.py:624
  367.8 2.1 collective-permute-done.51.refs_3_
  372.3 2.1 collective-permute-start.54
  375.9 1.9 collective-permute-start.56
  378.6 1.8 collective-permute-done.56.refs_5_
  382.2 1.8 first_back.1
  384.0 2.8 collective-permute-start.57
  387.9 1.9 collect_hidden.1
  390.5 2.1 convert_add_fusion
  (249 shorter events, 86.4 us)
Async XLA Ops:
  7.2 120.7 %all-gather.7.cloned.1.call-start = ((), (), s32[]{:S(2)}) async-start(), calls=%async_computation.8 | async-start | bytes 3481600 | tf_op jit(solution)/shard_map/all_gather | solution.py:100
  10.5 12.7 %collective-permute-start = (bf16[72,1280]{1,0:T(8,128)(2,1)S(1)}, bf16[72,1280]{1,0:T(8,128)(2,1)S(1)}, u32[]{:S(2)}, u32[]{:S(2)}) collective-permute-start(bf16[72,1280]{1,0:T(8,128)(2,1)S(1)} %get-tuple-element.167), channel_id=1, source_target_pairs={{0,16},{1,17},{2,18},{3,19},{4,20},{5,21},{6,22},{7,23},{8,24},{9,... | collective-permute-start | bytes 552968 | tf_op jit(solution)/shard_map/ppermute | solution.py:67
  23.8 15.4 %collective-permute-start.3 = (bf16[104,1280]{1,0:T(8,128)(2,1)S(1)}, bf16[104,1280]{1,0:T(8,128)(2,1)S(1)}, u32[]{:S(2)}, u32[]{:S(2)}) collective-permute-start(bf16[104,1280]{1,0:T(8,128)(2,1)S(1)} %pad_maximum_fusion.2), channel_id=1, source_target_pairs={{0,16},{1,17},{2,18},{3,19},{4,20},{5,21},{6,22},{7,23},{8,24},{9,... | collective-permute-start | bytes 798728 | tf_op jit(solution)/shard_map/ppermute | solution.py:67
  25.1 14.2 %collective-permute-start.5 = (bf16[1,64,1280]{2,1,0:T(8,128)(2,1)S(1)}, bf16[1,64,1280]{2,1,0:T(8,128)(2,1)S(1)}, u32[]{:S(2)}, u32[]{:S(2)}) collective-permute-start(bf16[1,64,1280]{2,1,0:T(8,128)(2,1)S(1)} %pad_maximum_fusion.4.refs_2_), channel_id=1, source_target_pairs={{0,2},{1,3},{2,0},{3,1},{4,6},{5,7},{6,4},{7,5},{8,10},{9,11},{10,... | collective-permute-start | bytes 491528 | tf_op jit(solution)/shard_map/ppermute | solution.py:67
  26.7 6.4 %collective-permute-start.2 = (bf16[1,48,1280]{2,1,0:T(8,128)(2,1)S(1)}, bf16[1,48,1280]{2,1,0:T(8,128)(2,1)S(1)}, u32[]{:S(2)}, u32[]{:S(2)}) collective-permute-start(bf16[1,48,1280]{2,1,0:T(8,128)(2,1)S(1)} %get-tuple-element.172.refs_0_), channel_id=1, source_target_pairs={{0,8},{1,9},{2,10},{3,11},{4,12},{5,13},{6,14},{7,15},{8,0},{9,1},... | collective-permute-start | bytes 368648 | tf_op jit(solution)/shard_map/ppermute | solution.py:67
  29.6 9.7 %collective-permute-start.4 = (bf16[1,48,1280]{2,1,0:T(8,128)(2,1)S(1)}, bf16[1,48,1280]{2,1,0:T(8,128)(2,1)S(1)}, u32[]{:S(2)}, u32[]{:S(2)}) collective-permute-start(bf16[1,48,1280]{2,1,0:T(8,128)(2,1)S(1)} %get-tuple-element.173.refs_1_), channel_id=1, source_target_pairs={{0,4},{1,5},{2,6},{3,7},{4,0},{5,1},{6,2},{7,3},{8,12},{9,13},{10,... | collective-permute-start | bytes 368648 | tf_op jit(solution)/shard_map/ppermute | solution.py:67
  39.6 14.0 %collective-permute-start.6 = (bf16[2,48,1280]{2,1,0:T(8,128)(2,1)S(1)}, bf16[2,48,1280]{2,1,0:T(8,128)(2,1)S(1)}, u32[]{:S(2)}, u32[]{:S(2)}) collective-permute-start(bf16[2,48,1280]{2,1,0:T(8,128)(2,1)S(1)} %get-tuple-element.179.refs_0_), channel_id=1, source_target_pairs={{0,4},{1,5},{2,6},{3,7},{4,0},{5,1},{6,2},{7,3},{8,12},{9,13},{10,... | collective-permute-start | bytes 737288 | tf_op jit(solution)/shard_map/ppermute | solution.py:67
  41.2 12.4 %collective-permute-start.8 = (bf16[2,48,1280]{2,1,0:T(8,128)(2,1)S(1)}, bf16[2,48,1280]{2,1,0:T(8,128)(2,1)S(1)}, u32[]{:S(2)}, u32[]{:S(2)}) collective-permute-start(bf16[2,48,1280]{2,1,0:T(8,128)(2,1)S(1)} %get-tuple-element.180.refs_1_), channel_id=1, source_target_pairs={{0,2},{1,3},{2,0},{3,1},{4,6},{5,7},{6,4},{7,5},{8,10},{9,11},{10,... | collective-permute-start | bytes 737288 | tf_op jit(solution)/shard_map/ppermute | solution.py:67
  42.7 13.1 %collective-permute-start.9 = (bf16[2,64,1280]{2,1,0:T(8,128)(2,1)S(1)}, bf16[2,64,1280]{2,1,0:T(8,128)(2,1)S(1)}, u32[]{:S(2)}, u32[]{:S(2)}) collective-permute-start(bf16[2,64,1280]{2,1,0:T(8,128)(2,1)S(1)} %get-tuple-element.181.refs_2_), channel_id=1, source_target_pairs={{0,8},{1,9},{2,10},{3,11},{4,12},{5,13},{6,14},{7,15},{8,0},{9,1},... | collective-permute-start | bytes 983048 | tf_op jit(solution)/shard_map/ppermute | solution.py:67
  43.4 10.2 %collective-permute-start.7 = (bf16[80,1280]{1,0:T(8,128)(2,1)S(1)}, bf16[80,1280]{1,0:T(8,128)(2,1)S(1)}, u32[]{:S(2)}, u32[]{:S(2)}) collective-permute-start(bf16[80,1280]{1,0:T(8,128)(2,1)S(1)} %get-tuple-element.182), channel_id=1, source_target_pairs={{0,16},{1,17},{2,18},{3,19},{4,20},{5,21},{6,22},{7,23},{8,24},{9,... | collective-permute-start | bytes 614408 | tf_op jit(solution)/shard_map/ppermute | solution.py:67
  56.9 14.5 %collective-permute-start.10 = (bf16[4,48,1280]{2,1,0:T(8,128)(2,1)}, bf16[4,48,1280]{2,1,0:T(8,128)(2,1)S(1)}, u32[]{:S(2)}, u32[]{:S(2)}) collective-permute-start(bf16[4,48,1280]{2,1,0:T(8,128)(2,1)} %get-tuple-element.192.refs_0_), channel_id=1, source_target_pairs={{0,2},{1,3},{2,0},{3,1},{4,6},{5,7},{6,4},{7,5},{8,10},{9,11},{10,... | collective-permute-start | bytes 1474568 | tf_op jit(solution)/shard_map/ppermute | solution.py:67
  57.4 15.6 %collective-permute-start.12 = (bf16[4,48,1280]{2,1,0:T(8,128)(2,1)S(1)}, bf16[4,48,1280]{2,1,0:T(8,128)(2,1)S(1)}, u32[]{:S(2)}, u32[]{:S(2)}) collective-permute-start(bf16[4,48,1280]{2,1,0:T(8,128)(2,1)S(1)} %get-tuple-element.193.refs_1_), channel_id=1, source_target_pairs={{0,8},{1,9},{2,10},{3,11},{4,12},{5,13},{6,14},{7,15},{8,0},{9,1},... | collective-permute-start | bytes 1474568 | tf_op jit(solution)/shard_map/ppermute | solution.py:67
  57.9 15.1 %collective-permute-start.13 = (bf16[4,64,1280]{2,1,0:T(8,128)(2,1)S(1)}, bf16[4,64,1280]{2,1,0:T(8,128)(2,1)S(1)}, u32[]{:S(2)}, u32[]{:S(2)}) collective-permute-start(bf16[4,64,1280]{2,1,0:T(8,128)(2,1)S(1)} %get-tuple-element.194.refs_2_), channel_id=1, source_target_pairs={{0,4},{1,5},{2,6},{3,7},{4,0},{5,1},{6,2},{7,3},{8,12},{9,13},{10,... | collective-permute-start | bytes 1966088 | tf_op jit(solution)/shard_map/ppermute | solution.py:67
  59.5 11.9 %collective-permute-start.11 = (bf16[80,1280]{1,0:T(8,128)(2,1)}, bf16[80,1280]{1,0:T(8,128)(2,1)}, u32[]{:S(2)}, u32[]{:S(2)}) collective-permute-start(bf16[80,1280]{1,0:T(8,128)(2,1)} %get-tuple-element.187), channel_id=1, source_target_pairs={{0,16},{1,17},{2,18},{3,19},{4,20},{5,21},{6,22},{7,23},{8,24},{9,... | collective-permute-start | bytes 614408 | tf_op jit(solution)/shard_map/ppermute | solution.py:67
  73.0 109.2 %all-gather.9.cloned.1.call-start = ((), (), s32[]{:S(2)}) async-start(), calls=%async_computation.9 | async-start | bytes 5570560 | tf_op jit(solution)/shard_map/all_gather | solution.py:100
  75.0 24.0 %all-to-all-start = ((bf16[32,40,240]{2,1,0:T(8,128)(2,1)}), bf16[32,40,240]{2,1,0:T(8,128)(2,1)S(1)}, u32[]{:S(2)}, u32[]{:S(2)}) async-start(bf16[32,40,240]{2,1,0:T(8,128)(2,1)} %get-tuple-element.191), calls=%async_computation | async-start | bytes 1310720 | tf_op jit(solution)/shard_map/all_to_all | solution.py:106
  79.0 12.1 %collective-permute-start.16 = (bf16[4,64,1280]{2,1,0:T(8,128)(2,1)S(1)}, bf16[4,64,1280]{2,1,0:T(8,128)(2,1)S(1)}, u32[]{:S(2)}, u32[]{:S(2)}) collective-permute-start(bf16[4,64,1280]{2,1,0:T(8,128)(2,1)S(1)} %get-tuple-element.194.refs_2_), channel_id=1, source_target_pairs={{0,1},{1,0},{2,3},{3,2},{4,5},{5,4},{6,7},{7,6},{8,9},{9,8},{10,11... | collective-permute-start | bytes 1966088 | tf_op jit(solution)/shard_map/ppermute | solution.py:67
  79.2 11.9 %collective-permute-start.19 = (bf16[4,64,1280]{2,1,0:T(8,128)(2,1)S(1)}, bf16[4,64,1280]{2,1,0:T(8,128)(2,1)S(1)}, u32[]{:S(2)}, u32[]{:S(2)}) collective-permute-start(bf16[4,64,1280]{2,1,0:T(8,128)(2,1)S(1)} %collective-permute-done.13.refs_5_), channel_id=1, source_target_pairs={{0,1},{1,0},{2,3},{3,2},{4,5},{5,4},{6,7},{7,6},{8,9},{9,8},{10,11... | collective-permute-start | bytes 1966088 | tf_op jit(solution)/shard_map/ppermute | solution.py:67
  79.5 11.6 %collective-permute-start.15 = (bf16[4,48,1280]{2,1,0:T(8,128)(2,1)}, bf16[4,48,1280]{2,1,0:T(8,128)(2,1)S(1)}, u32[]{:S(2)}, u32[]{:S(2)}) collective-permute-start(bf16[4,48,1280]{2,1,0:T(8,128)(2,1)} %copy-done.26), channel_id=1, source_target_pairs={{0,1},{1,0},{2,3},{3,2},{4,5},{5,4},{6,7},{7,6},{8,9},{9,8},{10,11... | collective-permute-start | bytes 1474568 | tf_op jit(solution)/shard_map/ppermute | solution.py:67
  79.7 11.3 %collective-permute-start.17 = (bf16[4,48,1280]{2,1,0:T(8,128)(2,1)}, bf16[4,48,1280]{2,1,0:T(8,128)(2,1)S(1)}, u32[]{:S(2)}, u32[]{:S(2)}) collective-permute-start(bf16[4,48,1280]{2,1,0:T(8,128)(2,1)} %copy-done.28), channel_id=1, source_target_pairs={{0,1},{1,0},{2,3},{3,2},{4,5},{5,4},{6,7},{7,6},{8,9},{9,8},{10,11... | collective-permute-start | bytes 1474568 | tf_op jit(solution)/shard_map/ppermute | solution.py:67
  80.8 10.3 %collective-permute-start.18 = (bf16[4,48,1280]{2,1,0:T(8,128)(2,1)}, bf16[4,48,1280]{2,1,0:T(8,128)(2,1)S(1)}, u32[]{:S(2)}, u32[]{:S(2)}) collective-permute-start(bf16[4,48,1280]{2,1,0:T(8,128)(2,1)} %copy-done.30), channel_id=1, source_target_pairs={{0,1},{1,0},{2,3},{3,2},{4,5},{5,4},{6,7},{7,6},{8,9},{9,8},{10,11... | collective-permute-start | bytes 1474568 | tf_op jit(solution)/shard_map/ppermute | solution.py:67
  99.0 25.0 %all-to-all-start.1 = ((bf16[32,8,1600]{2,1,0:T(8,128)(2,1)}), bf16[32,8,1600]{2,1,0:T(8,128)(2,1)S(1)}, u32[]{:S(2)}, u32[]{:S(2)}) async-start(bf16[32,8,1600]{2,1,0:T(8,128)(2,1)} %get-tuple-element.208), calls=%async_computation.1 | async-start | bytes 1703936 | tf_op jit(solution)/shard_map/all_to_all | solution.py:106
  124.0 12.0 %all-to-all-start.2 = ((bf16[16,80,128]{2,1,0:T(8,128)(2,1)}), bf16[16,80,128]{2,1,0:T(8,128)(2,1)S(1)}, u32[]{:S(2)}, u32[]{:S(2)}) async-start(bf16[16,80,128]{2,1,0:T(8,128)(2,1)} %get-tuple-element.290.o_ref), calls=%async_computation.2 | async-start | bytes 655360 | tf_op jit(solution)/shard_map/all_to_all | solution.py:103
  127.6 183.0 %reduce-scatter.2.cloned.1.call-start = ((), (), s32[]{:S(2)}) async-start(), calls=%async_computation.7 | async-start | bytes 5570560 | tf_op jit(solution)/shard_map/reduce_scatter | solution.py:1086
  139.8 9.2 %collective-permute-start.20 = (bf16[1,48,1280]{2,1,0:T(8,128)(2,1)S(1)}, bf16[1,48,1280]{2,1,0:T(8,128)(2,1)S(1)}, u32[]{:S(2)}, u32[]{:S(2)}) collective-permute-start(bf16[1,48,1280]{2,1,0:T(8,128)(2,1)S(1)} %get-tuple-element.212.refs_0_), channel_id=1, source_target_pairs={{0,8},{1,9},{2,10},{3,11},{4,12},{5,13},{6,14},{7,15},{8,0},{9,1},... | collective-permute-start | bytes 368648 | tf_op jit(solution)/shard_map/ppermute | solution.py:67
  140.9 8.0 %collective-permute-start.21 = (bf16[1,48,1280]{2,1,0:T(8,128)(2,1)S(1)}, bf16[1,48,1280]{2,1,0:T(8,128)(2,1)S(1)}, u32[]{:S(2)}, u32[]{:S(2)}) collective-permute-start(bf16[1,48,1280]{2,1,0:T(8,128)(2,1)S(1)} %get-tuple-element.213.refs_1_), channel_id=1, source_target_pairs={{0,4},{1,5},{2,6},{3,7},{4,0},{5,1},{6,2},{7,3},{8,12},{9,13},{10,... | collective-permute-start | bytes 368648 | tf_op jit(solution)/shard_map/ppermute | solution.py:67
  142.5 6.5 %collective-permute-start.22 = (bf16[1,32,1280]{2,1,0:T(8,128)(2,1)S(1)}, bf16[1,32,1280]{2,1,0:T(8,128)(2,1)S(1)}, u32[]{:S(2)}, u32[]{:S(2)}) collective-permute-start(bf16[1,32,1280]{2,1,0:T(8,128)(2,1)S(1)} %get-tuple-element.214.refs_2_), channel_id=1, source_target_pairs={{0,2},{1,3},{2,0},{3,1},{4,6},{5,7},{6,4},{7,5},{8,10},{9,11},{10,... | collective-permute-start | bytes 245768 | tf_op jit(solution)/shard_map/ppermute | solution.py:67
  149.2 13.2 %collective-permute-start.23 = (bf16[2,48,1280]{2,1,0:T(8,128)(2,1)S(1)}, bf16[2,48,1280]{2,1,0:T(8,128)(2,1)S(1)}, u32[]{:S(2)}, u32[]{:S(2)}) collective-permute-start(bf16[2,48,1280]{2,1,0:T(8,128)(2,1)S(1)} %get-tuple-element.215.refs_0_), channel_id=1, source_target_pairs={{0,4},{1,5},{2,6},{3,7},{4,0},{5,1},{6,2},{7,3},{8,12},{9,13},{10,... | collective-permute-start | bytes 737288 | tf_op jit(solution)/shard_map/ppermute | solution.py:67
  150.0 14.0 %collective-permute-start.24 = (bf16[2,48,1280]{2,1,0:T(8,128)(2,1)S(1)}, bf16[2,48,1280]{2,1,0:T(8,128)(2,1)S(1)}, u32[]{:S(2)}, u32[]{:S(2)}) collective-permute-start(bf16[2,48,1280]{2,1,0:T(8,128)(2,1)S(1)} %get-tuple-element.216.refs_1_), channel_id=1, source_target_pairs={{0,2},{1,3},{2,0},{3,1},{4,6},{5,7},{6,4},{7,5},{8,10},{9,11},{10,... | collective-permute-start | bytes 737288 | tf_op jit(solution)/shard_map/ppermute | solution.py:67
  152.5 9.9 %collective-permute-start.25 = (bf16[2,32,1280]{2,1,0:T(8,128)(2,1)S(1)}, bf16[2,32,1280]{2,1,0:T(8,128)(2,1)S(1)}, u32[]{:S(2)}, u32[]{:S(2)}) collective-permute-start(bf16[2,32,1280]{2,1,0:T(8,128)(2,1)S(1)} %get-tuple-element.217.refs_2_), channel_id=1, source_target_pairs={{0,8},{1,9},{2,10},{3,11},{4,12},{5,13},{6,14},{7,15},{8,0},{9,1},... | collective-permute-start | bytes 491528 | tf_op jit(solution)/shard_map/ppermute | solution.py:67
  165.1 13.1 %collective-permute-start.26 = (bf16[4,48,1280]{2,1,0:T(8,128)(2,1)}, bf16[4,48,1280]{2,1,0:T(8,128)(2,1)}, u32[]{:S(2)}, u32[]{:S(2)}) collective-permute-start(bf16[4,48,1280]{2,1,0:T(8,128)(2,1)} %get-tuple-element.218.refs_0_), channel_id=1, source_target_pairs={{0,2},{1,3},{2,0},{3,1},{4,6},{5,7},{6,4},{7,5},{8,10},{9,11},{10,... | collective-permute-start | bytes 1474568 | tf_op jit(solution)/shard_map/ppermute | solution.py:67
  167.1 12.6 %collective-permute-start.27 = (bf16[4,48,1280]{2,1,0:T(8,128)(2,1)}, bf16[4,48,1280]{2,1,0:T(8,128)(2,1)}, u32[]{:S(2)}, u32[]{:S(2)}) collective-permute-start(bf16[4,48,1280]{2,1,0:T(8,128)(2,1)} %get-tuple-element.219.refs_1_), channel_id=1, source_target_pairs={{0,8},{1,9},{2,10},{3,11},{4,12},{5,13},{6,14},{7,15},{8,0},{9,1},... | collective-permute-start | bytes 1474568 | tf_op jit(solution)/shard_map/ppermute | solution.py:67
  168.3 8.4 %collective-permute-start.28 = (bf16[4,32,1280]{2,1,0:T(8,128)(2,1)S(1)}, bf16[4,32,1280]{2,1,0:T(8,128)(2,1)}, u32[]{:S(2)}, u32[]{:S(2)}) collective-permute-start(bf16[4,32,1280]{2,1,0:T(8,128)(2,1)S(1)} %get-tuple-element.220.refs_2_), channel_id=1, source_target_pairs={{0,4},{1,5},{2,6},{3,7},{4,0},{5,1},{6,2},{7,3},{8,12},{9,13},{10,... | collective-permute-start | bytes 983048 | tf_op jit(solution)/shard_map/ppermute | solution.py:67
  169.1 7.7 %collective-permute-start.31 = (bf16[4,32,1280]{2,1,0:T(8,128)(2,1)S(1)}, bf16[4,32,1280]{2,1,0:T(8,128)(2,1)S(1)}, u32[]{:S(2)}, u32[]{:S(2)}) collective-permute-start(bf16[4,32,1280]{2,1,0:T(8,128)(2,1)S(1)} %get-tuple-element.220.refs_2_), channel_id=1, source_target_pairs={{0,1},{1,0},{2,3},{3,2},{4,5},{5,4},{6,7},{7,6},{8,9},{9,8},{10,11... | collective-permute-start | bytes 983048 | tf_op jit(solution)/shard_map/ppermute | solution.py:67
  171.0 23.0 %collective-permute-start.29 = (bf16[4,48,1280]{2,1,0:T(8,128)(2,1)}, bf16[4,48,1280]{2,1,0:T(8,128)(2,1)}, u32[]{:S(2)}, u32[]{:S(2)}) collective-permute-start(bf16[4,48,1280]{2,1,0:T(8,128)(2,1)} %get-tuple-element.218.refs_0_), channel_id=1, source_target_pairs={{0,1},{1,0},{2,3},{3,2},{4,5},{5,4},{6,7},{7,6},{8,9},{9,8},{10,11... | collective-permute-start | bytes 1474568 | tf_op jit(solution)/shard_map/ppermute | solution.py:67
  176.8 17.2 %collective-permute-start.30 = (bf16[4,48,1280]{2,1,0:T(8,128)(2,1)}, bf16[4,48,1280]{2,1,0:T(8,128)(2,1)}, u32[]{:S(2)}, u32[]{:S(2)}) collective-permute-start(bf16[4,48,1280]{2,1,0:T(8,128)(2,1)} %get-tuple-element.219.refs_1_), channel_id=1, source_target_pairs={{0,1},{1,0},{2,3},{3,2},{4,5},{5,4},{6,7},{7,6},{8,9},{9,8},{10,11... | collective-permute-start | bytes 1474568 | tf_op jit(solution)/shard_map/ppermute | solution.py:67
  177.5 16.5 %collective-permute-start.34 = (bf16[4,32,1280]{2,1,0:T(8,128)(2,1)}, bf16[4,32,1280]{2,1,0:T(8,128)(2,1)}, u32[]{:S(2)}, u32[]{:S(2)}) collective-permute-start(bf16[4,32,1280]{2,1,0:T(8,128)(2,1)} %collective-permute-done.28.refs_5_), channel_id=1, source_target_pairs={{0,1},{1,0},{2,3},{3,2},{4,5},{5,4},{6,7},{7,6},{8,9},{9,8},{10,11... | collective-permute-start | bytes 983048 | tf_op jit(solution)/shard_map/ppermute | solution.py:67
  178.2 15.8 %collective-permute-start.32 = (bf16[4,48,1280]{2,1,0:T(8,128)(2,1)}, bf16[4,48,1280]{2,1,0:T(8,128)(2,1)}, u32[]{:S(2)}, u32[]{:S(2)}) collective-permute-start(bf16[4,48,1280]{2,1,0:T(8,128)(2,1)} %collective-permute-done.26.refs_3_), channel_id=1, source_target_pairs={{0,1},{1,0},{2,3},{3,2},{4,5},{5,4},{6,7},{7,6},{8,9},{9,8},{10,11... | collective-permute-start | bytes 1474568 | tf_op jit(solution)/shard_map/ppermute | solution.py:67
  179.7 14.4 %collective-permute-start.33 = (bf16[4,48,1280]{2,1,0:T(8,128)(2,1)}, bf16[4,48,1280]{2,1,0:T(8,128)(2,1)}, u32[]{:S(2)}, u32[]{:S(2)}) collective-permute-start(bf16[4,48,1280]{2,1,0:T(8,128)(2,1)} %collective-permute-done.27.refs_4_), channel_id=1, source_target_pairs={{0,1},{1,0},{2,3},{3,2},{4,5},{5,4},{6,7},{7,6},{8,9},{9,8},{10,11... | collective-permute-start | bytes 1474568 | tf_op jit(solution)/shard_map/ppermute | solution.py:67
  204.9 154.0 %all-gather.11.cloned.1.call-start = ((), (), s32[]{:S(2)}) async-start(), calls=%async_computation.10 | async-start | bytes 5570560 | tf_op jit(solution)/shard_map/all_gather | solution.py:100
  213.8 18.6 %collective-permute-start.36 = (bf16[4,48,1280]{2,1,0:T(8,128)(2,1)S(1)}, bf16[4,48,1280]{2,1,0:T(8,128)(2,1)S(1)}, u32[]{:S(2)}, u32[]{:S(2)}) collective-permute-start(bf16[4,48,1280]{2,1,0:T(8,128)(2,1)S(1)} %get-tuple-element.232), channel_id=1, source_target_pairs={{0,8},{1,9},{2,10},{3,11},{4,12},{5,13},{6,14},{7,15},{8,0},{9,1},... | collective-permute-start | bytes 1474568 | tf_op jit(solution)/shard_map/ppermute | solution.py:67
  214.9 18.5 %collective-permute-start.37 = (bf16[4,48,1280]{2,1,0:T(8,128)(2,1)S(1)}, bf16[4,48,1280]{2,1,0:T(8,128)(2,1)S(1)}, u32[]{:S(2)}, u32[]{:S(2)}) collective-permute-start(bf16[4,48,1280]{2,1,0:T(8,128)(2,1)S(1)} %get-tuple-element.236), channel_id=1, source_target_pairs={{0,4},{1,5},{2,6},{3,7},{4,0},{5,1},{6,2},{7,3},{8,12},{9,13},{10,... | collective-permute-start | bytes 1474568 | tf_op jit(solution)/shard_map/ppermute | solution.py:67
  215.5 17.0 %collective-permute-start.38 = (bf16[4,32,1280]{2,1,0:T(8,128)(2,1)S(1)}, bf16[4,32,1280]{2,1,0:T(8,128)(2,1)S(1)}, u32[]{:S(2)}, u32[]{:S(2)}) collective-permute-start(bf16[4,32,1280]{2,1,0:T(8,128)(2,1)S(1)} %get-tuple-element.237), channel_id=1, source_target_pairs={{0,2},{1,3},{2,0},{3,1},{4,6},{5,7},{6,4},{7,5},{8,10},{9,11},{10,... | collective-permute-start | bytes 983048 | tf_op jit(solution)/shard_map/ppermute | solution.py:67
  235.5 26.4 %collective-permute-start.45 = (bf16[160,1280]{1,0:T(8,128)(2,1)S(1)}, bf16[160,1280]{1,0:T(8,128)(2,1)S(1)}, u32[]{:S(2)}, u32[]{:S(2)}) collective-permute-start(bf16[160,1280]{1,0:T(8,128)(2,1)S(1)} %get-tuple-element.317), channel_id=1, source_target_pairs={{0,16},{1,17},{2,18},{3,19},{4,20},{5,21},{6,22},{7,23},{8,24},{9,... | collective-permute-start | bytes 1228808 | tf_op jit(solution)/shard_map/ppermute | solution.py:67
  235.5 12.8 %collective-permute-start.39 = (bf16[2,48,1280]{2,1,0:T(8,128)(2,1)S(1)}, bf16[2,48,1280]{2,1,0:T(8,128)(2,1)S(1)}, u32[]{:S(2)}, u32[]{:S(2)}) collective-permute-start(bf16[2,48,1280]{2,1,0:T(8,128)(2,1)S(1)} %get-tuple-element.241), channel_id=1, source_target_pairs={{0,4},{1,5},{2,6},{3,7},{4,0},{5,1},{6,2},{7,3},{8,12},{9,13},{10,... | collective-permute-start | bytes 737288 | tf_op jit(solution)/shard_map/ppermute | solution.py:67
  236.9 15.7 %collective-permute-start.40 = (bf16[2,48,1280]{2,1,0:T(8,128)(2,1)S(1)}, bf16[2,48,1280]{2,1,0:T(8,128)(2,1)S(1)}, u32[]{:S(2)}, u32[]{:S(2)}) collective-permute-start(bf16[2,48,1280]{2,1,0:T(8,128)(2,1)S(1)} %get-tuple-element.245), channel_id=1, source_target_pairs={{0,2},{1,3},{2,0},{3,1},{4,6},{5,7},{6,4},{7,5},{8,10},{9,11},{10,... | collective-permute-start | bytes 737288 | tf_op jit(solution)/shard_map/ppermute | solution.py:67
  238.2 14.4 %collective-permute-start.41 = (bf16[2,32,1280]{2,1,0:T(8,128)(2,1)S(1)}, bf16[2,32,1280]{2,1,0:T(8,128)(2,1)S(1)}, u32[]{:S(2)}, u32[]{:S(2)}) collective-permute-start(bf16[2,32,1280]{2,1,0:T(8,128)(2,1)S(1)} %get-tuple-element.246), channel_id=1, source_target_pairs={{0,8},{1,9},{2,10},{3,11},{4,12},{5,13},{6,14},{7,15},{8,0},{9,1},... | collective-permute-start | bytes 491528 | tf_op jit(solution)/shard_map/ppermute | solution.py:67
  254.0 7.9 %collective-permute-start.42 = (bf16[1,48,1280]{2,1,0:T(8,128)(2,1)S(1)}, bf16[1,48,1280]{2,1,0:T(8,128)(2,1)S(1)}, u32[]{:S(2)}, u32[]{:S(2)}) collective-permute-start(bf16[1,48,1280]{2,1,0:T(8,128)(2,1)S(1)} %get-tuple-element.250), channel_id=1, source_target_pairs={{0,2},{1,3},{2,0},{3,1},{4,6},{5,7},{6,4},{7,5},{8,10},{9,11},{10,... | collective-permute-start | bytes 368648 | tf_op jit(solution)/shard_map/ppermute | solution.py:67
  254.0 7.9 %collective-permute-start.43 = (bf16[1,48,1280]{2,1,0:T(8,128)(2,1)S(1)}, bf16[1,48,1280]{2,1,0:T(8,128)(2,1)S(1)}, u32[]{:S(2)}, u32[]{:S(2)}) collective-permute-start(bf16[1,48,1280]{2,1,0:T(8,128)(2,1)S(1)} %get-tuple-element.251), channel_id=1, source_target_pairs={{0,8},{1,9},{2,10},{3,11},{4,12},{5,13},{6,14},{7,15},{8,0},{9,1},... | collective-permute-start | bytes 368648 | tf_op jit(solution)/shard_map/ppermute | solution.py:67
  256.5 5.4 %collective-permute-start.44 = (bf16[1,32,1280]{2,1,0:T(8,128)(2,1)S(1)}, bf16[1,32,1280]{2,1,0:T(8,128)(2,1)S(1)}, u32[]{:S(2)}, u32[]{:S(2)}) collective-permute-start(bf16[1,32,1280]{2,1,0:T(8,128)(2,1)S(1)} %get-tuple-element.252), channel_id=1, source_target_pairs={{0,4},{1,5},{2,6},{3,7},{4,0},{5,1},{6,2},{7,3},{8,12},{9,13},{10,... | collective-permute-start | bytes 245768 | tf_op jit(solution)/shard_map/ppermute | solution.py:67
  282.0 39.8 %all-to-all-start.4 = ((bf16[32,8,1600]{2,1,0:T(8,128)(2,1)}), bf16[32,8,1600]{2,1,0:T(8,128)(2,1)S(1)}, u32[]{:S(2)}, u32[]{:S(2)}) async-start(bf16[32,8,1600]{2,1,0:T(8,128)(2,1)} %fc1_grad.1), calls=%async_computation.5 | async-start | bytes 1703936 | tf_op jit(solution)/shard_map/all_to_all | solution.py:106
  329.0 11.8 %collective-permute-start.47 = (bf16[64,1280]{1,0:T(8,128)(2,1)S(1)}, bf16[64,1280]{1,0:T(8,128)(2,1)S(1)}, u32[]{:S(2)}, u32[]{:S(2)}) collective-permute-start(bf16[64,1280]{1,0:T(8,128)(2,1)S(1)} %dynamic-slice_bitcast_fusion.3), channel_id=1, source_target_pairs={{0,16},{1,17},{2,18},{3,19},{4,20},{5,21},{6,22},{7,23},{8,24},{9,... | collective-permute-start | bytes 491528 | tf_op jit(solution)/shard_map/ppermute | solution.py:67
  329.9 18.5 %collective-permute-start.48 = (bf16[4,48,1280]{2,1,0:T(8,128)(2,1)S(1)}, bf16[4,48,1280]{2,1,0:T(8,128)(2,1)S(1)}, u32[]{:S(2)}, u32[]{:S(2)}) collective-permute-start(bf16[4,48,1280]{2,1,0:T(8,128)(2,1)S(1)} %get-tuple-element.272), channel_id=1, source_target_pairs={{0,8},{1,9},{2,10},{3,11},{4,12},{5,13},{6,14},{7,15},{8,0},{9,1},... | collective-permute-start | bytes 1474568 | tf_op jit(solution)/shard_map/ppermute | solution.py:67
  331.7 16.7 %collective-permute-start.49 = (bf16[4,48,1280]{2,1,0:T(8,128)(2,1)S(1)}, bf16[4,48,1280]{2,1,0:T(8,128)(2,1)S(1)}, u32[]{:S(2)}, u32[]{:S(2)}) collective-permute-start(bf16[4,48,1280]{2,1,0:T(8,128)(2,1)S(1)} %get-tuple-element.283), channel_id=1, source_target_pairs={{0,4},{1,5},{2,6},{3,7},{4,0},{5,1},{6,2},{7,3},{8,12},{9,13},{10,... | collective-permute-start | bytes 1474568 | tf_op jit(solution)/shard_map/ppermute | solution.py:67
  332.1 16.2 %collective-permute-start.50 = (bf16[4,32,1280]{2,1,0:T(8,128)(2,1)S(1)}, bf16[4,32,1280]{2,1,0:T(8,128)(2,1)S(1)}, u32[]{:S(2)}, u32[]{:S(2)}) collective-permute-start(bf16[4,32,1280]{2,1,0:T(8,128)(2,1)S(1)} %get-tuple-element.284), channel_id=1, source_target_pairs={{0,2},{1,3},{2,0},{3,1},{4,6},{5,7},{6,4},{7,5},{8,10},{9,11},{10,... | collective-permute-start | bytes 983048 | tf_op jit(solution)/shard_map/ppermute | solution.py:67
  351.8 26.7 %all-to-all-start.5 = ((bf16[32,40,256]{2,1,0:T(8,128)(2,1)}), bf16[32,40,256]{2,1,0:T(8,128)(2,1)S(1)}, u32[]{:S(2)}, u32[]{:S(2)}) async-start(bf16[32,40,256]{2,1,0:T(8,128)(2,1)} %head_grad.1), calls=%async_computation.6 | async-start | bytes 1310720 | tf_op jit(solution)/shard_map/all_to_all | solution.py:106
  357.1 12.7 %collective-permute-start.51 = (bf16[2,48,1280]{2,1,0:T(8,128)(2,1)}, bf16[2,48,1280]{2,1,0:T(8,128)(2,1)S(1)}, u32[]{:S(2)}, u32[]{:S(2)}) collective-permute-start(bf16[2,48,1280]{2,1,0:T(8,128)(2,1)} %get-tuple-element.288), channel_id=1, source_target_pairs={{0,4},{1,5},{2,6},{3,7},{4,0},{5,1},{6,2},{7,3},{8,12},{9,13},{10,... | collective-permute-start | bytes 737288 | tf_op jit(solution)/shard_map/ppermute | solution.py:67
  358.9 12.0 %collective-permute-start.52 = (bf16[2,48,1280]{2,1,0:T(8,128)(2,1)}, bf16[2,48,1280]{2,1,0:T(8,128)(2,1)S(1)}, u32[]{:S(2)}, u32[]{:S(2)}) collective-permute-start(bf16[2,48,1280]{2,1,0:T(8,128)(2,1)} %get-tuple-element.293), channel_id=1, source_target_pairs={{0,2},{1,3},{2,0},{3,1},{4,6},{5,7},{6,4},{7,5},{8,10},{9,11},{10,... | collective-permute-start | bytes 737288 | tf_op jit(solution)/shard_map/ppermute | solution.py:67
  360.4 10.5 %collective-permute-start.53 = (bf16[2,32,1280]{2,1,0:T(8,128)(2,1)}, bf16[2,32,1280]{2,1,0:T(8,128)(2,1)S(1)}, u32[]{:S(2)}, u32[]{:S(2)}) collective-permute-start(bf16[2,32,1280]{2,1,0:T(8,128)(2,1)} %get-tuple-element.294), channel_id=1, source_target_pairs={{0,8},{1,9},{2,10},{3,11},{4,12},{5,13},{6,14},{7,15},{8,0},{9,1},... | collective-permute-start | bytes 491528 | tf_op jit(solution)/shard_map/ppermute | solution.py:67
  366.1 11.7 %collective-permute-start.59 = (bf16[40,1280]{1,0:T(8,128)(2,1)S(1)}, bf16[40,1280]{1,0:T(8,128)(2,1)S(1)}, u32[]{:S(2)}, u32[]{:S(2)}) collective-permute-start(bf16[40,1280]{1,0:T(8,128)(2,1)S(1)} %get-tuple-element.330), channel_id=1, source_target_pairs={{0,1},{1,3},{2,5},{3,7},{4,9},{5,11},{6,13},{7,15},{8,17},{9,19},{... | collective-permute-start | bytes 307208 | tf_op jit(solution)/shard_map/ppermute | solution.py:67
  366.2 11.7 %collective-permute-start.58 = (bf16[40,1280]{1,0:T(8,128)(2,1)S(1)}, bf16[40,1280]{1,0:T(8,128)(2,1)S(1)}, u32[]{:S(2)}, u32[]{:S(2)}) collective-permute-start(bf16[40,1280]{1,0:T(8,128)(2,1)S(1)} %get-tuple-element.329), channel_id=1, source_target_pairs={{0,0},{1,2},{2,4},{3,6},{4,8},{5,10},{6,12},{7,14},{8,16},{9,18},{... | collective-permute-start | bytes 307208 | tf_op jit(solution)/shard_map/ppermute | solution.py:67
  372.3 8.0 %collective-permute-start.54 = (bf16[1,48,1280]{2,1,0:T(8,128)(2,1)S(1)}, bf16[1,48,1280]{2,1,0:T(8,128)(2,1)S(1)}, u32[]{:S(2)}, u32[]{:S(2)}) collective-permute-start(bf16[1,48,1280]{2,1,0:T(8,128)(2,1)S(1)} %get-tuple-element.300), channel_id=1, source_target_pairs={{0,2},{1,3},{2,0},{3,1},{4,6},{5,7},{6,4},{7,5},{8,10},{9,11},{10,... | collective-permute-start | bytes 368648 | tf_op jit(solution)/shard_map/ppermute | solution.py:67
  374.5 5.9 %collective-permute-start.55 = (bf16[1,48,1280]{2,1,0:T(8,128)(2,1)S(1)}, bf16[1,48,1280]{2,1,0:T(8,128)(2,1)S(1)}, u32[]{:S(2)}, u32[]{:S(2)}) collective-permute-start(bf16[1,48,1280]{2,1,0:T(8,128)(2,1)S(1)} %get-tuple-element.301), channel_id=1, source_target_pairs={{0,8},{1,9},{2,10},{3,11},{4,12},{5,13},{6,14},{7,15},{8,0},{9,1},... | collective-permute-start | bytes 368648 | tf_op jit(solution)/shard_map/ppermute | solution.py:67
  384.0 9.9 %collective-permute-start.57 = (bf16[64,1280]{1,0:T(8,128)(2,1)S(1)}, bf16[64,1280]{1,0:T(8,128)(2,1)S(1)}, u32[]{:S(2)}, u32[]{:S(2)}) collective-permute-start(bf16[64,1280]{1,0:T(8,128)(2,1)S(1)} %dynamic-slice_bitcast_fusion.2), channel_id=1, source_target_pairs={{0,16},{1,17},{2,18},{3,19},{4,20},{5,21},{6,22},{7,23},{8,24},{9,... | collective-permute-start | bytes 491528 | tf_op jit(solution)/shard_map/ppermute | solution.py:67
  (55 other events, 524.1 us)
Sparse Core Ops, SparseCore 0:
  73.2 46.4 all-gather.6
  121.2 47.6 all-gather.8
  205.0 75.6 reduce-scatter.1
  282.1 59.1 all-gather.10
